TPU v7x, 32 devices: a whole 2x2x4 slice. The times are simulated.
32 devices in a mesh: band: 8 (over y, x, core), head: 4 (over z).
Axes of the slice: x: 2, y: 2, z: 4, core: 2. Of those that a mesh axis runs over, the one named last changes fastest.
Arguments:
- queries: bfloat16 [256, 8192], P('head', 'band'), may hold values from -76 to 76
- keys: bfloat16 [256, 8192], P('head', 'band'), may hold values from -6 to 6
- values: bfloat16 [256, 8192], P('head', 'band'), may hold values from -6 to 6
- grad_out: bfloat16 [256, 8192], P('head', 'band'), may hold values from -6 to 6
- w_out: bfloat16 [256, 256], P('head'), may hold values from -0.375 to 0.375
- key_lists: int32 [64, 8], P('band'), may hold values from 0 to 63, as said below
- key_counts: int32 [64], P('band'), may hold values from 2 to 8, as said below
Outputs:
- grad_queries: bfloat16 [256, 8192], P('head', 'band')
- grad_keys: bfloat16 [256, 8192], P('head', 'band')
- grad_values: bfloat16 [256, 8192], P('head', 'band')
- grad_w_out: float32 [256, 256], P('head')
Inputs may be any that keep to these rules, and one draw needn't show every extreme that they name: `key_lists`: row b holds 8 different blocks; the first is b itself and every entry lies within 8 blocks of b. `key_counts`: the number of leading entries of the row of key_lists that are used.
All inputs are finite; a program needn't handle non-finite values.
Results may differ from a plain program's by a relative error of at most 0.0058.
Values may be sent and summed in bfloat16 or wider, within the bound.
No kernel may reach another device: no remote copies, remote signals or barrier semaphores. Data moves between devices by JAX's collectives and lax.ppermute only.
A program may use at most 64 MiB of HBM per device.

v0:
```python
import jax
import jax.numpy as jnp
from jax import lax
from jax.sharding import PartitionSpec as P

HEAD_DIM = 32
BLOCK = 128
REACH = 4
MAX_KEYS = 8


def with_halo(block, sides, width):
    for axis, dim in sides:
        count = lax.axis_size(axis)
        forward = [(i, i + 1) for i in range(count - 1)]
        backward = [(target, source) for source, target in forward]
        low = lax.ppermute(
            lax.slice_in_dim(block, block.shape[dim] - width, None, axis=dim), axis, forward
        )
        high = lax.ppermute(lax.slice_in_dim(block, 0, width, axis=dim), axis, backward)
        block = jnp.concatenate([low, block, high], axis=dim)
    return block


def shifted(value, axis, steps):
    count = lax.axis_size(axis)
    initial, last = (max(0, -steps), min(count, count - steps))
    return lax.ppermute(value, axis, [(source, source + steps) for source in range(initial, last)])


def block_grads(query_blk, grad_blk, slots, usable, key_ext, value_ext, bias_ext):
    count = slots.shape[0]
    span = count * BLOCK
    chans = query_blk.shape[0]
    heads_here = chans // HEAD_DIM
    scale = HEAD_DIM ** (-0.5)
    picked_k = key_ext[:, slots].reshape(heads_here, HEAD_DIM, span)
    picked_v = value_ext[:, slots].reshape(heads_here, HEAD_DIM, span)
    key_bias = bias_ext[slots].reshape(span)
    live_keys = jnp.repeat(usable, BLOCK)
    query_h = query_blk.reshape(heads_here, HEAD_DIM, BLOCK)
    grad_h = grad_blk.reshape(heads_here, HEAD_DIM, BLOCK)
    scores = (
        jnp.einsum("hdq,hdk->hqk", query_h, picked_k, preferred_element_type=jnp.float32) * scale
        + key_bias
    )
    scores = jnp.where(live_keys, scores, -jnp.inf)
    peak = jnp.max(scores, axis=-1)
    log_total = peak + jnp.log(jnp.sum(jnp.exp(scores - peak[..., None]), axis=-1))
    probs = jnp.exp(scores - log_total[..., None])
    probs_low = probs.astype(jnp.bfloat16)
    dprobs = jnp.einsum("hdq,hdk->hqk", grad_h, picked_v, preferred_element_type=jnp.float32)
    spread = jnp.sum(probs * dprobs, axis=-1)
    dscores = (probs * (dprobs - spread[..., None]) * scale).astype(jnp.bfloat16)
    dquery = jnp.einsum(
        "hqk,hdk->hdq", dscores, picked_k, preferred_element_type=jnp.float32
    ).reshape(chans, BLOCK)
    dkey = jnp.einsum("hqk,hdq->hdk", dscores, query_h, preferred_element_type=jnp.float32).reshape(
        chans, count, BLOCK
    )
    dvalue = jnp.einsum(
        "hqk,hdq->hdk", probs_low, grad_h, preferred_element_type=jnp.float32
    ).reshape(chans, count, BLOCK)
    attended = jnp.einsum(
        "hqk,hdk->hdq", probs_low, picked_v, preferred_element_type=jnp.float32
    ).reshape(chans, BLOCK)
    return (dquery, dkey, dvalue, attended, log_total, spread)


def band_bias(first_block, ext_blocks, total_tokens):
    positions = first_block * BLOCK + jnp.arange(ext_blocks * BLOCK, dtype=jnp.int32)
    positions = jnp.clip(positions, 0, total_tokens - 1).astype(jnp.float32)
    return jnp.log(jnp.sin(jnp.pi * (positions + 0.5) / total_tokens)).reshape(ext_blocks, BLOCK)


def run_blocks(query_blocks, grad_blocks, slot_rows, use_rows, key_ext, value_ext, bias_ext):
    chans = query_blocks.shape[0]
    nblocks = query_blocks.shape[1]
    heads_here = chans // HEAD_DIM
    ext_blocks = key_ext.shape[1]
    zeros = jnp.zeros((chans, ext_blocks, BLOCK), jnp.float32)
    start = (
        zeros,
        zeros,
        jnp.zeros((chans, nblocks, BLOCK), jnp.bfloat16),
        jnp.zeros((chans, nblocks, BLOCK), jnp.bfloat16),
        jnp.zeros((nblocks, heads_here, BLOCK), jnp.float32),
        jnp.zeros((nblocks, heads_here, BLOCK), jnp.float32),
    )

    def run_width(index, carry):
        acc_k, acc_v, dq_all, att_all, lse_all, spread_all = carry
        query_blk = lax.dynamic_index_in_dim(query_blocks, index, 1, keepdims=False)
        grad_blk = lax.dynamic_index_in_dim(grad_blocks, index, 1, keepdims=False)
        slots = slot_rows[index]
        dquery, dkey, dvalue, attended, log_total, spread = block_grads(
            query_blk, grad_blk, slots, use_rows[index], key_ext, value_ext, bias_ext
        )
        acc_k = acc_k.at[:, slots].add(dkey)
        acc_v = acc_v.at[:, slots].add(dvalue)
        dq_all = dq_all.at[:, index].set(dquery.astype(jnp.bfloat16))
        att_all = att_all.at[:, index].set(attended.astype(jnp.bfloat16))
        lse_all = lse_all.at[index].set(log_total)
        spread_all = spread_all.at[index].set(spread)
        return (acc_k, acc_v, dq_all, att_all, lse_all, spread_all)

    def block_step(index, carry):
        return run_width(index, carry)

    return lax.fori_loop(0, nblocks, block_step, start)


def shards(queries, keys, values, grad_out, w_out, key_lists, key_counts):
    chans = queries.shape[0]
    blocks = queries.shape[1] // BLOCK
    rim_blocks = 2 * REACH
    ext_blocks = blocks + 2 * rim_blocks
    band_index = lax.axis_index("band")
    band_count = lax.axis_size("band")
    total_tokens = blocks * BLOCK * band_count
    full_grad = lax.all_gather(grad_out, "head", axis=0, tiled=True)
    grad_att = jnp.einsum("cd,dt->ct", w_out, full_grad, preferred_element_type=jnp.float32).astype(
        jnp.bfloat16
    )
    key_pairs = jnp.stack(
        [keys.reshape(chans, blocks, BLOCK), values.reshape(chans, blocks, BLOCK)]
    )
    pair_ext = with_halo(key_pairs, (("band", 2),), rim_blocks)
    key_ext = pair_ext[0]
    value_ext = pair_ext[1]
    first_block = band_index * blocks - rim_blocks
    bias_ext = band_bias(first_block, ext_blocks, total_tokens)
    slot_ids = jnp.arange(MAX_KEYS, dtype=jnp.int32)
    masked = jnp.where(slot_ids[None, :] < key_counts[:, None], key_lists, -1)
    usable = masked >= 0
    local_slots = jnp.clip(masked - first_block, 0, ext_blocks - 1)
    query_blocks = queries.reshape(chans, blocks, BLOCK)
    grad_blocks = grad_att.reshape(chans, blocks, BLOCK)
    acc_k, acc_v, dq_all, att_all, lse_all, spread_all = run_blocks(
        query_blocks, grad_blocks, local_slots, usable, key_ext, value_ext, bias_ext
    )
    lower_part = jnp.stack([acc_k[:, :rim_blocks], acc_v[:, :rim_blocks]])
    upper_part = jnp.stack([acc_k[:, rim_blocks + blocks :], acc_v[:, rim_blocks + blocks :]])
    from_above = shifted(lower_part.astype(jnp.bfloat16), "band", -1).astype(lower_part.dtype)
    from_below = shifted(upper_part.astype(jnp.bfloat16), "band", 1).astype(upper_part.dtype)
    owned = jnp.stack(
        [acc_k[:, rim_blocks : rim_blocks + blocks], acc_v[:, rim_blocks : rim_blocks + blocks]]
    )
    owned = owned.at[:, :, :rim_blocks].add(from_below)
    owned = owned.at[:, :, blocks - rim_blocks :].add(from_above)
    grad_queries = dq_all.reshape(chans, blocks * BLOCK)
    grad_keys = owned[0].reshape(chans, blocks * BLOCK).astype(jnp.bfloat16)
    grad_values = owned[1].reshape(chans, blocks * BLOCK).astype(jnp.bfloat16)
    attended = att_all.reshape(chans, blocks * BLOCK)
    partial_w = jnp.einsum("ct,dt->cd", attended, full_grad, preferred_element_type=jnp.float32)
    shared_part = lax.psum_scatter(partial_w, "band", scatter_dimension=1, tiled=True)
    grad_w_out = lax.all_gather(shared_part, "band", axis=1, tiled=True)
    return (grad_queries, grad_keys, grad_values, grad_w_out)


def solution(mesh):
    in_specs = (
        P("head", "band"),
        P("head", "band"),
        P("head", "band"),
        P("head", "band"),
        P("head", None),
        P("band", None),
        P("band"),
    )
    out_specs = (P("head", "band"), P("head", "band"), P("head", "band"), P("head", None))
    return jax.shard_map(shards, mesh=mesh, in_specs=in_specs, out_specs=out_specs, check_vma=False)
```

profile of v0, /device:TPU:0, one launch (start us, length us, event | category | flops | bytes accessed | tf_op | source)
XLA Modules:
  0.0 239.2 jit_solution(767924862107721020)
XLA Ops:
  10.5 3.0 %collective-permute-start = (bf16[2,64,8,128]{3,2,1,0:T(8,128)(2,1)S(1)}, bf16[2,64,8,128]{3,2,1,0:T(8,128)(2,1)S(1)}, u32[]{:S(2)}, u32[]{:S(2)}) collective-permute-start(bf16[2,64,8,128]{3,2,1,0:T(8,128)(2,1)S(1)} %bitcast_dynamic-update-slice_fusion), channel_id=1, source_target_pairs={{0,4},{4,8},{8,12},{12,16},{16,20},{20,24},{24,28},{1,5},{5,9},{9,... | collective-permute-start | bytes 786440 | tf_op jit(solution)/shard_map/ppermute | solution.py:17
  14.9 18.4 %all_gather.6 = bf16[256,1024]{1,0:T(8,128)(2,1)S(1)} all-gather(bf16[64,1024]{1,0:T(8,128)(2,1)S(1)} %copy-done.11), channel_id=1, replica_groups=mesh['band'=8,'head'=4] {'head'}, dimensions={0}, use_global_device_ids=true | all-gather | bytes 655360 | tf_op jit(solution)/shard_map/all_gather | solution.py:121
  38.7 139.4 %while.26 = (s32[]{:T(128)}, f32[64,24,128]{2,0,1:T(8,128)}, f32[64,24,128]{2,0,1:T(8,128)S(1)}, bf16[64,8,128]{2,0,1:T(8,128)(2,1)S(1)}, bf16[64,8,128]{2,0,1:T...) while((s32[]{:T(128)}, f32[64,24,128]{2,0,1:T(8,128)}, ...), condition=%wide.region_7.8_spmd.clone, body=%wide.region_0.7_spmd.clone.sunk | while | flops 107143464 | bytes 23508944 | solution.py:110
  42.9 1.6 gather_fusion.2
  50.4 1.8 fusion.90
  52.3 2.0 constant_dynamic-update-slice_fusion.3
  67.8 1.8 fusion.90
  69.8 2.0 constant_dynamic-update-slice_fusion.3
  85.2 1.8 fusion.90
  87.2 2.0 constant_dynamic-update-slice_fusion.3
  102.7 1.8 fusion.90
  104.6 2.0 constant_dynamic-update-slice_fusion.3
  112.6 1.6 gather_fusion.2
  120.1 1.8 fusion.90
  122.1 2.0 constant_dynamic-update-slice_fusion.3
  137.5 1.8 fusion.90
  139.5 2.0 constant_dynamic-update-slice_fusion.3
  155.0 1.8 fusion.90
  156.9 2.0 constant_dynamic-update-slice_fusion.3
  172.4 1.8 fusion.90
  174.4 2.0 constant_dynamic-update-slice_fusion.3
  182.0 3.0 %collective-permute-start.2 = (bf16[2,64,8,128]{3,1,2,0:T(8,128)(2,1)S(1)}, bf16[2,64,8,128]{3,1,2,0:T(8,128)(2,1)S(1)}, u32[]{:S(2)}, u32[]{:S(2)}) collective-permute-start(bf16[2,64,8,128]{3,1,2,0:T(8,128)(2,1)S(1)} %pad_maximum_fusion.1), channel_id=1, source_target_pairs={{0,4},{4,8},{8,12},{12,16},{16,20},{20,24},{24,28},{1,5},{5,9},{9,... | collective-permute-start | bytes 786440 | tf_op jit(solution)/shard_map/ppermute | solution.py:28
  186.7 34.1 %reduce-scatter.2.cloned.1.call-done = f32[64,32]{0,1:T(8,128)} async-done(((f32[64,256]{0,1:T(8,128)}), f32[64,32]{0,1:T(8,128)}) %reduce-scatter.2.cloned.1.call-update) | async-done | bytes 8208 | tf_op jit(solution)/shard_map/reduce_scatter | solution.py:156
  220.8 9.2 %all_gather.7 = f32[64,256]{0,1:T(8,128)S(1)} all-gather(f32[64,32]{0,1:T(8,128)} %reduce-scatter.2.cloned.1.call-done), channel_id=1, replica_groups=mesh['band'=8,'head'=4] {'band'}, dimensions={1}, use_global_device_ids=true | all-gather | bytes 73728 | tf_op jit(solution)/shard_map/all_gather | solution.py:157
  (422 shorter events, 121.8 us)
Async XLA Ops:
  7.2 27.2 %copy-start = (bf16[64,1024]{1,0:T(8,128)(2,1)S(1)}, bf16[64,1024]{1,0:T(8,128)(2,1)}, u32[]{:S(2)}) copy-start(bf16[64,1024]{1,0:T(8,128)(2,1)} %param.21) | copy-start | bytes 393220
  7.2 6.4 %copy-start.16 = (s32[8]{0:T(128)S(1)}, s32[8]{0:T(128)}, u32[]{:S(2)}) copy-start(s32[8]{0:T(128)} %param.27) | copy-start | bytes 100
  7.2 6.4 %copy-start.15 = (s32[8,8]{1,0:T(8,128)S(1)}, s32[8,8]{1,0:T(8,128)}, u32[]{:S(2)}) copy-start(s32[8,8]{1,0:T(8,128)} %param.26) | copy-start | bytes 772
  7.2 7.7 %copy-start.11 = (bf16[64,1024]{1,0:T(8,128)(2,1)S(1)}, bf16[64,1024]{1,0:T(8,128)(2,1)}, u32[]{:S(2)}) copy-start(bf16[64,1024]{1,0:T(8,128)(2,1)} %param.24) | copy-start | bytes 393220
  7.2 26.9 %copy-start.14 = (bf16[64,256]{1,0:T(8,128)(2,1)S(1)}, bf16[64,256]{1,0:T(8,128)(2,1)}, u32[]{:S(2)}) copy-start(bf16[64,256]{1,0:T(8,128)(2,1)} %param.25) | copy-start | bytes 98308
  7.2 213.5 %reduce-scatter.2.cloned.1.call-start = ((), (), s32[]{:S(2)}) async-start(), calls=%async_computation.1 | async-start | bytes 147456 | tf_op jit(solution)/shard_map/reduce_scatter | solution.py:156
  9.2 25.8 %collective-permute-start.1 = (bf16[2,64,8,128]{3,2,1,0:T(8,128)(2,1)S(1)}, bf16[2,64,8,128]{3,2,1,0:T(8,128)(2,1)S(1)}, u32[]{:S(2)}, u32[]{:S(2)}) collective-permute-start(bf16[2,64,8,128]{3,2,1,0:T(8,128)(2,1)S(1)} %bitcast_dynamic-update-slice_fusion), channel_id=1, source_target_pairs={{4,0},{8,4},{12,8},{16,12},{20,16},{24,20},{28,24},{5,1},{9,5},{13... | collective-permute-start | bytes 786440 | tf_op jit(solution)/shard_map/ppermute | solution.py:20
  10.5 24.5 %collective-permute-start = (bf16[2,64,8,128]{3,2,1,0:T(8,128)(2,1)S(1)}, bf16[2,64,8,128]{3,2,1,0:T(8,128)(2,1)S(1)}, u32[]{:S(2)}, u32[]{:S(2)}) collective-permute-start(bf16[2,64,8,128]{3,2,1,0:T(8,128)(2,1)S(1)} %bitcast_dynamic-update-slice_fusion), channel_id=1, source_target_pairs={{0,4},{4,8},{8,12},{12,16},{16,20},{20,24},{24,28},{1,5},{5,9},{9,... | collective-permute-start | bytes 786440 | tf_op jit(solution)/shard_map/ppermute | solution.py:17
  40.8 7.3 %copy-start.12 = (s32[8]{0:T(128)}, s32[8]{0:T(128)S(1)}, u32[]{:S(2)}) copy-start(s32[8]{0:T(128)S(1)} %fusion.86) | copy-start | bytes 100 | tf_op jit(solution)/shard_map/while
  56.1 5.8 %copy-start.8 = (bf16[64,8,128]{2,0,1:T(8,128)(2,1)}, bf16[64,8,128]{2,0,1:T(8,128)(2,1)S(1)}, u32[]{:S(2)}) copy-start(bf16[64,8,128]{2,0,1:T(8,128)(2,1)S(1)} %get-tuple-element.529) | copy-start | bytes 393220 | tf_op jit(solution)/shard_map/while
  58.2 7.3 %copy-start.12 = (s32[8]{0:T(128)}, s32[8]{0:T(128)S(1)}, u32[]{:S(2)}) copy-start(s32[8]{0:T(128)S(1)} %fusion.86) | copy-start | bytes 100 | tf_op jit(solution)/shard_map/while
  73.6 5.8 %copy-start.8 = (bf16[64,8,128]{2,0,1:T(8,128)(2,1)}, bf16[64,8,128]{2,0,1:T(8,128)(2,1)S(1)}, u32[]{:S(2)}) copy-start(bf16[64,8,128]{2,0,1:T(8,128)(2,1)S(1)} %get-tuple-element.529) | copy-start | bytes 393220 | tf_op jit(solution)/shard_map/while
  75.6 7.3 %copy-start.12 = (s32[8]{0:T(128)}, s32[8]{0:T(128)S(1)}, u32[]{:S(2)}) copy-start(s32[8]{0:T(128)S(1)} %fusion.86) | copy-start | bytes 100 | tf_op jit(solution)/shard_map/while
  91.0 5.8 %copy-start.8 = (bf16[64,8,128]{2,0,1:T(8,128)(2,1)}, bf16[64,8,128]{2,0,1:T(8,128)(2,1)S(1)}, u32[]{:S(2)}) copy-start(bf16[64,8,128]{2,0,1:T(8,128)(2,1)S(1)} %get-tuple-element.529) | copy-start | bytes 393220 | tf_op jit(solution)/shard_map/while
  93.1 7.3 %copy-start.12 = (s32[8]{0:T(128)}, s32[8]{0:T(128)S(1)}, u32[]{:S(2)}) copy-start(s32[8]{0:T(128)S(1)} %fusion.86) | copy-start | bytes 100 | tf_op jit(solution)/shard_map/while
  108.4 5.8 %copy-start.8 = (bf16[64,8,128]{2,0,1:T(8,128)(2,1)}, bf16[64,8,128]{2,0,1:T(8,128)(2,1)S(1)}, u32[]{:S(2)}) copy-start(bf16[64,8,128]{2,0,1:T(8,128)(2,1)S(1)} %get-tuple-element.529) | copy-start | bytes 393220 | tf_op jit(solution)/shard_map/while
  110.5 7.3 %copy-start.12 = (s32[8]{0:T(128)}, s32[8]{0:T(128)S(1)}, u32[]{:S(2)}) copy-start(s32[8]{0:T(128)S(1)} %fusion.86) | copy-start | bytes 100 | tf_op jit(solution)/shard_map/while
  125.8 5.8 %copy-start.8 = (bf16[64,8,128]{2,0,1:T(8,128)(2,1)}, bf16[64,8,128]{2,0,1:T(8,128)(2,1)S(1)}, u32[]{:S(2)}) copy-start(bf16[64,8,128]{2,0,1:T(8,128)(2,1)S(1)} %get-tuple-element.529) | copy-start | bytes 393220 | tf_op jit(solution)/shard_map/while
  127.9 7.3 %copy-start.12 = (s32[8]{0:T(128)}, s32[8]{0:T(128)S(1)}, u32[]{:S(2)}) copy-start(s32[8]{0:T(128)S(1)} %fusion.86) | copy-start | bytes 100 | tf_op jit(solution)/shard_map/while
  143.3 5.8 %copy-start.8 = (bf16[64,8,128]{2,0,1:T(8,128)(2,1)}, bf16[64,8,128]{2,0,1:T(8,128)(2,1)S(1)}, u32[]{:S(2)}) copy-start(bf16[64,8,128]{2,0,1:T(8,128)(2,1)S(1)} %get-tuple-element.529) | copy-start | bytes 393220 | tf_op jit(solution)/shard_map/while
  145.4 7.3 %copy-start.12 = (s32[8]{0:T(128)}, s32[8]{0:T(128)S(1)}, u32[]{:S(2)}) copy-start(s32[8]{0:T(128)S(1)} %fusion.86) | copy-start | bytes 100 | tf_op jit(solution)/shard_map/while
  162.8 7.3 %copy-start.12 = (s32[8]{0:T(128)}, s32[8]{0:T(128)S(1)}, u32[]{:S(2)}) copy-start(s32[8]{0:T(128)S(1)} %fusion.86) | copy-start | bytes 100 | tf_op jit(solution)/shard_map/while
  180.5 50.2 %collective-permute-start.3 = (bf16[2,64,8,128]{3,1,2,0:T(8,128)(2,1)S(1)}, bf16[2,64,8,128]{3,1,2,0:T(8,128)(2,1)S(1)}, u32[]{:S(2)}, u32[]{:S(2)}) collective-permute-start(bf16[2,64,8,128]{3,1,2,0:T(8,128)(2,1)S(1)} %pad_maximum_fusion.2), channel_id=1, source_target_pairs={{4,0},{8,4},{12,8},{16,12},{20,16},{24,20},{28,24},{5,1},{9,5},{13... | collective-permute-start | bytes 786440 | tf_op jit(solution)/shard_map/ppermute | solution.py:28
  182.0 48.7 %collective-permute-start.2 = (bf16[2,64,8,128]{3,1,2,0:T(8,128)(2,1)S(1)}, bf16[2,64,8,128]{3,1,2,0:T(8,128)(2,1)S(1)}, u32[]{:S(2)}, u32[]{:S(2)}) collective-permute-start(bf16[2,64,8,128]{3,1,2,0:T(8,128)(2,1)S(1)} %pad_maximum_fusion.1), channel_id=1, source_target_pairs={{0,4},{4,8},{8,12},{12,16},{16,20},{20,24},{24,28},{1,5},{5,9},{9,... | collective-permute-start | bytes 786440 | tf_op jit(solution)/shard_map/ppermute | solution.py:28
  (61 other events, 165.5 us)
Sparse Core Ops, SparseCore 0:
  186.1 34.5 reduce-scatter.1
where the time goes:
time: 242 us; the launch traced here: 239 us
  local copies, waits for them, and re-layouts  63.9 us (26%)
  other arithmetic  52.8 us (22%)
  matrix products  36 us (15%)
  waiting for transfers between devices  34.1 us (14%)
  blocking collectives  27.5 us (11%)
  between operations  14.3 us (6%)
  starting transfers between devices  8.85 us (4%)
    reduce_scatter x1, waiting for transfers between devices, shards(): lax.psum_scatter(partial_w, 'band', scatter_dimension=1, tiled=True)  34.1 us
    all_gather x1, blocking collectives, shards(): full_grad = lax.all_gather(grad_out, 'head', axis=0, tiled=True)  18.4 us
    scatter x8, other arithmetic, run_width(): att_all = att_all.at[:, index].set(attended.astype(jnp.bfloat16))  16 us
    dot_general x8, matrix products, block_grads(): jnp.einsum('hqk,hdq->hdk', dscores, query_h, preferred_element_type=jnp.f...  14.5 us
    gather x16, local copies, waits for them, and re-layouts, block_grads(): picked_k = key_ext[:, slots].reshape(heads_here, HEAD_DIM, span)  13.3 us
    gather x16, local copies, waits for them, and re-layouts, block_grads(): picked_v = value_ext[:, slots].reshape(heads_here, HEAD_DIM, span)  13.3 us
    another operation x11, other arithmetic  12.5 us
    all_gather x1, blocking collectives, shards(): grad_w_out = lax.all_gather(shared_part, 'band', axis=1, tiled=True)  9.18 us
  transfers between devices with their start and end apart: 5, of which 1 were waited for; matrix products, arithmetic and copies ran while one was open for 2% of the time, Pallas kernels for 0%

commit v1 on v0

v1 whole, which is shorter than its diff:
```python
import functools

import jax
import jax.numpy as jnp
from jax import lax
from jax.experimental import pallas as pl
from jax.experimental.pallas import tpu as pltpu
from jax.sharding import PartitionSpec as P

HEAD_DIM = 32
BLOCK = 128
REACH = 4
MAX_KEYS = 8
RIM = 2 * REACH
SCALE = HEAD_DIM ** (-0.5)
LOG2E = 1.4426950408889634
RAW = SCALE * LOG2E
MASKED = -1e30
AUG = 16
F32 = jnp.float32
BF16 = jnp.bfloat16
VMEM_LIMIT = 48 * 1024 * 1024


def dot(a, b):
    return lax.dot_general(a, b, (((1,), (0,)), ((), ())), preferred_element_type=F32)


def dot_nt(a, b):
    return lax.dot_general(a, b, (((1,), (1,)), ((), ())), preferred_element_type=F32)


def split3(x):
    hi = x.astype(BF16).astype(F32)
    rest = x - hi
    mid = rest.astype(BF16).astype(F32)
    return hi, mid, (rest - mid).astype(BF16).astype(F32)


def aug_rows(rows, width):
    at = lax.broadcasted_iota(jnp.int32, (AUG, width), 0)
    out = jnp.zeros((AUG, width), F32)
    for i, row in enumerate(rows):
        out = jnp.where(at == i, row, out)
    return out.astype(BF16)


def spread_heads(x, heads):
    zero = jnp.zeros((HEAD_DIM, BLOCK), x.dtype)
    rows = []
    for h in range(heads):
        part = x[h * HEAD_DIM : (h + 1) * HEAD_DIM]
        rows.append(jnp.concatenate([part if g == h else zero for g in range(heads)], axis=1))
    return jnp.concatenate(rows, axis=0)


def pick_heads(x, heads):
    return jnp.concatenate(
        [
            x[h * HEAD_DIM : (h + 1) * HEAD_DIM, h * BLOCK : (h + 1) * BLOCK]
            for h in range(heads)
        ],
        axis=0,
    )


def slot_of(lists_ref, counts_ref, row, j, first_block, ext):
    return jnp.where(j < counts_ref[row], lists_ref[row, j] - first_block, ext)


def lane_block(i):
    return pl.ds(pl.multiple_of(i * BLOCK, BLOCK), BLOCK)


def attend_kernel(
    total, lists_ref, counts_ref, q_ref, k_ref, v_ref, lo_ref, hi_ref,
    ka_ref, va_ref, kn_ref, att_ref, t_ref, vn_ref, s_ref,
):
    chans = q_ref.shape[0]
    heads = chans // HEAD_DIM
    blocks = q_ref.shape[1] // BLOCK
    ext = blocks + 2 * RIM
    width = heads * BLOCK
    first_block = lax.axis_index("band") * blocks - RIM

    at = lax.broadcasted_iota(jnp.int32, (ext, BLOCK), 0) * BLOCK
    at = at + lax.broadcasted_iota(jnp.int32, (ext, BLOCK), 1) + first_block * BLOCK
    at = jnp.clip(at, 0, total - 1).astype(F32)
    logw = jnp.log(jnp.sin(jnp.pi * (at + 0.5) / total))
    hi, mid, low = split3(logw * (1.0 / SCALE))
    pad = jnp.zeros((BLOCK - chans - AUG, BLOCK), BF16)
    v_aug = aug_rows([1.0, 1.0, 1.0], BLOCK)
    for b in range(ext + 1):
        if b == ext:
            k_blk = jnp.zeros((chans, BLOCK), BF16)
            v_blk = k_blk
            k_aug = aug_rows([MASKED, 0.0, 0.0, 1.0, 1.0, 1.0], BLOCK)
        else:
            if b < RIM:
                at_lanes = slice(b * BLOCK, (b + 1) * BLOCK)
                k_blk, v_blk = lo_ref[0, :, at_lanes], lo_ref[1, :, at_lanes]
            elif b < RIM + blocks:
                at_lanes = slice((b - RIM) * BLOCK, (b - RIM + 1) * BLOCK)
                k_blk, v_blk = k_ref[:, at_lanes], v_ref[:, at_lanes]
            else:
                at_lanes = slice((b - RIM - blocks) * BLOCK, (b - RIM - blocks + 1) * BLOCK)
                k_blk, v_blk = hi_ref[0, :, at_lanes], hi_ref[1, :, at_lanes]
            k_aug = aug_rows(
                [hi[b : b + 1], mid[b : b + 1], low[b : b + 1], 1.0, 1.0, 1.0], BLOCK
            )
        kn_ref[b] = k_blk
        v_with = jnp.concatenate([v_blk, v_aug], axis=0)
        vn_ref[b] = v_with
        ka_ref[b] = jnp.concatenate([k_blk, k_aug, pad], axis=0).T
        va_ref[b] = jnp.concatenate([v_with, pad], axis=0).T

    ones = aug_rows([1.0, 1.0, 1.0], width)
    pad_w = jnp.zeros((BLOCK - chans - AUG, width), BF16)

    def body(i, carry):
        q_aug = jnp.concatenate([spread_heads(q_ref[:, lane_block(i)], heads), ones, pad_w], axis=0)
        slots = [slot_of(lists_ref, counts_ref, i, j, first_block, ext) for j in range(MAX_KEYS)]
        peak = None
        for j in range(MAX_KEYS):
            s = dot(ka_ref[slots[j]], q_aug)
            s_ref[j * BLOCK : (j + 1) * BLOCK] = s
            top = jnp.max(s.reshape(BLOCK // 8, 8, width), axis=0)
            peak = top if peak is None else jnp.maximum(peak, top)
        peak = jnp.max(peak, axis=0, keepdims=True)
        acc = jnp.zeros((chans + AUG, width), F32)
        for j in range(0, MAX_KEYS, 2):
            e = jnp.exp2((s_ref[j * BLOCK : (j + 2) * BLOCK] - peak) * RAW)
            e_hi = e.astype(BF16)
            e_lo = (e - e_hi.astype(F32)).astype(BF16)
            v_pair = jnp.concatenate([vn_ref[slots[j]], vn_ref[slots[j + 1]]], axis=1)
            acc = acc + dot(v_pair, e_hi) + dot(v_pair, e_lo)
        whole = acc[chans : chans + 1]
        att_ref[:, lane_block(i)] = pick_heads(acc[:chans] * (1.0 / whole), heads)
        t_ref[pl.ds(i, 1), :] = peak + jnp.log2(whole) * (1.0 / RAW)
        return carry

    lax.fori_loop(0, blocks, body, 0)


def project_kernel(count, att_ref, w_ref, *refs):
    parts, (grad_ref, gw_ref) = refs[:count], refs[count:]
    depth = parts[0].shape[0]
    full = jnp.concatenate([p[...] for p in parts], axis=0)
    here = lax.axis_index("head") * depth
    wide = count * depth
    turned = pltpu.roll(w_ref[...].astype(F32), lax.rem(wide - here, wide), 1).astype(BF16)
    grad_ref[...] = dot(turned, full).astype(BF16)
    gw_ref[...] = pltpu.roll(dot_nt(att_ref[...].astype(BF16), full), here, 1)


def grads_kernel(
    lists_ref, counts_ref, q_ref, g_ref, att_ref, t_ref, ka_ref, va_ref, kn_ref,
    dq_ref, own_ref, lo_ref, hi_ref, acc_ref,
):
    chans = q_ref.shape[0]
    heads = chans // HEAD_DIM
    blocks = q_ref.shape[1] // BLOCK
    ext = blocks + 2 * RIM
    width = heads * BLOCK
    first_block = lax.axis_index("band") * blocks - RIM
    acc_ref[...] = jnp.zeros_like(acc_ref)
    pad_w = jnp.zeros((BLOCK - chans - AUG, width), BF16)
    none = jnp.zeros((chans, width), BF16)

    def body(i, carry):
        g_blk = g_ref[:, lane_block(i)]
        prod = g_blk.astype(F32) * att_ref[:, lane_block(i)]
        spread = jnp.concatenate(
            [
                jnp.sum(prod[h * HEAD_DIM : (h + 1) * HEAD_DIM], axis=0, keepdims=True)
                for h in range(heads)
            ],
            axis=1,
        )
        q_wide = spread_heads(q_ref[:, lane_block(i)], heads)
        g_wide = spread_heads(g_blk, heads)
        t_hi, t_mid, t_low = split3(-t_ref[pl.ds(i, 1), :])
        q_aug = jnp.concatenate(
            [q_wide, aug_rows([1.0, 1.0, 1.0, t_hi, t_mid, t_low], width), pad_w], axis=0
        )
        g_aug = jnp.concatenate([g_wide, aug_rows(split3(-spread), width), pad_w], axis=0)
        q_out = jnp.concatenate([q_wide, none], axis=0)
        g_out = jnp.concatenate([none, g_wide], axis=0)
        slots = [slot_of(lists_ref, counts_ref, i, j, first_block, ext) for j in range(MAX_KEYS)]
        dq = jnp.zeros((chans, width), F32)
        for j in range(0, MAX_KEYS, 2):
            lows = []
            for slot in slots[j : j + 2]:
                probs = jnp.exp2(dot(ka_ref[slot], q_aug) * RAW)
                dlow = (probs * dot(va_ref[slot], g_aug)).astype(BF16)
                acc_ref[slot] += dot_nt(probs.astype(BF16), g_out) + dot_nt(dlow, q_out)
                lows.append(dlow)
            k_pair = jnp.concatenate([kn_ref[slots[j]], kn_ref[slots[j + 1]]], axis=1)
            dq = dq + dot(k_pair, jnp.concatenate(lows, axis=0))
        dq_ref[:, lane_block(i)] = (pick_heads(dq, heads) * SCALE).astype(BF16)
        return carry

    lax.fori_loop(0, blocks, body, 0)
    lane = lax.broadcasted_iota(jnp.int32, (BLOCK, 2 * chans), 1)
    factor = jnp.where(lane < chans, SCALE, 1.0).astype(F32)
    for b in range(ext):
        x = acc_ref[b] * factor
        if b < RIM:
            lo_ref[b] = x.astype(BF16)
        elif b < RIM + blocks:
            own_ref[b - RIM] = x
        else:
            hi_ref[b - RIM - blocks] = x.astype(BF16)


def join_kernel(own_ref, below_ref, above_ref, dk_ref, dv_ref):
    blocks = own_ref.shape[0]
    chans = dk_ref.shape[0]
    for b in range(blocks):
        x = own_ref[b]
        if b < RIM:
            x = x + below_ref[b].astype(F32)
        if b >= blocks - RIM:
            x = x + above_ref[b - (blocks - RIM)].astype(F32)
        x = x.T
        dk_ref[:, b * BLOCK : (b + 1) * BLOCK] = x[:chans].astype(BF16)
        dv_ref[:, b * BLOCK : (b + 1) * BLOCK] = x[chans:].astype(BF16)


def kernel_call(body, outs, operands, scratch=(), smem=0, flops=0, transcendentals=0):
    size = sum(x.size * x.dtype.itemsize for x in operands + outs)
    vmem = pl.BlockSpec(memory_space=pltpu.VMEM)
    scalars = pl.BlockSpec(memory_space=pltpu.SMEM)
    return pl.pallas_call(
        body,
        out_shape=outs,
        in_specs=[scalars] * smem + [vmem] * (len(operands) - smem),
        out_specs=[vmem] * len(outs),
        scratch_shapes=list(scratch),
        compiler_params=pltpu.CompilerParams(vmem_limit_bytes=VMEM_LIMIT),
        cost_estimate=pl.CostEstimate(
            flops=flops, bytes_accessed=size, transcendentals=transcendentals
        ),
    )(*operands)


def moved(value, axis, steps):
    count = lax.axis_size(axis)
    return lax.ppermute(
        value, axis, [(i, i + steps) for i in range(count) if 0 <= i + steps < count]
    )


def sum_over(value, axis):
    count = lax.axis_size(axis)
    if count & (count - 1):
        return lax.psum(value, axis)
    step = 1
    while step < count:
        value = value + lax.ppermute(value, axis, [(i, i ^ step) for i in range(count)])
        step *= 2
    return value


def shards(queries, keys, values, grad_out, w_out, key_lists, key_counts):
    chans, tokens = queries.shape
    blocks = tokens // BLOCK
    heads = chans // HEAD_DIM
    ext = blocks + 2 * RIM
    width = heads * BLOCK
    total = tokens * lax.axis_size("band")
    head_count = lax.axis_size("head")
    rim = RIM * BLOCK
    shape = jax.ShapeDtypeStruct
    pairs = blocks * MAX_KEYS * width * BLOCK

    low = moved(jnp.stack([keys[:, -rim:], values[:, -rim:]]), "band", 1)
    high = moved(jnp.stack([keys[:, :rim], values[:, :rim]]), "band", -1)
    parts = [grad_out] + [
        lax.ppermute(grad_out, "head", [((i + s) % head_count, i) for i in range(head_count)])
        for s in range(1, head_count)
    ]
    ka, va, kn, att, t = kernel_call(
        functools.partial(attend_kernel, total),
        [
            shape((ext + 1, BLOCK, BLOCK), BF16),
            shape((ext + 1, BLOCK, BLOCK), BF16),
            shape((ext + 1, chans, BLOCK), BF16),
            shape((chans, tokens), F32),
            shape((blocks, width), F32),
        ],
        [key_lists, key_counts, queries, keys, values, low, high],
        [pltpu.VMEM((ext + 1, chans + AUG, BLOCK), BF16), pltpu.VMEM((MAX_KEYS * BLOCK, width), F32)],
        smem=2,
        flops=3 * 2 * pairs * BLOCK,
        transcendentals=pairs,
    )
    grad_att, part_w = kernel_call(
        functools.partial(project_kernel, head_count),
        [shape((chans, tokens), BF16), shape(w_out.shape, F32)],
        [att, w_out] + parts,
        flops=4 * w_out.size * tokens,
    )
    dq, own, lo, hi = kernel_call(
        grads_kernel,
        [
            shape((chans, tokens), BF16),
            shape((blocks, BLOCK, 2 * chans), F32),
            shape((RIM, BLOCK, 2 * chans), BF16),
            shape((RIM, BLOCK, 2 * chans), BF16),
        ],
        [key_lists, key_counts, queries, grad_att, att, t, ka, va, kn],
        [pltpu.VMEM((ext + 1, BLOCK, 2 * chans), F32)],
        smem=2,
        flops=5 * 2 * pairs * BLOCK,
        transcendentals=pairs,
    )
    above = moved(lo, "band", -1)
    below = moved(hi, "band", 1)
    grad_w = sum_over(part_w, "band")
    dk, dv = kernel_call(
        join_kernel,
        [shape((chans, tokens), BF16), shape((chans, tokens), BF16)],
        [own, below, above],
    )
    return (dq, dk, dv, grad_w)


def solution(mesh):
    in_specs = (
        P("head", "band"),
        P("head", "band"),
        P("head", "band"),
        P("head", "band"),
        P("head", None),
        P("band", None),
        P("band"),
    )
    out_specs = (P("head", "band"), P("head", "band"), P("head", "band"), P("head", None))
    return jax.shard_map(shards, mesh=mesh, in_specs=in_specs, out_specs=out_specs, check_vma=False)
```

time: 242 us -> 59.1 us (0.24); the launches traced: 239 us -> 58.8 us
  local copies, waits for them, and re-layouts: 63.9 us -> 2.01 us
  other arithmetic: 52.8 us -> 1.71 us
  matrix products: 36 us -> 0 us
  blocking collectives: 27.5 us -> 0 us
  waiting for transfers between devices: 34.1 us -> 9.26 us
  Pallas kernels: 0 us -> 24.3 us
  between operations: 14.3 us -> 0.81 us
  starting transfers between devices: 8.85 us -> 20.7 us
    dot_general x50 -> x0, matrix products: 36 us -> none  [the longest x8 14.5 us: block_grads(): jnp.einsum('hqk,hdq->hdk', dscores, query_h, preferred_element_type=jnp.f...]
    reduce_scatter x1 -> x0, waiting for transfers between devices: 34.1 us -> none  [shards(): lax.psum_scatter(partial_w, 'band', scatter_dimension=1, tiled=True)]
    gather x40 -> x0, local copies, waits for them, and re-layouts: 31 us -> none  [the longest x16 13.3 us: block_grads(): picked_k = key_ext[:, slots].reshape(heads_here, HEAD_DIM, span)]
    all_gather x2 -> x0, blocking collectives: 27.5 us -> none  [the longest x1 18.4 us: shards(): full_grad = lax.all_gather(grad_out, 'head', axis=0, tiled=True)]
    pallas_call x0 -> x4, Pallas kernels: none -> 24.3 us  [kernel_call(): pl.pallas_call(body, out_shape=outs, in_specs=[scalars] * smem + [vmem] *...]
    scatter x8 -> x0, other arithmetic: 16 us -> none  [run_width(): att_all = att_all.at[:, index].set(attended.astype(jnp.bfloat16))]
    scatter-add x16 -> x0, other arithmetic: 14.2 us -> none  [the longest x8 7.1 us: run_width(): acc_v = acc_v.at[:, slots].add(dvalue)]
    ppermute x4 -> x10, starting transfers between devices: 8.81 us -> 20.7 us  [the longest x4 7.8 us: moved(): lax.ppermute(value, axis, [(i, i + steps) for i in range(count) if 0 <= i...]
  transfers between devices with their start and end apart: 5 -> 10, of which waited for: 1 -> 3; matrix products, arithmetic and copies ran while one was open for 2% -> 1% of each run, Pallas kernels for 0% -> 15%
where the time goes in v1:
time: 59.1 us; the launch traced here: 58.8 us
  Pallas kernels  24.3 us (41%)
  starting transfers between devices  20.7 us (35%)
  waiting for transfers between devices  9.26 us (16%)
  local copies, waits for them, and re-layouts  2.01 us (3%)
  other arithmetic  1.71 us (3%)
  between operations  0.81 us (1%)
    pallas_call x4, Pallas kernels, kernel_call(): pl.pallas_call(body, out_shape=outs, in_specs=[scalars] * smem + [vmem] *...  24.3 us
    ppermute x3, waiting for transfers between devices, sum_over(): lax.ppermute(value, axis, [(i, i ^ step) for i in range(count)])  9.24 us
    ppermute x4, starting transfers between devices, moved(): lax.ppermute(value, axis, [(i, i + steps) for i in range(count) if 0 <= i...  7.8 us
    ppermute x3, starting transfers between devices, sum_over(): lax.ppermute(value, axis, [(i, i ^ step) for i in range(count)])  6.76 us
    ppermute x3, starting transfers between devices, shards(): lax.ppermute(grad_out, 'head', [((i + s) % head_count, i) for i in range(...  6.13 us
    unnamed x16, local copies, waits for them, and re-layouts  2.01 us
  transfers between devices with their start and end apart: 10, of which 3 were waited for; matrix products, arithmetic and copies ran while one was open for 1% of the time, Pallas kernels for 15%

profile of v1, /device:TPU:0, one launch (start us, length us, event | category | flops | bytes accessed | tf_op | source)
XLA Modules:
  0.0 58.8 jit_solution(18214407099491592761)
XLA Ops:
  0.7 1.1 %pad_maximum_fusion = bf16[2,64,1024]{2,1,0:T(8,128)(2,1)S(1)} fusion(bf16[1,64,1024]{2,1,0:T(8,128)(2,1)} %bitcast.3, bf16[1,64,1024]{2,1,0:T(8,128)(2,1)} %bitcast.2), kind=kLoop, calls=%fused_computation | loop fusion | flops 131072 | bytes 524288 | tf_op jit(solution)/shard_map/stack | solution.py:277
  1.7 0.0 copy-start.3
  1.7 1.3 %collective-permute-start.1 = (bf16[2,64,1024]{2,1,0:T(8,128)(2,1)S(1)}, bf16[2,64,1024]{2,1,0:T(8,128)(2,1)S(1)}, u32[]{:S(2)}, u32[]{:S(2)}) collective-permute-start(bf16[2,64,1024]{2,1,0:T(8,128)(2,1)S(1)} %pad_maximum_fusion), channel_id=1, source_target_pairs={{4,0},{8,4},{12,8},{16,12},{20,16},{24,20},{28,24},{5,1},{9,5},{13... | collective-permute-start | bytes 786440 | tf_op jit(solution)/shard_map/ppermute | solution.py:249
  3.0 3.0 %collective-permute-start = (bf16[2,64,1024]{2,1,0:T(8,128)(2,1)S(1)}, bf16[2,64,1024]{2,1,0:T(8,128)(2,1)S(1)}, u32[]{:S(2)}, u32[]{:S(2)}) collective-permute-start(bf16[2,64,1024]{2,1,0:T(8,128)(2,1)S(1)} %pad_maximum_fusion), channel_id=1, source_target_pairs={{0,4},{4,8},{8,12},{12,16},{16,20},{20,24},{24,28},{1,5},{5,9},{9,... | collective-permute-start | bytes 786440 | tf_op jit(solution)/shard_map/ppermute | solution.py:249
  6.1 4.1 %collective-permute-start.3 = (bf16[64,1024]{1,0:T(8,128)(2,1)S(1)}, bf16[64,1024]{1,0:T(8,128)(2,1)S(1)}, u32[]{:S(2)}, u32[]{:S(2)}) collective-permute-start(bf16[64,1024]{1,0:T(8,128)(2,1)S(1)} %copy-done), channel_id=1, source_target_pairs={{2,0},{3,1},{0,2},{1,3},{6,4},{7,5},{4,6},{5,7},{10,8},{11,9},{8,1... | collective-permute-start | bytes 393224 | tf_op jit(solution)/shard_map/ppermute | solution.py:280
  10.2 1.3 %collective-permute-start.2 = (bf16[64,1024]{1,0:T(8,128)(2,1)S(1)}, bf16[64,1024]{1,0:T(8,128)(2,1)S(1)}, u32[]{:S(2)}, u32[]{:S(2)}) collective-permute-start(bf16[64,1024]{1,0:T(8,128)(2,1)S(1)} %copy-done), channel_id=1, source_target_pairs={{1,0},{2,1},{3,2},{0,3},{5,4},{6,5},{7,6},{4,7},{9,8},{10,9},{11,1... | collective-permute-start | bytes 393224 | tf_op jit(solution)/shard_map/ppermute | solution.py:280
  11.6 0.7 %collective-permute-start.4 = (bf16[64,1024]{1,0:T(8,128)(2,1)S(1)}, bf16[64,1024]{1,0:T(8,128)(2,1)S(1)}, u32[]{:S(2)}, u32[]{:S(2)}) collective-permute-start(bf16[64,1024]{1,0:T(8,128)(2,1)S(1)} %copy-done), channel_id=1, source_target_pairs={{3,0},{0,1},{1,2},{2,3},{7,4},{4,5},{5,6},{6,7},{11,8},{8,9},{9,10... | collective-permute-start | bytes 393224 | tf_op jit(solution)/shard_map/ppermute | solution.py:280
  12.3 0.7 %copy-done.5 = s32[8,8]{1,0:T(8,128)S(1)} copy-done((s32[8,8]{1,0:T(8,128)S(1)}, s32[8,8]{1,0:T(8,128)}, u32[]{:S(2)}) %copy-start.5) | copy-done | bytes 280
  13.0 0.7 %copy-done.6 = s32[8]{0:T(128)S(1)} copy-done((s32[8]{0:T(128)S(1)}, s32[8]{0:T(128)}, u32[]{:S(2)}) %copy-start.6) | copy-done | bytes 56
  13.6 8.8 %shard_map.102 = (bf16[25,128,128]{2,1,0:T(8,128)(2,1)S(1)}, bf16[25,128,128]{2,1,0:T(8,128)(2,1)S(1)}, bf16[25,64,128]{2,1,0:T(8,128)(2,1)S(1)}, f32[64,1024]{1,0:T(8,128)S(1)}, f32[8,256]{1,0:T(8,128)S(1)}) custom-call(s32[8,8]{1,0:T(8,128)S(1)} %copy-done.5, s32[8]{0:T(128)S(1)} %copy-done.6, bf16[64,1024]{1,0:T(8,128)(2,1)S(1)} %copy-done.4, ...), custom_call_target="tpu_custom_call" | custom-call | flops 1610612736 | bytes 3236128 | tf_op jit(solution)/shard_map/pallas_call | solution.py:234
  22.5 0.5 shard_map.103
  22.9 0.0 copy-start.7
  23.0 0.6 %copy-done.7 = s32[8]{0:T(128)S(1)} copy-done((s32[8]{0:T(128)S(1)}, s32[8]{0:T(128)}, u32[]{:S(2)}) %copy-start.7) | copy-done | bytes 56
  23.6 14.2 %shard_map.104 = (bf16[64,1024]{1,0:T(8,128)(2,1)}, f32[8,128,128]{2,1,0:T(8,128)S(1)}, bf16[8,128,128]{2,1,0:T(8,128)(2,1)S(1)}, bf16[8,128,128]{2,1,0:T(8,128)(2,1)S(1)}) custom-call(s32[8,8]{1,0:T(8,128)S(1)} %copy-done.5, s32[8]{0:T(128)S(1)} %copy-done.7, bf16[64,1024]{1,0:T(8,128)(2,1)S(1)} %copy-done.4, bf16[64,1024]{1,0:T(8,128)(2,1)S(1)} %get-tuple-element.18.g_ref, ...), custom_call_target="tpu_custom_call" | custom-call | flops 2684354560 | bytes 3760416 | tf_op jit(solution)/shard_map/pallas_call | solution.py:234
  37.8 2.2 %collective-permute-start.5 = (bf16[8,128,128]{2,1,0:T(8,128)(2,1)S(1)}, bf16[8,128,128]{2,1,0:T(8,128)(2,1)S(1)}, u32[]{:S(2)}, u32[]{:S(2)}) collective-permute-start(bf16[8,128,128]{2,1,0:T(8,128)(2,1)S(1)} %get-tuple-element.25), channel_id=1, source_target_pairs={{0,4},{4,8},{8,12},{12,16},{16,20},{20,24},{24,28},{1,5},{5,9},{9,... | collective-permute-start | bytes 786440 | tf_op jit(solution)/shard_map/ppermute | solution.py:249
  40.0 1.3 %collective-permute-start.6 = (bf16[8,128,128]{2,1,0:T(8,128)(2,1)S(1)}, bf16[8,128,128]{2,1,0:T(8,128)(2,1)S(1)}, u32[]{:S(2)}, u32[]{:S(2)}) collective-permute-start(bf16[8,128,128]{2,1,0:T(8,128)(2,1)S(1)} %get-tuple-element.26), channel_id=1, source_target_pairs={{4,0},{8,4},{12,8},{16,12},{20,16},{24,20},{28,24},{5,1},{9,5},{13... | collective-permute-start | bytes 786440 | tf_op jit(solution)/shard_map/ppermute | solution.py:249
  41.3 2.6 %collective-permute-start.7 = (f32[64,256]{1,0:T(8,128)S(1)}, f32[64,256]{1,0:T(8,128)S(1)}, u32[]{:S(2)}, u32[]{:S(2)}) collective-permute-start(f32[64,256]{1,0:T(8,128)S(1)} %get-tuple-element.29), channel_id=1, source_target_pairs={{0,4},{4,0},{8,12},{12,8},{16,20},{20,16},{24,28},{28,24},{1,5},{5... | collective-permute-start | bytes 196616 | tf_op jit(solution)/shard_map/ppermute | solution.py:260
  43.9 1.0 %collective-permute-done.7 = f32[64,256]{1,0:T(8,128)S(1)} collective-permute-done((f32[64,256]{1,0:T(8,128)S(1)}, f32[64,256]{1,0:T(8,128)S(1)}, u32[]{:S(2)}, u32[]{:S(2)}) %collective-permute-start.7) | collective-permute-done | bytes 65568 | tf_op jit(solution)/shard_map/ppermute | solution.py:260
  44.9 3.3 %collective-permute-start.8 = (f32[64,256]{1,0:T(8,128)S(1)}, f32[64,256]{1,0:T(8,128)S(1)}, u32[]{:S(2)}, u32[]{:S(2)}) collective-permute-start(f32[64,256]{1,0:T(8,128)S(1)} %add.9), channel_id=1, source_target_pairs={{0,8},{4,12},{8,0},{12,4},{16,24},{20,28},{24,16},{28,20},{1,9},{5... | collective-permute-start | bytes 196616 | tf_op jit(solution)/shard_map/ppermute | solution.py:260
  48.3 4.7 %collective-permute-done.8 = f32[64,256]{1,0:T(8,128)S(1)} collective-permute-done((f32[64,256]{1,0:T(8,128)S(1)}, f32[64,256]{1,0:T(8,128)S(1)}, u32[]{:S(2)}, u32[]{:S(2)}) %collective-permute-start.8) | collective-permute-done | bytes 65568 | tf_op jit(solution)/shard_map/ppermute | solution.py:260
  53.0 0.9 %collective-permute-start.9 = (f32[64,256]{1,0:T(8,128)S(1)}, f32[64,256]{1,0:T(8,128)S(1)}, u32[]{:S(2)}, u32[]{:S(2)}) collective-permute-start(f32[64,256]{1,0:T(8,128)S(1)} %add.10), channel_id=1, source_target_pairs={{0,16},{4,20},{8,24},{12,28},{16,0},{20,4},{24,8},{28,12},{1,17},{... | collective-permute-start | bytes 196616 | tf_op jit(solution)/shard_map/ppermute | solution.py:260
  53.9 3.5 %collective-permute-done.9 = f32[64,256]{1,0:T(8,128)S(1)} collective-permute-done((f32[64,256]{1,0:T(8,128)S(1)}, f32[64,256]{1,0:T(8,128)S(1)}, u32[]{:S(2)}, u32[]{:S(2)}) %collective-permute-start.9) | collective-permute-done | bytes 65568 | tf_op jit(solution)/shard_map/ppermute | solution.py:260
  57.3 0.6 %add.11 = f32[64,256]{1,0:T(8,128)} add(f32[64,256]{1,0:T(8,128)S(1)} %add.10, f32[64,256]{1,0:T(8,128)S(1)} %collective-permute-done.9) | non-fusion elementwise | flops 16384 | bytes 196608 | tf_op jit(solution)/shard_map/add | solution.py:260
  58.0 0.8 %shard_map.105 = (bf16[64,1024]{1,0:T(8,128)(2,1)}, bf16[64,1024]{1,0:T(8,128)(2,1)}) custom-call(f32[8,128,128]{2,1,0:T(8,128)S(1)} %get-tuple-element.24.own_ref, bf16[8,128,128]{2,1,0:T(8,128)(2,1)S(1)} %collective-permute-done.5.below_ref, bf16[8,128,128]{2,1,0:T(8,128)(2,1)S(1)} %collective-permute-done.6.above_ref), custom_call_target="tpu_custom_call" | custom-call | bytes 1310720 | tf_op jit(solution)/shard_map/pallas_call | solution.py:234
  (20 shorter events, 0.1 us)
Async XLA Ops:
  0.6 5.5 %copy-start = (bf16[64,1024]{1,0:T(8,128)(2,1)S(1)}, bf16[64,1024]{1,0:T(8,128)(2,1)}, u32[]{:S(2)}) copy-start(bf16[64,1024]{1,0:T(8,128)(2,1)} %refs_0_.1) | copy-start | bytes 393220
  0.6 11.6 %copy-start.1 = (bf16[64,1024]{1,0:T(8,128)(2,1)S(1)}, bf16[64,1024]{1,0:T(8,128)(2,1)}, u32[]{:S(2)}) copy-start(bf16[64,1024]{1,0:T(8,128)(2,1)} %k_ref.1) | copy-start | bytes 393220
  0.7 11.6 %copy-start.2 = (bf16[64,1024]{1,0:T(8,128)(2,1)S(1)}, bf16[64,1024]{1,0:T(8,128)(2,1)}, u32[]{:S(2)}) copy-start(bf16[64,1024]{1,0:T(8,128)(2,1)} %v_ref.1) | copy-start | bytes 393220
  0.7 11.6 %copy-start.4 = (bf16[64,1024]{1,0:T(8,128)(2,1)S(1)}, bf16[64,1024]{1,0:T(8,128)(2,1)}, u32[]{:S(2)}) copy-start(bf16[64,1024]{1,0:T(8,128)(2,1)} %q_ref.3) | copy-start | bytes 393220
  1.7 20.7 %copy-start.3 = (bf16[64,256]{1,0:T(8,128)(2,1)S(1)}, bf16[64,256]{1,0:T(8,128)(2,1)}, u32[]{:S(2)}) copy-start(bf16[64,256]{1,0:T(8,128)(2,1)} %w_ref.1) | copy-start | bytes 98308
  1.7 10.5 %collective-permute-start.1 = (bf16[2,64,1024]{2,1,0:T(8,128)(2,1)S(1)}, bf16[2,64,1024]{2,1,0:T(8,128)(2,1)S(1)}, u32[]{:S(2)}, u32[]{:S(2)}) collective-permute-start(bf16[2,64,1024]{2,1,0:T(8,128)(2,1)S(1)} %pad_maximum_fusion), channel_id=1, source_target_pairs={{4,0},{8,4},{12,8},{16,12},{20,16},{24,20},{28,24},{5,1},{9,5},{13... | collective-permute-start | bytes 786440 | tf_op jit(solution)/shard_map/ppermute | solution.py:249
  3.0 9.2 %collective-permute-start = (bf16[2,64,1024]{2,1,0:T(8,128)(2,1)S(1)}, bf16[2,64,1024]{2,1,0:T(8,128)(2,1)S(1)}, u32[]{:S(2)}, u32[]{:S(2)}) collective-permute-start(bf16[2,64,1024]{2,1,0:T(8,128)(2,1)S(1)} %pad_maximum_fusion), channel_id=1, source_target_pairs={{0,4},{4,8},{8,12},{12,16},{16,20},{20,24},{24,28},{1,5},{5,9},{9,... | collective-permute-start | bytes 786440 | tf_op jit(solution)/shard_map/ppermute | solution.py:249
  6.1 16.3 %collective-permute-start.3 = (bf16[64,1024]{1,0:T(8,128)(2,1)S(1)}, bf16[64,1024]{1,0:T(8,128)(2,1)S(1)}, u32[]{:S(2)}, u32[]{:S(2)}) collective-permute-start(bf16[64,1024]{1,0:T(8,128)(2,1)S(1)} %copy-done), channel_id=1, source_target_pairs={{2,0},{3,1},{0,2},{1,3},{6,4},{7,5},{4,6},{5,7},{10,8},{11,9},{8,1... | collective-permute-start | bytes 393224 | tf_op jit(solution)/shard_map/ppermute | solution.py:280
  10.2 12.2 %collective-permute-start.2 = (bf16[64,1024]{1,0:T(8,128)(2,1)S(1)}, bf16[64,1024]{1,0:T(8,128)(2,1)S(1)}, u32[]{:S(2)}, u32[]{:S(2)}) collective-permute-start(bf16[64,1024]{1,0:T(8,128)(2,1)S(1)} %copy-done), channel_id=1, source_target_pairs={{1,0},{2,1},{3,2},{0,3},{5,4},{6,5},{7,6},{4,7},{9,8},{10,9},{11,1... | collective-permute-start | bytes 393224 | tf_op jit(solution)/shard_map/ppermute | solution.py:280
  11.6 10.9 %collective-permute-start.4 = (bf16[64,1024]{1,0:T(8,128)(2,1)S(1)}, bf16[64,1024]{1,0:T(8,128)(2,1)S(1)}, u32[]{:S(2)}, u32[]{:S(2)}) collective-permute-start(bf16[64,1024]{1,0:T(8,128)(2,1)S(1)} %copy-done), channel_id=1, source_target_pairs={{3,0},{0,1},{1,2},{2,3},{7,4},{4,5},{5,6},{6,7},{11,8},{8,9},{9,10... | collective-permute-start | bytes 393224 | tf_op jit(solution)/shard_map/ppermute | solution.py:280
  12.3 0.7 %copy-start.5 = (s32[8,8]{1,0:T(8,128)S(1)}, s32[8,8]{1,0:T(8,128)}, u32[]{:S(2)}) copy-start(s32[8,8]{1,0:T(8,128)} %lists_ref.3) | copy-start | bytes 772
  13.0 0.7 %copy-start.6 = (s32[8]{0:T(128)S(1)}, s32[8]{0:T(128)}, u32[]{:S(2)}) copy-start(s32[8]{0:T(128)} %counts_ref.3) | copy-start | bytes 100
  22.9 0.7 %copy-start.7 = (s32[8]{0:T(128)S(1)}, s32[8]{0:T(128)}, u32[]{:S(2)}) copy-start(s32[8]{0:T(128)} %counts_ref.3) | copy-start | bytes 100
  37.8 20.1 %collective-permute-start.5 = (bf16[8,128,128]{2,1,0:T(8,128)(2,1)S(1)}, bf16[8,128,128]{2,1,0:T(8,128)(2,1)S(1)}, u32[]{:S(2)}, u32[]{:S(2)}) collective-permute-start(bf16[8,128,128]{2,1,0:T(8,128)(2,1)S(1)} %get-tuple-element.25), channel_id=1, source_target_pairs={{0,4},{4,8},{8,12},{12,16},{16,20},{20,24},{24,28},{1,5},{5,9},{9,... | collective-permute-start | bytes 786440 | tf_op jit(solution)/shard_map/ppermute | solution.py:249
  40.0 18.0 %collective-permute-start.6 = (bf16[8,128,128]{2,1,0:T(8,128)(2,1)S(1)}, bf16[8,128,128]{2,1,0:T(8,128)(2,1)S(1)}, u32[]{:S(2)}, u32[]{:S(2)}) collective-permute-start(bf16[8,128,128]{2,1,0:T(8,128)(2,1)S(1)} %get-tuple-element.26), channel_id=1, source_target_pairs={{4,0},{8,4},{12,8},{16,12},{20,16},{24,20},{28,24},{5,1},{9,5},{13... | collective-permute-start | bytes 786440 | tf_op jit(solution)/shard_map/ppermute | solution.py:249
  41.3 3.6 %collective-permute-start.7 = (f32[64,256]{1,0:T(8,128)S(1)}, f32[64,256]{1,0:T(8,128)S(1)}, u32[]{:S(2)}, u32[]{:S(2)}) collective-permute-start(f32[64,256]{1,0:T(8,128)S(1)} %get-tuple-element.29), channel_id=1, source_target_pairs={{0,4},{4,0},{8,12},{12,8},{16,20},{20,16},{24,28},{28,24},{1,5},{5... | collective-permute-start | bytes 196616 | tf_op jit(solution)/shard_map/ppermute | solution.py:260
  44.9 8.1 %collective-permute-start.8 = (f32[64,256]{1,0:T(8,128)S(1)}, f32[64,256]{1,0:T(8,128)S(1)}, u32[]{:S(2)}, u32[]{:S(2)}) collective-permute-start(f32[64,256]{1,0:T(8,128)S(1)} %add.9), channel_id=1, source_target_pairs={{0,8},{4,12},{8,0},{12,4},{16,24},{20,28},{24,16},{28,20},{1,9},{5... | collective-permute-start | bytes 196616 | tf_op jit(solution)/shard_map/ppermute | solution.py:260
  53.0 4.3 %collective-permute-start.9 = (f32[64,256]{1,0:T(8,128)S(1)}, f32[64,256]{1,0:T(8,128)S(1)}, u32[]{:S(2)}, u32[]{:S(2)}) collective-permute-start(f32[64,256]{1,0:T(8,128)S(1)} %add.10), channel_id=1, source_target_pairs={{0,16},{4,20},{8,24},{12,28},{16,0},{20,4},{24,8},{28,12},{1,17},{... | collective-permute-start | bytes 196616 | tf_op jit(solution)/shard_map/ppermute | solution.py:260

commit v2 on v1

--- a/solution.py
+++ b/solution.py
@@ -120,26 +120,20 @@
     def body(i, carry):
         q_aug = jnp.concatenate([spread_heads(q_ref[:, lane_block(i)], heads), ones, pad_w], axis=0)
         slots = [slot_of(lists_ref, counts_ref, i, j, first_block, ext) for j in range(MAX_KEYS)]
-        peak = None
-        for j in range(MAX_KEYS):
-            s = dot(ka_ref[slots[j]], q_aug)
-            s_ref[j * BLOCK : (j + 1) * BLOCK] = s
-            top = jnp.max(s.reshape(BLOCK // 8, 8, width), axis=0)
-            peak = top if peak is None else jnp.maximum(peak, top)
-        peak = jnp.max(peak, axis=0, keepdims=True)
-        acc = jnp.zeros((chans + AUG, width), F32)
-        for j in range(0, MAX_KEYS, 2):
-            e = jnp.exp2((s_ref[j * BLOCK : (j + 2) * BLOCK] - peak) * RAW)
-            e_hi = e.astype(BF16)
-            e_lo = (e - e_hi.astype(F32)).astype(BF16)
-            v_pair = jnp.concatenate([vn_ref[slots[j]], vn_ref[slots[j + 1]]], axis=1)
-            acc = acc + dot(v_pair, e_hi) + dot(v_pair, e_lo)
+        k_rows = jnp.concatenate([ka_ref[slot] for slot in slots], axis=0)
+        s = dot(k_rows, q_aug)
+        peak = jnp.max(jnp.max(s.reshape(-1, 8, width), axis=0), axis=0, keepdims=True)
+        e = jnp.exp2((s - peak) * RAW)
+        e_hi = e.astype(BF16)
+        e_lo = (e - e_hi.astype(F32)).astype(BF16)
+        v_cols = jnp.concatenate([vn_ref[slot] for slot in slots], axis=1)
+        acc = dot(v_cols, e_hi) + dot(v_cols, e_lo)
         whole = acc[chans : chans + 1]
         att_ref[:, lane_block(i)] = pick_heads(acc[:chans] * (1.0 / whole), heads)
         t_ref[pl.ds(i, 1), :] = peak + jnp.log2(whole) * (1.0 / RAW)
         return carry
 
-    lax.fori_loop(0, blocks, body, 0)
+    lax.fori_loop(0, blocks, body, 0, unroll=8)
 
 
 def project_kernel(count, att_ref, w_ref, *refs):
@@ -187,20 +181,18 @@
         q_out = jnp.concatenate([q_wide, none], axis=0)
         g_out = jnp.concatenate([none, g_wide], axis=0)
         slots = [slot_of(lists_ref, counts_ref, i, j, first_block, ext) for j in range(MAX_KEYS)]
-        dq = jnp.zeros((chans, width), F32)
-        for j in range(0, MAX_KEYS, 2):
-            lows = []
-            for slot in slots[j : j + 2]:
-                probs = jnp.exp2(dot(ka_ref[slot], q_aug) * RAW)
-                dlow = (probs * dot(va_ref[slot], g_aug)).astype(BF16)
-                acc_ref[slot] += dot_nt(probs.astype(BF16), g_out) + dot_nt(dlow, q_out)
-                lows.append(dlow)
-            k_pair = jnp.concatenate([kn_ref[slots[j]], kn_ref[slots[j + 1]]], axis=1)
-            dq = dq + dot(k_pair, jnp.concatenate(lows, axis=0))
+        k_rows = jnp.concatenate([ka_ref[slot] for slot in slots], axis=0)
+        v_rows = jnp.concatenate([va_ref[slot] for slot in slots], axis=0)
+        probs = jnp.exp2(dot(k_rows, q_aug) * RAW)
+        dlow = (probs * dot(v_rows, g_aug)).astype(BF16)
+        both = dot_nt(probs.astype(BF16), g_out) + dot_nt(dlow, q_out)
+        for j in range(MAX_KEYS):
+            acc_ref[slots[j]] += both[j * BLOCK : (j + 1) * BLOCK]
+        dq = dot(jnp.concatenate([kn_ref[slot] for slot in slots], axis=1), dlow)
         dq_ref[:, lane_block(i)] = (pick_heads(dq, heads) * SCALE).astype(BF16)
         return carry
 
-    lax.fori_loop(0, blocks, body, 0)
+    lax.fori_loop(0, blocks, body, 0, unroll=8)
     lane = lax.broadcasted_iota(jnp.int32, (BLOCK, 2 * chans), 1)
     factor = jnp.where(lane < chans, SCALE, 1.0).astype(F32)
     for b in range(ext):

time: 59.1 us -> 48.7 us (0.82)
  Pallas kernels: 24.3 us -> 12.9 us
  waiting for transfers between devices: 9.26 us -> 12.1 us
  starting transfers between devices: 20.7 us -> 18.6 us
    pallas_call x4, Pallas kernels: 24.3 us -> 12.9 us  [kernel_call(): pl.pallas_call(body, out_shape=outs, in_specs=[scalars] * smem + [vmem] *...]
    ppermute x3, waiting for transfers between devices: 0.01 us -> 2.87 us  [shards(): lax.ppermute(grad_out, 'head', [((i + s) % head_count, i) for i in range(...]
    ppermute x3, starting transfers between devices: 6.76 us -> 4.91 us  [sum_over(): lax.ppermute(value, axis, [(i, i ^ step) for i in range(count)])]
  transfers between devices with their start and end apart: 10 -> 10, of which waited for: 3 -> 4; matrix products, arithmetic and copies ran while one was open for 1% -> 1% of each run, Pallas kernels for 15% -> 10%
where the time goes in v2:
time: 48.7 us; the launch traced here: 48.2 us
  starting transfers between devices  18.6 us (38%)
  Pallas kernels  12.9 us (26%)
  waiting for transfers between devices  12.1 us (25%)
  local copies, waits for them, and re-layouts  2.01 us (4%)
  other arithmetic  1.71 us (4%)
  between operations  0.8 us (2%)
    pallas_call x4, Pallas kernels, kernel_call(): pl.pallas_call(body, out_shape=outs, in_specs=[scalars] * smem + [vmem] *...  12.9 us
    ppermute x3, waiting for transfers between devices, sum_over(): lax.ppermute(value, axis, [(i, i ^ step) for i in range(count)])  9.24 us
    ppermute x4, starting transfers between devices, moved(): lax.ppermute(value, axis, [(i, i + steps) for i in range(count) if 0 <= i...  7.6 us
    ppermute x3, starting transfers between devices, shards(): lax.ppermute(grad_out, 'head', [((i + s) % head_count, i) for i in range(...  6.13 us
    ppermute x3, starting transfers between devices, sum_over(): lax.ppermute(value, axis, [(i, i ^ step) for i in range(count)])  4.91 us
    ppermute x3, waiting for transfers between devices, shards(): lax.ppermute(grad_out, 'head', [((i + s) % head_count, i) for i in range(...  2.87 us
    unnamed x16, local copies, waits for them, and re-layouts  2.01 us
    another operation x1, other arithmetic, shards(): low = moved(jnp.stack([keys[:, -rim:], values[:, -rim:]]), 'band', 1)  1.05 us
  transfers between devices with their start and end apart: 10, of which 4 were waited for; matrix products, arithmetic and copies ran while one was open for 1% of the time, Pallas kernels for 10%

profile of v2, /device:TPU:0, one launch (start us, length us, event | category | flops | bytes accessed | tf_op | source)
XLA Modules:
  0.0 48.2 jit_solution(8111193464351377289)
XLA Ops:
  0.7 1.1 %pad_maximum_fusion = bf16[2,64,1024]{2,1,0:T(8,128)(2,1)S(1)} fusion(bf16[1,64,1024]{2,1,0:T(8,128)(2,1)} %bitcast.3, bf16[1,64,1024]{2,1,0:T(8,128)(2,1)} %bitcast.2), kind=kLoop, calls=%fused_computation | loop fusion | flops 131072 | bytes 524288 | tf_op jit(solution)/shard_map/stack | solution.py:269
  1.7 0.0 copy-start.3
  1.7 1.3 %collective-permute-start.1 = (bf16[2,64,1024]{2,1,0:T(8,128)(2,1)S(1)}, bf16[2,64,1024]{2,1,0:T(8,128)(2,1)S(1)}, u32[]{:S(2)}, u32[]{:S(2)}) collective-permute-start(bf16[2,64,1024]{2,1,0:T(8,128)(2,1)S(1)} %pad_maximum_fusion), channel_id=1, source_target_pairs={{4,0},{8,4},{12,8},{16,12},{20,16},{24,20},{28,24},{5,1},{9,5},{13... | collective-permute-start | bytes 786440 | tf_op jit(solution)/shard_map/ppermute | solution.py:241
  3.0 3.0 %collective-permute-start = (bf16[2,64,1024]{2,1,0:T(8,128)(2,1)S(1)}, bf16[2,64,1024]{2,1,0:T(8,128)(2,1)S(1)}, u32[]{:S(2)}, u32[]{:S(2)}) collective-permute-start(bf16[2,64,1024]{2,1,0:T(8,128)(2,1)S(1)} %pad_maximum_fusion), channel_id=1, source_target_pairs={{0,4},{4,8},{8,12},{12,16},{16,20},{20,24},{24,28},{1,5},{5,9},{9,... | collective-permute-start | bytes 786440 | tf_op jit(solution)/shard_map/ppermute | solution.py:241
  6.1 4.1 %collective-permute-start.3 = (bf16[64,1024]{1,0:T(8,128)(2,1)S(1)}, bf16[64,1024]{1,0:T(8,128)(2,1)S(1)}, u32[]{:S(2)}, u32[]{:S(2)}) collective-permute-start(bf16[64,1024]{1,0:T(8,128)(2,1)S(1)} %copy-done), channel_id=1, source_target_pairs={{2,0},{3,1},{0,2},{1,3},{6,4},{7,5},{4,6},{5,7},{10,8},{11,9},{8,1... | collective-permute-start | bytes 393224 | tf_op jit(solution)/shard_map/ppermute | solution.py:272
  10.2 1.3 %collective-permute-start.2 = (bf16[64,1024]{1,0:T(8,128)(2,1)S(1)}, bf16[64,1024]{1,0:T(8,128)(2,1)S(1)}, u32[]{:S(2)}, u32[]{:S(2)}) collective-permute-start(bf16[64,1024]{1,0:T(8,128)(2,1)S(1)} %copy-done), channel_id=1, source_target_pairs={{1,0},{2,1},{3,2},{0,3},{5,4},{6,5},{7,6},{4,7},{9,8},{10,9},{11,1... | collective-permute-start | bytes 393224 | tf_op jit(solution)/shard_map/ppermute | solution.py:272
  11.6 0.7 %collective-permute-start.4 = (bf16[64,1024]{1,0:T(8,128)(2,1)S(1)}, bf16[64,1024]{1,0:T(8,128)(2,1)S(1)}, u32[]{:S(2)}, u32[]{:S(2)}) collective-permute-start(bf16[64,1024]{1,0:T(8,128)(2,1)S(1)} %copy-done), channel_id=1, source_target_pairs={{3,0},{0,1},{1,2},{2,3},{7,4},{4,5},{5,6},{6,7},{11,8},{8,9},{9,10... | collective-permute-start | bytes 393224 | tf_op jit(solution)/shard_map/ppermute | solution.py:272
  12.3 0.7 %copy-done.5 = s32[8,8]{1,0:T(8,128)S(1)} copy-done((s32[8,8]{1,0:T(8,128)S(1)}, s32[8,8]{1,0:T(8,128)}, u32[]{:S(2)}) %copy-start.5) | copy-done | bytes 280
  13.0 0.7 %copy-done.6 = s32[8]{0:T(128)S(1)} copy-done((s32[8]{0:T(128)S(1)}, s32[8]{0:T(128)}, u32[]{:S(2)}) %copy-start.6) | copy-done | bytes 56
  13.6 5.0 %shard_map.102 = (bf16[25,128,128]{2,1,0:T(8,128)(2,1)S(1)}, bf16[25,128,128]{2,1,0:T(8,128)(2,1)S(1)}, bf16[25,64,128]{2,1,0:T(8,128)(2,1)S(1)}, f32[64,1024]{1,0:T(8,128)S(1)}, f32[8,256]{1,0:T(8,128)S(1)}) custom-call(s32[8,8]{1,0:T(8,128)S(1)} %copy-done.5, s32[8]{0:T(128)S(1)} %copy-done.6, bf16[64,1024]{1,0:T(8,128)(2,1)S(1)} %copy-done.4, ...), custom_call_target="tpu_custom_call" | custom-call | flops 1610612736 | bytes 3236128 | tf_op jit(solution)/shard_map/pallas_call | solution.py:226
  18.7 2.9 %collective-permute-done.4.refs_3_ = bf16[64,1024]{1,0:T(8,128)(2,1)S(1)} collective-permute-done((bf16[64,1024]{1,0:T(8,128)(2,1)S(1)}, bf16[64,1024]{1,0:T(8,128)(2,1)S(1)}, u32[]{:S(2)}, u32[]{:S(2)}) %collective-permute-start.4) | collective-permute-done | bytes 131104 | tf_op jit(solution)/shard_map/ppermute | solution.py:272
  21.5 0.5 %shard_map.103 = (bf16[64,1024]{1,0:T(8,128)(2,1)S(1)}, f32[64,256]{1,0:T(8,128)S(1)}) custom-call(f32[64,1024]{1,0:T(8,128)S(1)} %get-tuple-element.17.att_ref, bf16[64,256]{1,0:T(8,128)(2,1)S(1)} %copy-done.3, bf16[64,1024]{1,0:T(8,128)(2,1)S(1)} %copy-done, bf16[64,1024]{1,0:T(8,128)(2,1)S(1)} %collective-permute-done.2.refs_1_, ...), custom_call_target="tpu_custom_call" | custom-call | flops 67108864 | bytes 1015808 | tf_op jit(solution)/shard_map/pallas_call | solution.py:226
  22.0 0.6 %copy-done.7 = s32[8]{0:T(128)S(1)} copy-done((s32[8]{0:T(128)S(1)}, s32[8]{0:T(128)}, u32[]{:S(2)}) %copy-start.7) | copy-done | bytes 56
  22.7 6.5 %shard_map.104 = (bf16[64,1024]{1,0:T(8,128)(2,1)}, f32[8,128,128]{2,1,0:T(8,128)S(1)}, bf16[8,128,128]{2,1,0:T(8,128)(2,1)S(1)}, bf16[8,128,128]{2,1,0:T(8,128)(2,1)S(1)}) custom-call(s32[8,8]{1,0:T(8,128)S(1)} %copy-done.5, s32[8]{0:T(128)S(1)} %copy-done.7, bf16[64,1024]{1,0:T(8,128)(2,1)S(1)} %copy-done.4, bf16[64,1024]{1,0:T(8,128)(2,1)S(1)} %get-tuple-element.18.g_ref, ...), custom_call_target="tpu_custom_call" | custom-call | flops 2684354560 | bytes 3760416 | tf_op jit(solution)/shard_map/pallas_call | solution.py:226
  29.2 2.0 %collective-permute-start.5 = (bf16[8,128,128]{2,1,0:T(8,128)(2,1)S(1)}, bf16[8,128,128]{2,1,0:T(8,128)(2,1)S(1)}, u32[]{:S(2)}, u32[]{:S(2)}) collective-permute-start(bf16[8,128,128]{2,1,0:T(8,128)(2,1)S(1)} %get-tuple-element.25), channel_id=1, source_target_pairs={{0,4},{4,8},{8,12},{12,16},{16,20},{20,24},{24,28},{1,5},{5,9},{9,... | collective-permute-start | bytes 786440 | tf_op jit(solution)/shard_map/ppermute | solution.py:241
  31.2 1.3 %collective-permute-start.6 = (bf16[8,128,128]{2,1,0:T(8,128)(2,1)S(1)}, bf16[8,128,128]{2,1,0:T(8,128)(2,1)S(1)}, u32[]{:S(2)}, u32[]{:S(2)}) collective-permute-start(bf16[8,128,128]{2,1,0:T(8,128)(2,1)S(1)} %get-tuple-element.26), channel_id=1, source_target_pairs={{4,0},{8,4},{12,8},{16,12},{20,16},{24,20},{28,24},{5,1},{9,5},{13... | collective-permute-start | bytes 786440 | tf_op jit(solution)/shard_map/ppermute | solution.py:241
  32.5 1.4 %collective-permute-start.7 = (f32[64,256]{1,0:T(8,128)S(1)}, f32[64,256]{1,0:T(8,128)S(1)}, u32[]{:S(2)}, u32[]{:S(2)}) collective-permute-start(f32[64,256]{1,0:T(8,128)S(1)} %get-tuple-element.29), channel_id=1, source_target_pairs={{0,4},{4,0},{8,12},{12,8},{16,20},{20,16},{24,28},{28,24},{1,5},{5... | collective-permute-start | bytes 196616 | tf_op jit(solution)/shard_map/ppermute | solution.py:252
  33.9 1.0 %collective-permute-done.7 = f32[64,256]{1,0:T(8,128)S(1)} collective-permute-done((f32[64,256]{1,0:T(8,128)S(1)}, f32[64,256]{1,0:T(8,128)S(1)}, u32[]{:S(2)}, u32[]{:S(2)}) %collective-permute-start.7) | collective-permute-done | bytes 65568 | tf_op jit(solution)/shard_map/ppermute | solution.py:252
  34.9 2.7 %collective-permute-start.8 = (f32[64,256]{1,0:T(8,128)S(1)}, f32[64,256]{1,0:T(8,128)S(1)}, u32[]{:S(2)}, u32[]{:S(2)}) collective-permute-start(f32[64,256]{1,0:T(8,128)S(1)} %add.9), channel_id=1, source_target_pairs={{0,8},{4,12},{8,0},{12,4},{16,24},{20,28},{24,16},{28,20},{1,9},{5... | collective-permute-start | bytes 196616 | tf_op jit(solution)/shard_map/ppermute | solution.py:252
  37.6 4.7 %collective-permute-done.8 = f32[64,256]{1,0:T(8,128)S(1)} collective-permute-done((f32[64,256]{1,0:T(8,128)S(1)}, f32[64,256]{1,0:T(8,128)S(1)}, u32[]{:S(2)}, u32[]{:S(2)}) %collective-permute-start.8) | collective-permute-done | bytes 65568 | tf_op jit(solution)/shard_map/ppermute | solution.py:252
  42.4 0.9 %collective-permute-start.9 = (f32[64,256]{1,0:T(8,128)S(1)}, f32[64,256]{1,0:T(8,128)S(1)}, u32[]{:S(2)}, u32[]{:S(2)}) collective-permute-start(f32[64,256]{1,0:T(8,128)S(1)} %add.10), channel_id=1, source_target_pairs={{0,16},{4,20},{8,24},{12,28},{16,0},{20,4},{24,8},{28,12},{1,17},{... | collective-permute-start | bytes 196616 | tf_op jit(solution)/shard_map/ppermute | solution.py:252
  43.2 3.5 %collective-permute-done.9 = f32[64,256]{1,0:T(8,128)S(1)} collective-permute-done((f32[64,256]{1,0:T(8,128)S(1)}, f32[64,256]{1,0:T(8,128)S(1)}, u32[]{:S(2)}, u32[]{:S(2)}) %collective-permute-start.9) | collective-permute-done | bytes 65568 | tf_op jit(solution)/shard_map/ppermute | solution.py:252
  46.7 0.6 %add.11 = f32[64,256]{1,0:T(8,128)} add(f32[64,256]{1,0:T(8,128)S(1)} %add.10, f32[64,256]{1,0:T(8,128)S(1)} %collective-permute-done.9) | non-fusion elementwise | flops 16384 | bytes 196608 | tf_op jit(solution)/shard_map/add | solution.py:252
  47.3 0.8 %shard_map.105 = (bf16[64,1024]{1,0:T(8,128)(2,1)}, bf16[64,1024]{1,0:T(8,128)(2,1)}) custom-call(f32[8,128,128]{2,1,0:T(8,128)S(1)} %get-tuple-element.24.own_ref, bf16[8,128,128]{2,1,0:T(8,128)(2,1)S(1)} %collective-permute-done.5.below_ref, bf16[8,128,128]{2,1,0:T(8,128)(2,1)S(1)} %collective-permute-done.6.above_ref), custom_call_target="tpu_custom_call" | custom-call | bytes 1310720 | tf_op jit(solution)/shard_map/pallas_call | solution.py:226
  (20 shorter events, 0.1 us)
Async XLA Ops:
  0.6 5.5 %copy-start = (bf16[64,1024]{1,0:T(8,128)(2,1)S(1)}, bf16[64,1024]{1,0:T(8,128)(2,1)}, u32[]{:S(2)}) copy-start(bf16[64,1024]{1,0:T(8,128)(2,1)} %refs_0_.1) | copy-start | bytes 393220
  0.6 11.6 %copy-start.1 = (bf16[64,1024]{1,0:T(8,128)(2,1)S(1)}, bf16[64,1024]{1,0:T(8,128)(2,1)}, u32[]{:S(2)}) copy-start(bf16[64,1024]{1,0:T(8,128)(2,1)} %k_ref.1) | copy-start | bytes 393220
  0.7 11.6 %copy-start.2 = (bf16[64,1024]{1,0:T(8,128)(2,1)S(1)}, bf16[64,1024]{1,0:T(8,128)(2,1)}, u32[]{:S(2)}) copy-start(bf16[64,1024]{1,0:T(8,128)(2,1)} %v_ref.1) | copy-start | bytes 393220
  0.7 11.6 %copy-start.4 = (bf16[64,1024]{1,0:T(8,128)(2,1)S(1)}, bf16[64,1024]{1,0:T(8,128)(2,1)}, u32[]{:S(2)}) copy-start(bf16[64,1024]{1,0:T(8,128)(2,1)} %q_ref.3) | copy-start | bytes 393220
  1.7 19.8 %copy-start.3 = (bf16[64,256]{1,0:T(8,128)(2,1)S(1)}, bf16[64,256]{1,0:T(8,128)(2,1)}, u32[]{:S(2)}) copy-start(bf16[64,256]{1,0:T(8,128)(2,1)} %w_ref.1) | copy-start | bytes 98308
  1.7 10.5 %collective-permute-start.1 = (bf16[2,64,1024]{2,1,0:T(8,128)(2,1)S(1)}, bf16[2,64,1024]{2,1,0:T(8,128)(2,1)S(1)}, u32[]{:S(2)}, u32[]{:S(2)}) collective-permute-start(bf16[2,64,1024]{2,1,0:T(8,128)(2,1)S(1)} %pad_maximum_fusion), channel_id=1, source_target_pairs={{4,0},{8,4},{12,8},{16,12},{20,16},{24,20},{28,24},{5,1},{9,5},{13... | collective-permute-start | bytes 786440 | tf_op jit(solution)/shard_map/ppermute | solution.py:241
  3.0 9.2 %collective-permute-start = (bf16[2,64,1024]{2,1,0:T(8,128)(2,1)S(1)}, bf16[2,64,1024]{2,1,0:T(8,128)(2,1)S(1)}, u32[]{:S(2)}, u32[]{:S(2)}) collective-permute-start(bf16[2,64,1024]{2,1,0:T(8,128)(2,1)S(1)} %pad_maximum_fusion), channel_id=1, source_target_pairs={{0,4},{4,8},{8,12},{12,16},{16,20},{20,24},{24,28},{1,5},{5,9},{9,... | collective-permute-start | bytes 786440 | tf_op jit(solution)/shard_map/ppermute | solution.py:241
  6.1 12.5 %collective-permute-start.3 = (bf16[64,1024]{1,0:T(8,128)(2,1)S(1)}, bf16[64,1024]{1,0:T(8,128)(2,1)S(1)}, u32[]{:S(2)}, u32[]{:S(2)}) collective-permute-start(bf16[64,1024]{1,0:T(8,128)(2,1)S(1)} %copy-done), channel_id=1, source_target_pairs={{2,0},{3,1},{0,2},{1,3},{6,4},{7,5},{4,6},{5,7},{10,8},{11,9},{8,1... | collective-permute-start | bytes 393224 | tf_op jit(solution)/shard_map/ppermute | solution.py:272
  10.2 8.4 %collective-permute-start.2 = (bf16[64,1024]{1,0:T(8,128)(2,1)S(1)}, bf16[64,1024]{1,0:T(8,128)(2,1)S(1)}, u32[]{:S(2)}, u32[]{:S(2)}) collective-permute-start(bf16[64,1024]{1,0:T(8,128)(2,1)S(1)} %copy-done), channel_id=1, source_target_pairs={{1,0},{2,1},{3,2},{0,3},{5,4},{6,5},{7,6},{4,7},{9,8},{10,9},{11,1... | collective-permute-start | bytes 393224 | tf_op jit(solution)/shard_map/ppermute | solution.py:272
  11.6 10.0 %collective-permute-start.4 = (bf16[64,1024]{1,0:T(8,128)(2,1)S(1)}, bf16[64,1024]{1,0:T(8,128)(2,1)S(1)}, u32[]{:S(2)}, u32[]{:S(2)}) collective-permute-start(bf16[64,1024]{1,0:T(8,128)(2,1)S(1)} %copy-done), channel_id=1, source_target_pairs={{3,0},{0,1},{1,2},{2,3},{7,4},{4,5},{5,6},{6,7},{11,8},{8,9},{9,10... | collective-permute-start | bytes 393224 | tf_op jit(solution)/shard_map/ppermute | solution.py:272
  12.3 0.7 %copy-start.5 = (s32[8,8]{1,0:T(8,128)S(1)}, s32[8,8]{1,0:T(8,128)}, u32[]{:S(2)}) copy-start(s32[8,8]{1,0:T(8,128)} %lists_ref.3) | copy-start | bytes 772
  13.0 0.7 %copy-start.6 = (s32[8]{0:T(128)S(1)}, s32[8]{0:T(128)}, u32[]{:S(2)}) copy-start(s32[8]{0:T(128)} %counts_ref.3) | copy-start | bytes 100
  22.0 0.7 %copy-start.7 = (s32[8]{0:T(128)S(1)}, s32[8]{0:T(128)}, u32[]{:S(2)}) copy-start(s32[8]{0:T(128)} %counts_ref.3) | copy-start | bytes 100
  29.2 18.1 %collective-permute-start.5 = (bf16[8,128,128]{2,1,0:T(8,128)(2,1)S(1)}, bf16[8,128,128]{2,1,0:T(8,128)(2,1)S(1)}, u32[]{:S(2)}, u32[]{:S(2)}) collective-permute-start(bf16[8,128,128]{2,1,0:T(8,128)(2,1)S(1)} %get-tuple-element.25), channel_id=1, source_target_pairs={{0,4},{4,8},{8,12},{12,16},{16,20},{20,24},{24,28},{1,5},{5,9},{9,... | collective-permute-start | bytes 786440 | tf_op jit(solution)/shard_map/ppermute | solution.py:241
  31.2 16.1 %collective-permute-start.6 = (bf16[8,128,128]{2,1,0:T(8,128)(2,1)S(1)}, bf16[8,128,128]{2,1,0:T(8,128)(2,1)S(1)}, u32[]{:S(2)}, u32[]{:S(2)}) collective-permute-start(bf16[8,128,128]{2,1,0:T(8,128)(2,1)S(1)} %get-tuple-element.26), channel_id=1, source_target_pairs={{4,0},{8,4},{12,8},{16,12},{20,16},{24,20},{28,24},{5,1},{9,5},{13... | collective-permute-start | bytes 786440 | tf_op jit(solution)/shard_map/ppermute | solution.py:241
  32.5 2.4 %collective-permute-start.7 = (f32[64,256]{1,0:T(8,128)S(1)}, f32[64,256]{1,0:T(8,128)S(1)}, u32[]{:S(2)}, u32[]{:S(2)}) collective-permute-start(f32[64,256]{1,0:T(8,128)S(1)} %get-tuple-element.29), channel_id=1, source_target_pairs={{0,4},{4,0},{8,12},{12,8},{16,20},{20,16},{24,28},{28,24},{1,5},{5... | collective-permute-start | bytes 196616 | tf_op jit(solution)/shard_map/ppermute | solution.py:252
  34.9 7.4 %collective-permute-start.8 = (f32[64,256]{1,0:T(8,128)S(1)}, f32[64,256]{1,0:T(8,128)S(1)}, u32[]{:S(2)}, u32[]{:S(2)}) collective-permute-start(f32[64,256]{1,0:T(8,128)S(1)} %add.9), channel_id=1, source_target_pairs={{0,8},{4,12},{8,0},{12,4},{16,24},{20,28},{24,16},{28,20},{1,9},{5... | collective-permute-start | bytes 196616 | tf_op jit(solution)/shard_map/ppermute | solution.py:252
  42.4 4.3 %collective-permute-start.9 = (f32[64,256]{1,0:T(8,128)S(1)}, f32[64,256]{1,0:T(8,128)S(1)}, u32[]{:S(2)}, u32[]{:S(2)}) collective-permute-start(f32[64,256]{1,0:T(8,128)S(1)} %add.10), channel_id=1, source_target_pairs={{0,16},{4,20},{8,24},{12,28},{16,0},{20,4},{24,8},{28,12},{1,17},{... | collective-permute-start | bytes 196616 | tf_op jit(solution)/shard_map/ppermute | solution.py:252

commit v3 on v2

v3 whole, which is shorter than its diff:
```python
import functools

import jax
import jax.numpy as jnp
from jax import lax
from jax.experimental import pallas as pl
from jax.experimental.pallas import tpu as pltpu
from jax.sharding import PartitionSpec as P

HEAD_DIM = 32
BLOCK = 128
REACH = 4
MAX_KEYS = 8
RIM = 2 * REACH
SCALE = HEAD_DIM ** (-0.5)
LOG2E = 1.4426950408889634
RAW = SCALE * LOG2E
MASKED = -1e30
AUG = 16
F32 = jnp.float32
BF16 = jnp.bfloat16
VMEM_LIMIT = 48 * 1024 * 1024


def dot(a, b):
    return lax.dot_general(a, b, (((1,), (0,)), ((), ())), preferred_element_type=F32)


def dot_nt(a, b):
    return lax.dot_general(a, b, (((1,), (1,)), ((), ())), preferred_element_type=F32)


def split3(x):
    hi = x.astype(BF16).astype(F32)
    rest = x - hi
    mid = rest.astype(BF16).astype(F32)
    return hi, mid, (rest - mid).astype(BF16).astype(F32)


def aug_rows(rows, width):
    at = lax.broadcasted_iota(jnp.int32, (AUG, width), 0)
    out = jnp.zeros((AUG, width), F32)
    for i, row in rows.items():
        out = jnp.where(at == i, row, out)
    return out.astype(BF16)


ROW_BIAS, ROW_LSE, ROW_SPREAD, ROW_UP, ROW_DOWN = 0, 3, 8, 12, 13


def three(first, rows):
    return {first + i: row for i, row in enumerate(rows)}


ONES = (1.0, 1.0, 1.0)


def spread_heads(x, heads):
    zero = jnp.zeros((HEAD_DIM, BLOCK), x.dtype)
    rows = []
    for h in range(heads):
        part = x[h * HEAD_DIM : (h + 1) * HEAD_DIM]
        rows.append(jnp.concatenate([part if g == h else zero for g in range(heads)], axis=1))
    return jnp.concatenate(rows, axis=0)


def pick_heads(x, heads):
    return jnp.concatenate(
        [
            x[h * HEAD_DIM : (h + 1) * HEAD_DIM, h * BLOCK : (h + 1) * BLOCK]
            for h in range(heads)
        ],
        axis=0,
    )


def lane_block(i):
    return slice(i * BLOCK, (i + 1) * BLOCK)


def start_copies(srcs, dsts, sems):
    copies = [pltpu.make_async_copy(s, d, sems.at[i]) for i, (s, d) in enumerate(zip(srcs, dsts))]
    for copy in copies:
        copy.start()
    return copies


def rim_bases(blocks):
    odd = lax.rem(lax.axis_index("band"), 2) == 1
    low, high = 0, RIM + blocks
    return jnp.where(odd, low, high), jnp.where(odd, high, low)


def rim_bases(blocks):
    odd = lax.rem(lax.axis_index("band"), 2) == 1
    low, high = 0, RIM + blocks
    return jnp.where(odd, low, high), jnp.where(odd, high, low)


def in_order(steps, begin, finish, ahead):
    begun = []
    for n, step in enumerate(steps):
        while len(begun) <= ahead and n + len(begun) < len(steps):
            begun.append(begin(steps[n + len(begun)]))
        finish(step, *begun.pop(0))


def place(refs, b, k_blk, v_blk, bias):
    ka_ref, va_ref, kn_ref, vn_ref = refs
    pad = jnp.zeros((BLOCK - k_blk.shape[0] - AUG, BLOCK), BF16)
    k_aug = aug_rows(three(ROW_BIAS, bias) | three(ROW_LSE, ONES), BLOCK)
    v_with = jnp.concatenate([v_blk, aug_rows(three(ROW_SPREAD, ONES), BLOCK)], axis=0)
    kn_ref[b] = k_blk
    vn_ref[b] = v_with
    ka_ref[b] = jnp.concatenate([k_blk, k_aug, pad], axis=0).T
    va_ref[b] = jnp.concatenate([v_with, pad], axis=0).T


def add_kernel(a_ref, b_ref, out_ref):
    out_ref[...] = a_ref[...] + b_ref[...]


def packed(chosen, values):
    shape = values.shape
    lane = lax.broadcasted_iota(jnp.int32, shape, 1)
    before = (
        lax.broadcasted_iota(jnp.int32, (BLOCK, BLOCK), 0)
        < lax.broadcasted_iota(jnp.int32, (BLOCK, BLOCK), 1)
    )
    rank = dot(chosen.astype(F32), before.astype(F32))
    out = jnp.zeros(shape, F32)
    for r in range(MAX_KEYS):
        hit = jnp.logical_and(chosen, rank == r)
        value = jnp.sum(jnp.where(hit, values.astype(F32) + 1.0, 0.0), axis=1, keepdims=True)
        out = jnp.where(lane == r, value, out)
    return out


def prepare_kernel(
    total, own_ref, lists_ref, counts_ref,
    slots_ref, carry_ref, bias_ref, ka_ref, va_ref, kn_ref, vn_ref,
    wide_ref, counts_smem, sems,
):
    copies = start_copies((counts_ref,), (counts_smem,), sems)
    chans = own_ref.shape[1]
    blocks = own_ref.shape[2] // BLOCK
    ext = blocks + 2 * RIM
    first_block = lax.axis_index("band") * blocks - RIM
    at = lax.broadcasted_iota(jnp.int32, (ext, BLOCK), 0) * BLOCK
    at = at + lax.broadcasted_iota(jnp.int32, (ext, BLOCK), 1) + first_block * BLOCK
    at = jnp.clip(at, 0, total - 1).astype(F32)
    logw = jnp.log(jnp.sin(jnp.pi * (at + 0.5) / total))
    bias = split3(logw * (1.0 / SCALE))
    for i, part in enumerate(bias):
        bias_ref[i] = part
    refs = (ka_ref, va_ref, kn_ref, vn_ref)
    none = jnp.zeros((chans, BLOCK), BF16)
    place(refs, ext, none, none, [MASKED, 0.0, 0.0])
    for b in range(blocks):
        rows = [part[RIM + b : RIM + b + 1] for part in bias]
        place(refs, RIM + b, own_ref[0, :, lane_block(b)], own_ref[1, :, lane_block(b)], rows)
    for copy in copies:
        copy.wait()
    wide_ref[...] = jnp.zeros_like(wide_ref)
    wide_ref[:, :MAX_KEYS] = lists_ref[...]
    lane = lax.broadcasted_iota(jnp.int32, (blocks, BLOCK), 1)
    row = lax.broadcasted_iota(jnp.int32, (blocks, BLOCK), 0)
    used = jnp.zeros((blocks, BLOCK), jnp.int32)
    for i in range(blocks):
        used = jnp.where(row == i, counts_smem[i], used)
    slots = jnp.where(lane < used, wide_ref[...] - first_block, ext)
    slots_ref[...] = slots
    upper = RIM + blocks
    carry_ref[0] = packed(jnp.logical_and(slots >= upper, slots < ext), slots - upper)
    carry_ref[1] = packed(slots < RIM, slots)


def attend_kernel(
    slots_vmem, own_ref, bias_ref, pair_ref, other_ref, ka_in, va_in, kn_in, vn_in,
    ka_ref, va_ref, kn_ref, vn_ref, att_ref, t_ref, slots_ref, sems,
):
    copies = start_copies((slots_vmem,), (slots_ref,), sems)
    chans = own_ref.shape[1]
    heads = chans // HEAD_DIM
    blocks = own_ref.shape[2] // BLOCK
    width = heads * BLOCK
    refs = (ka_ref, va_ref, kn_ref, vn_ref)
    for base, ref in zip(rim_bases(blocks), (pair_ref, other_ref)):
        for b in range(RIM):
            rows = [bias_ref[i, pl.ds(base + b, 1), :] for i in range(3)]
            place(refs, base + b, ref[0, :, lane_block(b)], ref[1, :, lane_block(b)], rows)
    for copy in copies:
        copy.wait()

    ones = aug_rows(three(ROW_BIAS, ONES), width)
    pad_w = jnp.zeros((BLOCK - chans - AUG, width), BF16)

    def scores(i):
        q_aug = jnp.concatenate([spread_heads(own_ref[2, :, lane_block(i)], heads), ones, pad_w], axis=0)
        slots = [slots_ref[i, j] for j in range(MAX_KEYS)]
        k_rows = jnp.concatenate([ka_ref[slot] for slot in slots], axis=0)
        s = dot(k_rows, q_aug)
        peak = jnp.max(jnp.max(s.reshape(-1, 8, width), axis=0), axis=0, keepdims=True)
        return slots, s, peak

    def finish(i, slots, s, peak):
        e = jnp.exp2((s - peak) * RAW)
        v_cols = jnp.concatenate([vn_ref[slot] for slot in slots], axis=1)
        acc = dot(v_cols, e.astype(BF16))
        whole = acc[chans + ROW_SPREAD : chans + ROW_SPREAD + 1]
        att_ref[:, lane_block(i)] = pick_heads(acc[:chans] * (1.0 / whole), heads)
        t_ref[i : i + 1] = peak + jnp.log2(whole) * (1.0 / RAW)

    in_order(range(blocks), scores, finish, 2)


def reorder(x, count):
    depth = x.shape[1] // count
    here = lax.axis_index("head")
    bit = 1
    while bit < count:
        parts = [x[:, (m ^ bit) * depth : ((m ^ bit) + 1) * depth] for m in range(count)]
        x = jnp.where((here & bit) != 0, jnp.concatenate(parts, axis=1), x)
        bit *= 2
    return x


def project_kernel(count, att_ref, t_ref, carry_ref, w_ref, *refs):
    parts, (z_ref, gw_ref) = refs[:count], refs[count:]
    chans, tokens = att_ref.shape
    full = jnp.concatenate([p[...] for p in parts], axis=0)
    turned = reorder(w_ref[...].astype(F32), count).astype(BF16)
    grad = dot(turned, full).astype(BF16)
    z_ref[:chans] = grad
    prod = grad.astype(F32) * att_ref[...]
    for h in range(chans // HEAD_DIM):
        spread = jnp.sum(prod[h * HEAD_DIM : (h + 1) * HEAD_DIM], axis=0, keepdims=True)
        first = chans + h * AUG
        for i in range(tokens // BLOCK):
            t = t_ref[i : i + 1, h * BLOCK : (h + 1) * BLOCK]
            rows = three(ROW_BIAS, ONES) | three(ROW_LSE, split3(-t))
            rows |= three(ROW_SPREAD, split3(-spread[:, lane_block(i)]))
            rows |= {ROW_UP: carry_ref[0, i : i + 1, :], ROW_DOWN: carry_ref[1, i : i + 1, :]}
            z_ref[first : first + AUG, lane_block(i)] = aug_rows(rows, BLOCK)
    gw_ref[...] = reorder(dot_nt(att_ref[...].astype(BF16), full), count)


def query_side(q_ref, z_ref, here):
    chans = q_ref.shape[0]
    heads = chans // HEAD_DIM
    width = heads * BLOCK
    q_wide = spread_heads(q_ref[:, here], heads)
    g_wide = spread_heads(z_ref[:chans, here], heads)
    tiles = [z_ref[chans + h * AUG : chans + (h + 1) * AUG, here] for h in range(heads)]
    aug = jnp.concatenate(tiles, axis=1)
    pad = jnp.zeros((BLOCK - chans - AUG, width), BF16)
    none = jnp.zeros((chans, width), BF16)
    q_aug = jnp.concatenate([q_wide, aug, pad], axis=0)
    g_aug = jnp.concatenate([g_wide, aug, pad], axis=0)
    q_out = jnp.concatenate([q_wide, none], axis=0)
    g_out = jnp.concatenate([none, g_wide], axis=0)
    return q_aug, g_aug, q_out, g_out


def products(side, slots, ka_ref, va_ref):
    q_aug, g_aug = side[:2]
    k_rows = jnp.concatenate([ka_ref[slot] for slot in slots], axis=0)
    v_rows = jnp.concatenate([va_ref[slot] for slot in slots], axis=0)
    return dot(k_rows, q_aug), dot(v_rows, g_aug)


def pair_grads(side, slots, scores, dprobs, acc_ref):
    q_out, g_out = side[2:]
    probs = jnp.exp2(scores * RAW)
    dlow = (probs * dprobs).astype(BF16)
    both = dot_nt(probs.astype(BF16), g_out) + dot_nt(dlow, q_out)
    for j, slot in enumerate(slots):
        acc_ref[slot] += both[j * BLOCK : (j + 1) * BLOCK]
    return dlow


def grads_kernel(start, stop, slots_vmem, own_ref, z_ref, ka_ref, va_ref, kn_ref, *refs):
    dq_ref, acc_ref, slots_ref, sems = refs[-4:]
    copies = start_copies((slots_vmem,), (slots_ref,), sems)
    chans = dq_ref.shape[0]
    heads = chans // HEAD_DIM
    if start == 0:
        acc_ref[...] = jnp.zeros_like(acc_ref)
    for copy in copies:
        copy.wait()
    def begin(i):
        slots = [slots_ref[i, j] for j in range(MAX_KEYS)]
        side = query_side(own_ref.at[2], z_ref, lane_block(i))
        return side, slots, *products(side, slots, ka_ref, va_ref)

    def finish(i, side, slots, scores, dprobs):
        dlow = pair_grads(side, slots, scores, dprobs, acc_ref)
        dq = dot(jnp.concatenate([kn_ref[slot] for slot in slots], axis=1), dlow)
        dq_ref[:, lane_block(i - start)] = (pick_heads(dq, heads) * SCALE).astype(BF16)

    in_order(range(start, stop), begin, finish, 1)


def neighbours_kernel(
    dq_low, dq_high, past_ref, pair_own, other_own, pair_ref, other_ref, ka_ref, va_ref,
    dq_ref, dk_ref, dv_ref, acc_ref, q_all, z_all, lists_vmem, todo_ref, lists_ref, sems,
):
    chans = dk_ref.shape[0]
    blocks = dk_ref.shape[1] // BLOCK
    ext = blocks + 2 * RIM
    odd = lax.rem(lax.axis_index("band"), 2) == 1
    for s, (ref, below) in enumerate(((pair_ref, odd), (other_ref, jnp.logical_not(odd)))):
        rows = ref[chans : chans + AUG].astype(F32)
        row = jnp.where(below, rows[ROW_UP : ROW_UP + 1], rows[ROW_DOWN : ROW_DOWN + 1])
        for i in range(blocks):
            at = s * blocks + i
            lists_vmem[at : at + 1] = row[:, lane_block(i)].astype(jnp.int32)
    lists_vmem[2 * blocks :] = jnp.zeros_like(lists_vmem[2 * blocks :])
    copies = start_copies((lists_vmem,), (lists_ref,), sems)
    q_all[0] = pair_own[2]
    q_all[1] = other_own[2]
    z_all[0] = pair_ref[...]
    z_all[1] = other_ref[...]
    half = dq_low.shape[1]
    dq_ref[:, :half] = dq_low[...]
    dq_ref[:, half:] = dq_high[...]
    for b in range(blocks):
        acc_ref[RIM + b] = past_ref[RIM + b]
    acc_ref[ext] = past_ref[ext]
    for copy in copies:
        copy.wait()
    step, many = 2, 3
    count = 0
    for row in range(2 * blocks):
        for c in range(0, MAX_KEYS, step):
            todo_ref[count] = row * MAX_KEYS + c
            count = count + (lists_ref[row, c] > 0).astype(jnp.int32)
    for j in range(many):
        todo_ref[count + j] = 2 * blocks * MAX_KEYS

    def body(k, carry):
        begun = []
        for j in range(many):
            todo = todo_ref[k * many + j]
            row, c = todo // MAX_KEYS, todo % MAX_KEYS
            here = pl.ds(pl.multiple_of(row % blocks * BLOCK, BLOCK), BLOCK)
            at = jnp.minimum(row // blocks, 1)
            side = query_side(q_all.at[at], z_all.at[at], here)
            slots = []
            for n in range(step):
                place_of = lists_ref[row, c + n]
                slots.append(jnp.where(place_of > 0, RIM - 1 + place_of, ext))
            begun.append((side, slots, *products(side, slots, ka_ref, va_ref)))
        for one in begun:
            pair_grads(*one, acc_ref)
        return carry

    lax.fori_loop(0, (count + many - 1) // many, body, 0)
    factor = part_factor(2 * chans)
    for b in range(blocks):
        x = (acc_ref[RIM + b] * factor).T
        dk_ref[:, lane_block(b)] = x[:chans].astype(BF16)
        dv_ref[:, lane_block(b)] = x[chans:].astype(BF16)


def part_factor(lanes):
    lane = lax.broadcasted_iota(jnp.int32, (BLOCK, lanes), 1)
    return jnp.where(lane < lanes // 2, SCALE, 1.0).astype(F32)


def kernel_call(body, outs, operands, scalars=(), scratch=(), flops=0, transcendentals=0, aliases=None):
    size = sum(x.size * x.dtype.itemsize for x in operands + outs)
    vmem = pl.BlockSpec(memory_space=pltpu.VMEM)
    copies = [pltpu.SMEM(x.shape, x.dtype) for x in scalars]
    if copies:
        copies.append(pltpu.SemaphoreType.DMA((len(copies),)))
    return pl.pallas_call(
        body,
        out_shape=outs,
        in_specs=[vmem] * len(operands),
        out_specs=[vmem] * len(outs),
        scratch_shapes=list(scratch) + copies,
        input_output_aliases=aliases or {},
        compiler_params=pltpu.CompilerParams(vmem_limit_bytes=VMEM_LIMIT),
        cost_estimate=pl.CostEstimate(
            flops=flops, bytes_accessed=size, transcendentals=transcendentals
        ),
    )(*operands)


def to_pair(value, axis):
    last = lax.axis_size(axis) - 1
    return lax.ppermute(value, axis, [(i, i ^ 1) for i in range(last + 1) if i ^ 1 <= last])


def to_other(value, axis):
    last = lax.axis_size(axis) - 1
    swap = [(i, ((i + 1) ^ 1) - 1) for i in range(last + 1)]
    return lax.ppermute(value, axis, [(i, j) for i, j in swap if 0 <= j <= last])


def gathered(value, axis):
    count = lax.axis_size(axis)
    if count & (count - 1):
        raise ValueError("axis size")
    step, parts = count // 2, {0: value}
    while step:
        swap = [(i, i ^ step) for i in range(count)]
        parts.update({m ^ step: lax.ppermute(x, axis, swap) for m, x in list(parts.items())})
        step //= 2
    return [parts[m] for m in range(count)]


class sum_steps:
    def __init__(self, value, axis):
        self.axis, self.count, self.value = axis, lax.axis_size(axis), value
        if self.count & (self.count - 1):
            raise ValueError("axis size")
        sizes = [1 << i for i in range(self.count.bit_length() - 1)]
        self.steps = sizes[:1] + sizes[:0:-1]
        self.send()

    def send(self):
        step = self.steps.pop(0)
        swap = [(i, i ^ step) for i in range(self.count)]
        self.came = lax.ppermute(self.value, self.axis, swap)

    def add(self):
        shape = jax.ShapeDtypeStruct(self.value.shape, self.value.dtype)
        (self.value,) = kernel_call(add_kernel, [shape], [self.value, self.came])

    def go_on(self):
        self.add()
        self.send()


def shards(queries, keys, values, grad_out, w_out, key_lists, key_counts):
    chans, tokens = queries.shape
    blocks = tokens // BLOCK
    heads = chans // HEAD_DIM
    ext = blocks + 2 * RIM
    width = heads * BLOCK
    total = tokens * lax.axis_size("band")
    head_count = lax.axis_size("head")
    shape = jax.ShapeDtypeStruct
    pairs = blocks * MAX_KEYS * width * BLOCK

    if blocks != RIM:
        raise ValueError("band size")
    like = lambda x: shape(x.shape, x.dtype)
    own = jnp.stack([keys, values, queries])
    other_own = to_other(own, "band")
    pair_own = to_pair(own, "band")
    parts = gathered(grad_out, "head")
    slots, carry, bias, *state = kernel_call(
        functools.partial(prepare_kernel, total),
        [
            shape((blocks, BLOCK), jnp.int32),
            shape((2, blocks, BLOCK), F32),
            shape((3, ext, BLOCK), F32),
            shape((ext + 1, BLOCK, BLOCK), BF16),
            shape((ext + 1, BLOCK, BLOCK), BF16),
            shape((ext + 1, chans, BLOCK), BF16),
            shape((ext + 1, chans + AUG, BLOCK), BF16),
        ],
        [own, key_lists, key_counts],
        [key_counts],
        scratch=[pltpu.VMEM((blocks, BLOCK), jnp.int32)],
    )
    ka, va, kn, vn, att, t = kernel_call(
        attend_kernel,
        [like(x) for x in state] + [shape((chans, tokens), F32), shape((blocks, width), F32)],
        [slots, own, bias, pair_own, other_own] + state,
        [slots],
        flops=3 * 2 * pairs * BLOCK,
        transcendentals=pairs,
        aliases={5 + i: i for i in range(4)},
    )
    z, part_w = kernel_call(
        functools.partial(project_kernel, head_count),
        [shape((chans + heads * AUG, tokens), BF16), shape(w_out.shape, F32)],
        [att, t, carry, w_out] + parts,
        flops=4 * w_out.size * tokens,
    )
    other = to_other(z, "band")
    pair = to_pair(z, "band")
    sums = sum_steps(part_w, "band")
    acc = shape((ext + 1, BLOCK, 2 * chans), F32)
    common, state, dq_parts = [slots, own, z, ka, va, kn], [], []
    cuts = [0, blocks // 2, blocks]
    for start, stop in zip(cuts, cuts[1:]):
        dq, done = kernel_call(
            functools.partial(grads_kernel, start, stop),
            [shape((chans, (stop - start) * BLOCK), BF16), acc],
            common + state,
            [slots],
            flops=10 * pairs * BLOCK * (stop - start) // blocks,
            transcendentals=pairs * (stop - start) // blocks,
            aliases={len(common): 1} if state else None,
        )
        dq_parts.append(dq)
        done, sums.came = lax.optimization_barrier((done, sums.came))
        if sums.steps:
            sums.go_on()
            done, sums.value = lax.optimization_barrier((done, sums.value))
        state = [done]
    dq, dk, dv = kernel_call(
        neighbours_kernel,
        [shape((chans, tokens), BF16)] * 3,
        dq_parts + state + [pair_own, other_own, pair, other, ka, va],
        scratch=[
            pltpu.VMEM(acc.shape, F32),
            pltpu.VMEM((2,) + queries.shape, BF16),
            pltpu.VMEM((2,) + z.shape, BF16),
            pltpu.VMEM((2 * blocks + 8, BLOCK), jnp.int32),
            pltpu.SMEM((2 * blocks * MAX_KEYS + 8,), jnp.int32),
            pltpu.SMEM((2 * blocks + 8, BLOCK), jnp.int32),
            pltpu.SemaphoreType.DMA((1,)),
        ],
        flops=4 * pairs * BLOCK,
        transcendentals=pairs // 2,
    )
    dk, sums.came = lax.optimization_barrier((dk, sums.came))
    while sums.steps:
        sums.go_on()
    sums.add()
    return (dq, dk, dv, sums.value)


def solution(mesh):
    in_specs = (
        P("head", "band"),
        P("head", "band"),
        P("head", "band"),
        P("head", "band"),
        P("head", None),
        P("band", None),
        P("band"),
    )
    out_specs = (P("head", "band"), P("head", "band"), P("head", "band"), P("head", None))
    return jax.shard_map(shards, mesh=mesh, in_specs=in_specs, out_specs=out_specs, check_vma=False)
```

time: 48.7 us -> 38.9 us (0.80)
  waiting for transfers between devices: 12.1 us -> 0.84 us
  Pallas kernels: 12.9 us -> 14.7 us
  starting transfers between devices: 18.6 us -> 19.6 us
  local copies, waits for them, and re-layouts: 2.01 us -> 1.35 us
  other arithmetic: 1.71 us -> 1.08 us
    ppermute x10, waiting for transfers between devices: 12.1 us -> 0.84 us  [the longest x3 0.82 us: send(): self.came = lax.ppermute(self.value, self.axis, swap)]
    pallas_call x4 -> x9, Pallas kernels: 12.9 us -> 14.7 us  [kernel_call(): pl.pallas_call(body, out_shape=outs, in_specs=[vmem] * len(operands), out...]
    ppermute x10, starting transfers between devices: 18.6 us -> 19.6 us  [the longest x3 9.28 us: gathered(): lax.ppermute(x, axis, swap)]
    unnamed x16 -> x8, local copies, waits for them, and re-layouts: 2.01 us -> 1.35 us
    add x3 -> x0, other arithmetic: 0.66 us -> none  [sum_over(): value + lax.ppermute(value, axis, [(i, i ^ step) for i in range(count)])]
  transfers between devices with their start and end apart: 10 -> 10, of which waited for: 4 -> 1; matrix products, arithmetic and copies ran while one was open for 1% -> 0% of each run, Pallas kernels for 10% -> 35%
where the time goes in v3:
time: 38.9 us; the launch traced here: 38.4 us
  starting transfers between devices  19.6 us (50%)
  Pallas kernels  14.7 us (38%)
  local copies, waits for them, and re-layouts  1.35 us (3%)
  other arithmetic  1.08 us (3%)
  waiting for transfers between devices  0.84 us (2%)
  between operations  0.78 us (2%)
    pallas_call x9, Pallas kernels, kernel_call(): pl.pallas_call(body, out_shape=outs, in_specs=[vmem] * len(operands), out...  14.7 us
    ppermute x3, starting transfers between devices, gathered(): lax.ppermute(x, axis, swap)  9.28 us
    ppermute x3, starting transfers between devices, send(): self.came = lax.ppermute(self.value, self.axis, swap)  7.26 us
    ppermute x2, starting transfers between devices, to_pair(): lax.ppermute(value, axis, [(i, i ^ 1) for i in range(last + 1) if i ^ 1 <...  1.75 us
    unnamed x8, local copies, waits for them, and re-layouts  1.35 us
    ppermute x2, starting transfers between devices, to_other(): lax.ppermute(value, axis, [(i, j) for i, j in swap if 0 <= j <= last])  1.33 us
    another operation x1, other arithmetic, shards(): own = jnp.stack([keys, values, queries])  1.08 us
    ppermute x3, waiting for transfers between devices, send(): self.came = lax.ppermute(self.value, self.axis, swap)  0.82 us
  transfers between devices with their start and end apart: 10, of which 1 were waited for; matrix products, arithmetic and copies ran while one was open for 0% of the time, Pallas kernels for 35%

profile of v3, /device:TPU:0, one launch (start us, length us, event | category | flops | bytes accessed | tf_op | source)
XLA Modules:
  0.0 38.4 jit_solution(7388744533146302612)
XLA Ops:
  0.6 1.1 %pad_maximum_fusion.own_ref = bf16[3,64,1024]{2,1,0:T(8,128)(2,1)S(1)} fusion(bf16[1,64,1024]{2,1,0:T(8,128)(2,1)} %bitcast.3, bf16[1,64,1024]{2,1,0:T(8,128)(2,1)} %bitcast.4, bf16[1,64,1024]{2,1,0:T(8,128)(2,1)} %bitcast.5), kind=kLoop, calls=%fused_computation | loop fusion | flops 393216 | bytes 786432 | tf_op jit(solution)/shard_map/stack | solution.py:451
  1.7 0.5 %collective-permute-start = (bf16[3,64,1024]{2,1,0:T(8,128)(2,1)S(1)}, bf16[3,64,1024]{2,1,0:T(8,128)(2,1)S(1)}, u32[]{:S(2)}, u32[]{:S(2)}) collective-permute-start(bf16[3,64,1024]{2,1,0:T(8,128)(2,1)S(1)} %pad_maximum_fusion.own_ref), channel_id=1, source_target_pairs={{0,4},{4,0},{8,12},{12,8},{16,20},{20,16},{24,28},{28,24},{1,5},{5... | collective-permute-start | bytes 1179656 | tf_op jit(solution)/shard_map/ppermute | solution.py:393
  2.2 0.7 %collective-permute-start.1 = (bf16[3,64,1024]{2,1,0:T(8,128)(2,1)S(1)}, bf16[3,64,1024]{2,1,0:T(8,128)(2,1)S(1)}, u32[]{:S(2)}, u32[]{:S(2)}) collective-permute-start(bf16[3,64,1024]{2,1,0:T(8,128)(2,1)S(1)} %pad_maximum_fusion.own_ref), channel_id=1, source_target_pairs={{4,8},{8,4},{12,16},{16,12},{20,24},{24,20},{5,9},{9,5},{13,17},{1... | collective-permute-start | bytes 1179656 | tf_op jit(solution)/shard_map/ppermute | solution.py:399
  2.9 3.7 %collective-permute-start.3 = (bf16[64,1024]{1,0:T(8,128)(2,1)}, bf16[64,1024]{1,0:T(8,128)(2,1)S(1)}, u32[]{:S(2)}, u32[]{:S(2)}) collective-permute-start(bf16[64,1024]{1,0:T(8,128)(2,1)} %refs_0_.1), channel_id=1, source_target_pairs={{0,2},{1,3},{2,0},{3,1},{4,6},{5,7},{6,4},{7,5},{8,10},{9,11},{10,... | collective-permute-start | bytes 393224 | tf_op jit(solution)/shard_map/ppermute | solution.py:409
  6.6 1.6 %collective-permute-start.2 = (bf16[64,1024]{1,0:T(8,128)(2,1)}, bf16[64,1024]{1,0:T(8,128)(2,1)S(1)}, u32[]{:S(2)}, u32[]{:S(2)}) collective-permute-start(bf16[64,1024]{1,0:T(8,128)(2,1)} %refs_0_.1), channel_id=1, source_target_pairs={{0,1},{1,0},{2,3},{3,2},{4,5},{5,4},{6,7},{7,6},{8,9},{9,8},{10,11... | collective-permute-start | bytes 393224 | tf_op jit(solution)/shard_map/ppermute | solution.py:409
  8.2 0.7 %copy-done.2 = s32[8,8]{1,0:T(8,128)S(1)} copy-done((s32[8,8]{1,0:T(8,128)S(1)}, s32[8,8]{1,0:T(8,128)}, u32[]{:S(2)}) %copy-start.2) | copy-done | bytes 280
  8.9 0.7 %copy-done.3 = s32[8]{0:T(128)S(1)} copy-done((s32[8]{0:T(128)S(1)}, s32[8]{0:T(128)}, u32[]{:S(2)}) %copy-start.3) | copy-done | bytes 56
  9.5 0.8 %shard_map.102 = (s32[8,128]{1,0:T(8,128)S(1)}, f32[2,8,128]{2,1,0:T(8,128)S(1)}, f32[3,24,128]{2,1,0:T(8,128)S(1)}, bf16[25,128,128]{2,1,0:T(8,128)(2,1)S(1)}, ...) custom-call(bf16[3,64,1024]{2,1,0:T(8,128)(2,1)S(1)} %pad_maximum_fusion.own_re, ...), custom_call_target="tpu_custom_call" | custom-call | bytes 3002656 | tf_op jit(solution)/shard_map/pallas_call | solution.py:377
  10.3 4.0 %collective-permute-start.4 = (bf16[64,1024]{1,0:T(8,128)(2,1)S(1)}, bf16[64,1024]{1,0:T(8,128)(2,1)S(1)}, u32[]{:S(2)}, u32[]{:S(2)}) collective-permute-start(bf16[64,1024]{1,0:T(8,128)(2,1)S(1)} %collective-permute-done.3.refs_2_), channel_id=1, source_target_pairs={{0,1},{1,0},{2,3},{3,2},{4,5},{5,4},{6,7},{7,6},{8,9},{9,8},{10,11... | collective-permute-start | bytes 393224 | tf_op jit(solution)/shard_map/ppermute | solution.py:409
  14.4 0.0 copy-start.1
  14.4 3.9 %shard_map.103 = (bf16[25,128,128]{2,1,0:T(8,128)(2,1)S(1)}, bf16[25,128,128]{2,1,0:T(8,128)(2,1)S(1)}, bf16[25,64,128]{2,1,0:T(8,128)(2,1)S(1)}, bf16[25,80,128...) custom-call(s32[8,128]{1,0:T(8,128)S(1)} %get-tuple-element.35.slots, ...), custom_call_target="tpu_custom_call", output_to_operand_aliasing={{0}: (5, {}), {1}: (6, {}), {2}: (7, {}), {3}: (8, {})} | custom-call | flops 1610612736 | bytes 6610944 | tf_op jit(solution)/shard_map/pallas_call | solution.py:377
  18.3 0.0 collective-permute-done.4.refs_3_
  18.3 0.5 %shard_map.104 = (bf16[96,1024]{1,0:T(8,128)(2,1)S(1)}, f32[64,256]{1,0:T(8,128)S(1)}) custom-call(f32[64,1024]{1,0:T(8,128)S(1)} %get-tuple-element.41.att_ref, f32[8,256]{1,0:T(8,128)S(1)} %get-tuple-element.42.t_ref, f32[2,8,128]{2,1,0:T(8,128)S(1)} %get-tuple-element.43.carry_ref, bf16[64,256]{1,0:T(8,128)(2,1)S(1)} %copy-done.1, ...), custom_call_target="tpu_custom_call" | custom-call | flops 67108864 | bytes 1097728 | tf_op jit(solution)/shard_map/pallas_call | solution.py:377
  18.8 1.2 %collective-permute-start.7 = (bf16[96,1024]{1,0:T(8,128)(2,1)S(1)}, bf16[96,1024]{1,0:T(8,128)(2,1)S(1)}, u32[]{:S(2)}, u32[]{:S(2)}) collective-permute-start(bf16[96,1024]{1,0:T(8,128)(2,1)S(1)} %get-tuple-element.44.z_ref), channel_id=1, source_target_pairs={{0,4},{4,0},{8,12},{12,8},{16,20},{20,16},{24,28},{28,24},{1,5},{5... | collective-permute-start | bytes 589832 | tf_op jit(solution)/shard_map/ppermute | solution.py:393
  20.1 0.7 %collective-permute-start.8 = (bf16[96,1024]{1,0:T(8,128)(2,1)S(1)}, bf16[96,1024]{1,0:T(8,128)(2,1)S(1)}, u32[]{:S(2)}, u32[]{:S(2)}) collective-permute-start(bf16[96,1024]{1,0:T(8,128)(2,1)S(1)} %get-tuple-element.44.z_ref), channel_id=1, source_target_pairs={{4,8},{8,4},{12,16},{16,12},{20,24},{24,20},{5,9},{9,5},{13,17},{1... | collective-permute-start | bytes 589832 | tf_op jit(solution)/shard_map/ppermute | solution.py:399
  20.7 4.7 %collective-permute-start.5 = (f32[64,256]{1,0:T(8,128)S(1)}, f32[64,256]{1,0:T(8,128)S(1)}, u32[]{:S(2)}, u32[]{:S(2)}) collective-permute-start(f32[64,256]{1,0:T(8,128)S(1)} %get-tuple-element.50.a_ref), channel_id=1, source_target_pairs={{0,4},{4,0},{8,12},{12,8},{16,20},{20,16},{24,28},{28,24},{1,5},{5... | collective-permute-start | bytes 196616 | tf_op jit(solution)/shard_map/ppermute | solution.py:426
  25.4 3.3 %shard_map.105 = (bf16[64,512]{1,0:T(8,128)(2,1)S(1)}, f32[25,128,128]{2,1,0:T(8,128)S(1)}) custom-call(s32[8,128]{1,0:T(8,128)S(1)} %get-tuple-element.35.slots_vmem, bf16[3,64,1024]{2,1,0:T(8,128)(2,1)S(1)} %pad_maximum_fusion.own_ref, bf16[96,1024]{1,0:T(8,128)(2,1)S(1)} %get-tuple-element.44.z_ref, bf16[25,128,128]{2,1,0:T(8,128)(2,1)S(1)} %get-tuple-element.45.ka_ref, ...), custom_call_target="tpu_custom_call" | custom-call | flops 1342177280 | bytes 4345856 | tf_op jit(solution)/shard_map/pallas_call | solution.py:377
  28.7 0.0 collective-permute-done.5.b_ref
  28.7 1.4 %collective-permute-start.6 = (f32[64,256]{1,0:T(8,128)S(1)}, f32[64,256]{1,0:T(8,128)S(1)}, u32[]{:S(2)}, u32[]{:S(2)}) collective-permute-start(f32[64,256]{1,0:T(8,128)S(1)} %shard_map.106.a_ref), channel_id=1, source_target_pairs={{0,16},{4,20},{8,24},{12,28},{16,0},{20,4},{24,8},{28,12},{1,17},{... | collective-permute-start | bytes 196616 | tf_op jit(solution)/shard_map/ppermute | solution.py:426
  30.1 3.3 %shard_map.107 = (bf16[64,512]{1,0:T(8,128)(2,1)S(1)}, f32[25,128,128]{2,1,0:T(8,128)S(1)}) custom-call(s32[8,128]{1,0:T(8,128)S(1)} %get-tuple-element.35.slots_vmem, bf16[3,64,1024]{2,1,0:T(8,128)(2,1)S(1)} %pad_maximum_fusion.own_ref, bf16[96,1024]{1,0:T(8,128)(2,1)S(1)} %get-tuple-element.44.z_ref, ...), custom_call_target="tpu_custom_call", output_to_operand_aliasing={{1}: (6, {})} | custom-call | flops 1342177280 | bytes 5984256 | tf_op jit(solution)/shard_map/pallas_call | solution.py:377
  33.4 1.2 %collective-permute-start.9 = (f32[64,256]{1,0:T(8,128)S(1)}, f32[64,256]{1,0:T(8,128)S(1)}, u32[]{:S(2)}, u32[]{:S(2)}) collective-permute-start(f32[64,256]{1,0:T(8,128)S(1)} %shard_map.108.a_ref), channel_id=1, source_target_pairs={{0,8},{4,12},{8,0},{12,4},{16,24},{20,28},{24,16},{28,20},{1,9},{5... | collective-permute-start | bytes 196616 | tf_op jit(solution)/shard_map/ppermute | solution.py:426
  34.6 2.3 %shard_map.109 = (bf16[64,1024]{1,0:T(8,128)(2,1)}, bf16[64,1024]{1,0:T(8,128)(2,1)}, bf16[64,1024]{1,0:T(8,128)(2,1)}) custom-call(bf16[64,512]{1,0:T(8,128)(2,1)S(1)} %get-tuple-element.48.dq_low, bf16[64,512]{1,0:T(8,128)(2,1)S(1)} %get-tuple-element.54.dq_high, f32[25,128,128]{2,1,0:T(8,128)S(1)} %get-tuple-element.59.past_ref, ...), custom_call_target="tpu_custom_call" | custom-call | flops 1073741824 | bytes 4980736 | tf_op jit(solution)/shard_map/pallas_call | solution.py:377
  36.9 0.8 %collective-permute-done.9.b_ref = f32[64,256]{1,0:T(8,128)S(1)} collective-permute-done((f32[64,256]{1,0:T(8,128)S(1)}, f32[64,256]{1,0:T(8,128)S(1)}, u32[]{:S(2)}, u32[]{:S(2)}) %collective-permute-start.9) | collective-permute-done | bytes 65568 | tf_op jit(solution)/shard_map/ppermute | solution.py:426
  37.7 0.6 %shard_map.110 = f32[64,256]{1,0:T(8,128)} custom-call(f32[64,256]{1,0:T(8,128)S(1)} %shard_map.108.a_ref, f32[64,256]{1,0:T(8,128)S(1)} %collective-permute-done.9.b_ref), custom_call_target="tpu_custom_call" | custom-call | bytes 196608 | tf_op jit(solution)/shard_map/pallas_call | solution.py:377
  (14 shorter events, 0.0 us)
Async XLA Ops:
  1.7 12.6 %collective-permute-start = (bf16[3,64,1024]{2,1,0:T(8,128)(2,1)S(1)}, bf16[3,64,1024]{2,1,0:T(8,128)(2,1)S(1)}, u32[]{:S(2)}, u32[]{:S(2)}) collective-permute-start(bf16[3,64,1024]{2,1,0:T(8,128)(2,1)S(1)} %pad_maximum_fusion.own_ref), channel_id=1, source_target_pairs={{0,4},{4,0},{8,12},{12,8},{16,20},{20,16},{24,28},{28,24},{1,5},{5... | collective-permute-start | bytes 1179656 | tf_op jit(solution)/shard_map/ppermute | solution.py:393
  2.2 12.1 %collective-permute-start.1 = (bf16[3,64,1024]{2,1,0:T(8,128)(2,1)S(1)}, bf16[3,64,1024]{2,1,0:T(8,128)(2,1)S(1)}, u32[]{:S(2)}, u32[]{:S(2)}) collective-permute-start(bf16[3,64,1024]{2,1,0:T(8,128)(2,1)S(1)} %pad_maximum_fusion.own_ref), channel_id=1, source_target_pairs={{4,8},{8,4},{12,16},{16,12},{20,24},{24,20},{5,9},{9,5},{13,17},{1... | collective-permute-start | bytes 1179656 | tf_op jit(solution)/shard_map/ppermute | solution.py:399
  2.9 7.4 %collective-permute-start.3 = (bf16[64,1024]{1,0:T(8,128)(2,1)}, bf16[64,1024]{1,0:T(8,128)(2,1)S(1)}, u32[]{:S(2)}, u32[]{:S(2)}) collective-permute-start(bf16[64,1024]{1,0:T(8,128)(2,1)} %refs_0_.1), channel_id=1, source_target_pairs={{0,2},{1,3},{2,0},{3,1},{4,6},{5,7},{6,4},{7,5},{8,10},{9,11},{10,... | collective-permute-start | bytes 393224 | tf_op jit(solution)/shard_map/ppermute | solution.py:409
  6.6 11.7 %collective-permute-start.2 = (bf16[64,1024]{1,0:T(8,128)(2,1)}, bf16[64,1024]{1,0:T(8,128)(2,1)S(1)}, u32[]{:S(2)}, u32[]{:S(2)}) collective-permute-start(bf16[64,1024]{1,0:T(8,128)(2,1)} %refs_0_.1), channel_id=1, source_target_pairs={{0,1},{1,0},{2,3},{3,2},{4,5},{5,4},{6,7},{7,6},{8,9},{9,8},{10,11... | collective-permute-start | bytes 393224 | tf_op jit(solution)/shard_map/ppermute | solution.py:409
  8.2 0.7 %copy-start.2 = (s32[8,8]{1,0:T(8,128)S(1)}, s32[8,8]{1,0:T(8,128)}, u32[]{:S(2)}) copy-start(s32[8,8]{1,0:T(8,128)} %lists_ref.1) | copy-start | bytes 772
  8.8 0.7 %copy-start.3 = (s32[8]{0:T(128)S(1)}, s32[8]{0:T(128)}, u32[]{:S(2)}) copy-start(s32[8]{0:T(128)} %counts_ref.1) | copy-start | bytes 100
  10.3 8.0 %collective-permute-start.4 = (bf16[64,1024]{1,0:T(8,128)(2,1)S(1)}, bf16[64,1024]{1,0:T(8,128)(2,1)S(1)}, u32[]{:S(2)}, u32[]{:S(2)}) collective-permute-start(bf16[64,1024]{1,0:T(8,128)(2,1)S(1)} %collective-permute-done.3.refs_2_), channel_id=1, source_target_pairs={{0,1},{1,0},{2,3},{3,2},{4,5},{5,4},{6,7},{7,6},{8,9},{9,8},{10,11... | collective-permute-start | bytes 393224 | tf_op jit(solution)/shard_map/ppermute | solution.py:409
  14.3 4.0 %copy-start = (bf16[64,1024]{1,0:T(8,128)(2,1)S(1)}, bf16[64,1024]{1,0:T(8,128)(2,1)}, u32[]{:S(2)}) copy-start(bf16[64,1024]{1,0:T(8,128)(2,1)} %refs_0_.1) | copy-start | bytes 393220
  14.4 4.0 %copy-start.1 = (bf16[64,256]{1,0:T(8,128)(2,1)S(1)}, bf16[64,256]{1,0:T(8,128)(2,1)}, u32[]{:S(2)}) copy-start(bf16[64,256]{1,0:T(8,128)(2,1)} %w_ref.1) | copy-start | bytes 98308
  18.8 15.8 %collective-permute-start.7 = (bf16[96,1024]{1,0:T(8,128)(2,1)S(1)}, bf16[96,1024]{1,0:T(8,128)(2,1)S(1)}, u32[]{:S(2)}, u32[]{:S(2)}) collective-permute-start(bf16[96,1024]{1,0:T(8,128)(2,1)S(1)} %get-tuple-element.44.z_ref), channel_id=1, source_target_pairs={{0,4},{4,0},{8,12},{12,8},{16,20},{20,16},{24,28},{28,24},{1,5},{5... | collective-permute-start | bytes 589832 | tf_op jit(solution)/shard_map/ppermute | solution.py:393
  20.1 14.5 %collective-permute-start.8 = (bf16[96,1024]{1,0:T(8,128)(2,1)S(1)}, bf16[96,1024]{1,0:T(8,128)(2,1)S(1)}, u32[]{:S(2)}, u32[]{:S(2)}) collective-permute-start(bf16[96,1024]{1,0:T(8,128)(2,1)S(1)} %get-tuple-element.44.z_ref), channel_id=1, source_target_pairs={{4,8},{8,4},{12,16},{16,12},{20,24},{24,20},{5,9},{9,5},{13,17},{1... | collective-permute-start | bytes 589832 | tf_op jit(solution)/shard_map/ppermute | solution.py:399
  20.7 8.0 %collective-permute-start.5 = (f32[64,256]{1,0:T(8,128)S(1)}, f32[64,256]{1,0:T(8,128)S(1)}, u32[]{:S(2)}, u32[]{:S(2)}) collective-permute-start(f32[64,256]{1,0:T(8,128)S(1)} %get-tuple-element.50.a_ref), channel_id=1, source_target_pairs={{0,4},{4,0},{8,12},{12,8},{16,20},{20,16},{24,28},{28,24},{1,5},{5... | collective-permute-start | bytes 196616 | tf_op jit(solution)/shard_map/ppermute | solution.py:426
  28.7 4.7 %collective-permute-start.6 = (f32[64,256]{1,0:T(8,128)S(1)}, f32[64,256]{1,0:T(8,128)S(1)}, u32[]{:S(2)}, u32[]{:S(2)}) collective-permute-start(f32[64,256]{1,0:T(8,128)S(1)} %shard_map.106.a_ref), channel_id=1, source_target_pairs={{0,16},{4,20},{8,24},{12,28},{16,0},{20,4},{24,8},{28,12},{1,17},{... | collective-permute-start | bytes 196616 | tf_op jit(solution)/shard_map/ppermute | solution.py:426
  33.4 4.3 %collective-permute-start.9 = (f32[64,256]{1,0:T(8,128)S(1)}, f32[64,256]{1,0:T(8,128)S(1)}, u32[]{:S(2)}, u32[]{:S(2)}) collective-permute-start(f32[64,256]{1,0:T(8,128)S(1)} %shard_map.108.a_ref), channel_id=1, source_target_pairs={{0,8},{4,12},{8,0},{12,4},{16,24},{20,28},{24,16},{28,20},{1,9},{5... | collective-permute-start | bytes 196616 | tf_op jit(solution)/shard_map/ppermute | solution.py:426

commit v4 on v3

--- a/solution.py
+++ b/solution.py
@@ -17,6 +17,8 @@
 RAW = SCALE * LOG2E
 MASKED = -1e30
 AUG = 16
+SIZES = (4, 6, MAX_KEYS)
+EARLY = (4, 4, 4)
 F32 = jnp.float32
 BF16 = jnp.bfloat16
 VMEM_LIMIT = 48 * 1024 * 1024
@@ -114,6 +116,12 @@
     vn_ref[b] = v_with
     ka_ref[b] = jnp.concatenate([k_blk, k_aug, pad], axis=0).T
     va_ref[b] = jnp.concatenate([v_with, pad], axis=0).T
+
+
+def by_need(slots_ref, run):
+    most = slots_ref[0, MAX_KEYS]
+    for low, high in zip((0,) + SIZES, SIZES):
+        pl.when(jnp.logical_and(most > low, most <= high))(functools.partial(run, high))
 
 
 def add_kernel(a_ref, b_ref, out_ref):
@@ -165,11 +173,12 @@
     wide_ref[:, :MAX_KEYS] = lists_ref[...]
     lane = lax.broadcasted_iota(jnp.int32, (blocks, BLOCK), 1)
     row = lax.broadcasted_iota(jnp.int32, (blocks, BLOCK), 0)
-    used = jnp.zeros((blocks, BLOCK), jnp.int32)
+    used, most = jnp.zeros((blocks, BLOCK), jnp.int32), 0
     for i in range(blocks):
         used = jnp.where(row == i, counts_smem[i], used)
+        most = jnp.maximum(most, counts_smem[i])
     slots = jnp.where(lane < used, wide_ref[...] - first_block, ext)
-    slots_ref[...] = slots
+    slots_ref[...] = jnp.where(lane == MAX_KEYS, most, slots)
     upper = RIM + blocks
     carry_ref[0] = packed(jnp.logical_and(slots >= upper, slots < ext), slots - upper)
     carry_ref[1] = packed(slots < RIM, slots)
@@ -226,7 +235,7 @@
 
 
 def project_kernel(count, att_ref, t_ref, carry_ref, w_ref, *refs):
-    parts, (z_ref, gw_ref) = refs[:count], refs[count:]
+    parts, (z_ref, both_ref) = refs[:count], refs[count:]
     chans, tokens = att_ref.shape
     full = jnp.concatenate([p[...] for p in parts], axis=0)
     turned = reorder(w_ref[...].astype(F32), count).astype(BF16)
@@ -242,7 +251,37 @@
             rows |= three(ROW_SPREAD, split3(-spread[:, lane_block(i)]))
             rows |= {ROW_UP: carry_ref[0, i : i + 1, :], ROW_DOWN: carry_ref[1, i : i + 1, :]}
             z_ref[first : first + AUG, lane_block(i)] = aug_rows(rows, BLOCK)
-    gw_ref[...] = reorder(dot_nt(att_ref[...].astype(BF16), full), count)
+    rows = z_ref.shape[0]
+    both_ref[:rows] = z_ref[...]
+    part = reorder(dot_nt(att_ref[...].astype(BF16), full), count)
+    high = part.astype(BF16)
+    low = (part - high.astype(F32)).astype(BF16)
+    for x, places in zip((high, low), part_places(part.shape, tokens, rows)):
+        for i, (row, lanes) in enumerate(places):
+            both_ref[row : row + AUG, lanes] = x[i * AUG : (i + 1) * AUG]
+
+
+def part_places(shape, tokens, first):
+    per_row = tokens // shape[1]
+    tiles = shape[0] // AUG
+    terms = []
+    for _ in range(2):
+        at = [divmod(i, per_row) for i in range(tiles)]
+        terms.append(
+            [(first + r * AUG, slice(c * shape[1], (c + 1) * shape[1])) for r, c in at]
+        )
+        first += -(-tiles // per_row) * AUG
+    return terms
+
+
+def parts_kernel(first, mine_ref, came_ref, out_ref):
+    shape, tokens = out_ref.shape, mine_ref.shape[1]
+    for tile, ends in enumerate(zip(*part_places(shape, tokens, first))):
+        total = None
+        for ref in (mine_ref, came_ref):
+            terms = [ref[row : row + AUG, lanes].astype(F32) for row, lanes in ends]
+            total = sum(terms) if total is None else total + sum(terms)
+        out_ref[tile * AUG : (tile + 1) * AUG] = total
 
 
 def query_side(q_ref, z_ref, here):
@@ -266,43 +305,46 @@
     q_aug, g_aug = side[:2]
     k_rows = jnp.concatenate([ka_ref[slot] for slot in slots], axis=0)
     v_rows = jnp.concatenate([va_ref[slot] for slot in slots], axis=0)
-    return dot(k_rows, q_aug), dot(v_rows, g_aug)
-
-
-def pair_grads(side, slots, scores, dprobs, acc_ref):
+    probs = jnp.exp2(dot(k_rows, q_aug) * RAW)
+    return probs.astype(BF16), (probs * dot(v_rows, g_aug)).astype(BF16)
+
+
+def pair_grads(side, slots, probs, dlow, acc_ref):
     q_out, g_out = side[2:]
-    probs = jnp.exp2(scores * RAW)
-    dlow = (probs * dprobs).astype(BF16)
-    both = dot_nt(probs.astype(BF16), g_out) + dot_nt(dlow, q_out)
+    both = dot_nt(probs, g_out) + dot_nt(dlow, q_out)
     for j, slot in enumerate(slots):
         acc_ref[slot] += both[j * BLOCK : (j + 1) * BLOCK]
-    return dlow
-
-
-def grads_kernel(start, stop, slots_vmem, own_ref, z_ref, ka_ref, va_ref, kn_ref, *refs):
+
+
+def grads_kernel(late, slots_vmem, own_ref, z_ref, ka_ref, va_ref, kn_ref, *refs):
     dq_ref, acc_ref, slots_ref, sems = refs[-4:]
     copies = start_copies((slots_vmem,), (slots_ref,), sems)
-    chans = dq_ref.shape[0]
-    heads = chans // HEAD_DIM
-    if start == 0:
+    blocks = dq_ref.shape[1] // BLOCK
+    heads = dq_ref.shape[0] // HEAD_DIM
+    if not late:
         acc_ref[...] = jnp.zeros_like(acc_ref)
     for copy in copies:
         copy.wait()
-    def begin(i):
-        slots = [slots_ref[i, j] for j in range(MAX_KEYS)]
-        side = query_side(own_ref.at[2], z_ref, lane_block(i))
-        return side, slots, *products(side, slots, ka_ref, va_ref)
-
-    def finish(i, side, slots, scores, dprobs):
-        dlow = pair_grads(side, slots, scores, dprobs, acc_ref)
-        dq = dot(jnp.concatenate([kn_ref[slot] for slot in slots], axis=1), dlow)
-        dq_ref[:, lane_block(i - start)] = (pick_heads(dq, heads) * SCALE).astype(BF16)
-
-    in_order(range(start, stop), begin, finish, 1)
+
+    def run(count):
+        def begin(i):
+            slots = [slots_ref[i, j] for j in range(count)]
+            side = query_side(own_ref.at[2], z_ref, lane_block(i))
+            return side, slots, *products(side, slots, ka_ref, va_ref)
+
+        def finish(i, side, slots, probs, dlow):
+            pair_grads(side, slots, probs, dlow, acc_ref)
+            dq = dot(jnp.concatenate([kn_ref[slot] for slot in slots], axis=1), dlow)
+            dq_ref[:, lane_block(i)] = (pick_heads(dq, heads) * SCALE).astype(BF16)
+
+        cut = EARLY[SIZES.index(count)] * blocks // 8
+        in_order(range(cut, blocks) if late else range(cut), begin, finish, 1)
+
+    by_need(slots_ref, run)
 
 
 def neighbours_kernel(
-    dq_low, dq_high, past_ref, pair_own, other_own, pair_ref, other_ref, ka_ref, va_ref,
+    dq_in, past_ref, pair_own, other_own, pair_ref, other_ref, ka_ref, va_ref,
     dq_ref, dk_ref, dv_ref, acc_ref, q_all, z_all, lists_vmem, todo_ref, lists_ref, sems,
 ):
     chans = dk_ref.shape[0]
@@ -319,17 +361,15 @@
     copies = start_copies((lists_vmem,), (lists_ref,), sems)
     q_all[0] = pair_own[2]
     q_all[1] = other_own[2]
-    z_all[0] = pair_ref[...]
+    z_all[0] = pair_ref[: z_all.shape[1]]
     z_all[1] = other_ref[...]
-    half = dq_low.shape[1]
-    dq_ref[:, :half] = dq_low[...]
-    dq_ref[:, half:] = dq_high[...]
+    dq_ref[...] = dq_in[...]
     for b in range(blocks):
         acc_ref[RIM + b] = past_ref[RIM + b]
     acc_ref[ext] = past_ref[ext]
     for copy in copies:
         copy.wait()
-    step, many = 2, 3
+    step, many = 1, 6
     count = 0
     for row in range(2 * blocks):
         for c in range(0, MAX_KEYS, step):
@@ -413,12 +453,8 @@
 
 class sum_steps:
     def __init__(self, value, axis):
-        self.axis, self.count, self.value = axis, lax.axis_size(axis), value
-        if self.count & (self.count - 1):
-            raise ValueError("axis size")
-        sizes = [1 << i for i in range(self.count.bit_length() - 1)]
-        self.steps = sizes[:1] + sizes[:0:-1]
-        self.send()
+        self.axis, self.count, self.value, self.came = axis, lax.axis_size(axis), value, None
+        self.steps = [1 << i for i in range(self.count.bit_length() - 1)][:0:-1]
 
     def send(self):
         step = self.steps.pop(0)
@@ -426,12 +462,10 @@
         self.came = lax.ppermute(self.value, self.axis, swap)
 
     def add(self):
-        shape = jax.ShapeDtypeStruct(self.value.shape, self.value.dtype)
-        (self.value,) = kernel_call(add_kernel, [shape], [self.value, self.came])
-
-    def go_on(self):
-        self.add()
-        self.send()
+        if self.came is not None:
+            shape = jax.ShapeDtypeStruct(self.value.shape, self.value.dtype)
+            (self.value,) = kernel_call(add_kernel, [shape], [self.value, self.came])
+            self.came = None
 
 
 def shards(queries, keys, values, grad_out, w_out, key_lists, key_counts):
@@ -476,40 +510,47 @@
         transcendentals=pairs,
         aliases={5 + i: i for i in range(4)},
     )
-    z, part_w = kernel_call(
+    z_rows = chans + heads * AUG
+    tail = [AUG + term[-1][0] for term in part_places(w_out.shape, tokens, z_rows)][-1]
+    z, z_and_part = kernel_call(
         functools.partial(project_kernel, head_count),
-        [shape((chans + heads * AUG, tokens), BF16), shape(w_out.shape, F32)],
+        [shape((z_rows, tokens), BF16), shape((tail, tokens), BF16)],
         [att, t, carry, w_out] + parts,
         flops=4 * w_out.size * tokens,
     )
+    pair = to_pair(z_and_part, "band")
     other = to_other(z, "band")
-    pair = to_pair(z, "band")
+    state = [shape((chans, tokens), BF16), shape((ext + 1, BLOCK, 2 * chans), F32)]
+    common = [slots, own, z, ka, va, kn]
+    cost = dict(flops=5 * pairs * BLOCK, transcendentals=pairs // 2)
+    done = kernel_call(functools.partial(grads_kernel, False), state, common, [slots], **cost)
+    done, pair = lax.optimization_barrier((done, pair))
+    (part_w,) = kernel_call(
+        functools.partial(parts_kernel, z_rows), [shape(w_out.shape, F32)], [z_and_part, pair]
+    )
     sums = sum_steps(part_w, "band")
-    acc = shape((ext + 1, BLOCK, 2 * chans), F32)
-    common, state, dq_parts = [slots, own, z, ka, va, kn], [], []
-    cuts = [0, blocks // 2, blocks]
-    for start, stop in zip(cuts, cuts[1:]):
-        dq, done = kernel_call(
-            functools.partial(grads_kernel, start, stop),
-            [shape((chans, (stop - start) * BLOCK), BF16), acc],
-            common + state,
-            [slots],
-            flops=10 * pairs * BLOCK * (stop - start) // blocks,
-            transcendentals=pairs * (stop - start) // blocks,
-            aliases={len(common): 1} if state else None,
-        )
-        dq_parts.append(dq)
+    if sums.steps:
+        sums.send()
+        done, sums.value = lax.optimization_barrier((done, sums.value))
+    done = kernel_call(
+        functools.partial(grads_kernel, True),
+        state,
+        common + list(done),
+        [slots],
+        aliases={len(common): 0, len(common) + 1: 1},
+        **cost,
+    )
+    if sums.steps:
         done, sums.came = lax.optimization_barrier((done, sums.came))
-        if sums.steps:
-            sums.go_on()
-            done, sums.value = lax.optimization_barrier((done, sums.value))
-        state = [done]
+        sums.add()
+        sums.send()
+        done, sums.value = lax.optimization_barrier((done, sums.value))
     dq, dk, dv = kernel_call(
         neighbours_kernel,
         [shape((chans, tokens), BF16)] * 3,
-        dq_parts + state + [pair_own, other_own, pair, other, ka, va],
+        list(done) + [pair_own, other_own, pair, other, ka, va],
         scratch=[
-            pltpu.VMEM(acc.shape, F32),
+            pltpu.VMEM(state[1].shape, F32),
             pltpu.VMEM((2,) + queries.shape, BF16),
             pltpu.VMEM((2,) + z.shape, BF16),
             pltpu.VMEM((2 * blocks + 8, BLOCK), jnp.int32),
@@ -520,10 +561,12 @@
         flops=4 * pairs * BLOCK,
         transcendentals=pairs // 2,
     )
-    dk, sums.came = lax.optimization_barrier((dk, sums.came))
+    if sums.came is not None:
+        dk, sums.came = lax.optimization_barrier((dk, sums.came))
+    sums.add()
     while sums.steps:
-        sums.go_on()
-    sums.add()
+        sums.send()
+        sums.add()
     return (dq, dk, dv, sums.value)
 
 

time: 38.9 us -> 37.6 us (0.967)
  starting transfers between devices: 19.6 us -> 18.5 us
  Pallas kernels: 14.7 us -> 15.7 us
  waiting for transfers between devices: 0.84 us -> 0.02 us
    ppermute x3 -> x2, starting transfers between devices: 7.26 us -> 6.12 us  [send(): self.came = lax.ppermute(self.value, self.axis, swap)]
    pallas_call x9, Pallas kernels: 14.7 us -> 15.7 us  [kernel_call(): pl.pallas_call(body, out_shape=outs, in_specs=[vmem] * len(operands), out...]
    ppermute x3 -> x2, waiting for transfers between devices: 0.82 us -> 0.01 us  [send(): self.came = lax.ppermute(self.value, self.axis, swap)]
  transfers between devices with their start and end apart: 10 -> 9, of which waited for: 1 -> 0; matrix products, arithmetic and copies ran while one was open for 0% -> 0% of each run, Pallas kernels for 35% -> 39%
where the time goes in v4:
time: 37.6 us; the launch traced here: 37.4 us
  starting transfers between devices  18.5 us (49%)
  Pallas kernels  15.7 us (42%)
  local copies, waits for them, and re-layouts  1.35 us (4%)
  other arithmetic  1.08 us (3%)
  between operations  0.79 us (2%)
    pallas_call x9, Pallas kernels, kernel_call(): pl.pallas_call(body, out_shape=outs, in_specs=[vmem] * len(operands), out...  15.7 us
    ppermute x3, starting transfers between devices, gathered(): lax.ppermute(x, axis, swap)  9.28 us
    ppermute x2, starting transfers between devices, send(): self.came = lax.ppermute(self.value, self.axis, swap)  6.12 us
    ppermute x2, starting transfers between devices, to_pair(): lax.ppermute(value, axis, [(i, i ^ 1) for i in range(last + 1) if i ^ 1 <...  1.75 us
    unnamed x8, local copies, waits for them, and re-layouts  1.35 us
    ppermute x2, starting transfers between devices, to_other(): lax.ppermute(value, axis, [(i, j) for i, j in swap if 0 <= j <= last])  1.33 us
    another operation x1, other arithmetic, shards(): own = jnp.stack([keys, values, queries])  1.08 us
  transfers between devices with their start and end apart: 9, of which 0 were waited for; matrix products, arithmetic and copies ran while one was open for 0% of the time, Pallas kernels for 39%

profile of v4, /device:TPU:0, one launch (start us, length us, event | category | flops | bytes accessed | tf_op | source)
XLA Modules:
  0.0 37.4 jit_solution(3136437047041006381)
XLA Ops:
  0.6 1.1 %pad_maximum_fusion.own_ref = bf16[3,64,1024]{2,1,0:T(8,128)(2,1)S(1)} fusion(bf16[1,64,1024]{2,1,0:T(8,128)(2,1)} %bitcast.3, bf16[1,64,1024]{2,1,0:T(8,128)(2,1)} %bitcast.4, bf16[1,64,1024]{2,1,0:T(8,128)(2,1)} %bitcast.5), kind=kLoop, calls=%fused_computation | loop fusion | flops 393216 | bytes 786432 | tf_op jit(solution)/shard_map/stack | solution.py:485
  1.7 0.5 %collective-permute-start = (bf16[3,64,1024]{2,1,0:T(8,128)(2,1)S(1)}, bf16[3,64,1024]{2,1,0:T(8,128)(2,1)S(1)}, u32[]{:S(2)}, u32[]{:S(2)}) collective-permute-start(bf16[3,64,1024]{2,1,0:T(8,128)(2,1)S(1)} %pad_maximum_fusion.own_ref), channel_id=1, source_target_pairs={{0,4},{4,0},{8,12},{12,8},{16,20},{20,16},{24,28},{28,24},{1,5},{5... | collective-permute-start | bytes 1179656 | tf_op jit(solution)/shard_map/ppermute | solution.py:433
  2.2 0.7 %collective-permute-start.1 = (bf16[3,64,1024]{2,1,0:T(8,128)(2,1)S(1)}, bf16[3,64,1024]{2,1,0:T(8,128)(2,1)S(1)}, u32[]{:S(2)}, u32[]{:S(2)}) collective-permute-start(bf16[3,64,1024]{2,1,0:T(8,128)(2,1)S(1)} %pad_maximum_fusion.own_ref), channel_id=1, source_target_pairs={{4,8},{8,4},{12,16},{16,12},{20,24},{24,20},{5,9},{9,5},{13,17},{1... | collective-permute-start | bytes 1179656 | tf_op jit(solution)/shard_map/ppermute | solution.py:439
  2.9 3.7 %collective-permute-start.3 = (bf16[64,1024]{1,0:T(8,128)(2,1)}, bf16[64,1024]{1,0:T(8,128)(2,1)S(1)}, u32[]{:S(2)}, u32[]{:S(2)}) collective-permute-start(bf16[64,1024]{1,0:T(8,128)(2,1)} %refs_0_.1), channel_id=1, source_target_pairs={{0,2},{1,3},{2,0},{3,1},{4,6},{5,7},{6,4},{7,5},{8,10},{9,11},{10,... | collective-permute-start | bytes 393224 | tf_op jit(solution)/shard_map/ppermute | solution.py:449
  6.6 1.6 %collective-permute-start.2 = (bf16[64,1024]{1,0:T(8,128)(2,1)}, bf16[64,1024]{1,0:T(8,128)(2,1)S(1)}, u32[]{:S(2)}, u32[]{:S(2)}) collective-permute-start(bf16[64,1024]{1,0:T(8,128)(2,1)} %refs_0_.1), channel_id=1, source_target_pairs={{0,1},{1,0},{2,3},{3,2},{4,5},{5,4},{6,7},{7,6},{8,9},{9,8},{10,11... | collective-permute-start | bytes 393224 | tf_op jit(solution)/shard_map/ppermute | solution.py:449
  8.2 0.7 %copy-done.2 = s32[8,8]{1,0:T(8,128)S(1)} copy-done((s32[8,8]{1,0:T(8,128)S(1)}, s32[8,8]{1,0:T(8,128)}, u32[]{:S(2)}) %copy-start.2) | copy-done | bytes 280
  8.9 0.7 %copy-done.3 = s32[8]{0:T(128)S(1)} copy-done((s32[8]{0:T(128)S(1)}, s32[8]{0:T(128)}, u32[]{:S(2)}) %copy-start.3) | copy-done | bytes 56
  9.5 0.8 %shard_map.102 = (s32[8,128]{1,0:T(8,128)S(1)}, f32[2,8,128]{2,1,0:T(8,128)S(1)}, f32[3,24,128]{2,1,0:T(8,128)S(1)}, bf16[25,128,128]{2,1,0:T(8,128)(2,1)S(1)}, ...) custom-call(bf16[3,64,1024]{2,1,0:T(8,128)(2,1)S(1)} %pad_maximum_fusion.own_re, ...), custom_call_target="tpu_custom_call" | custom-call | bytes 3002656 | tf_op jit(solution)/shard_map/pallas_call | solution.py:417
  10.3 0.0 collective-permute-done.3.refs_2_
  10.3 4.0 %collective-permute-start.4 = (bf16[64,1024]{1,0:T(8,128)(2,1)S(1)}, bf16[64,1024]{1,0:T(8,128)(2,1)S(1)}, u32[]{:S(2)}, u32[]{:S(2)}) collective-permute-start(bf16[64,1024]{1,0:T(8,128)(2,1)S(1)} %collective-permute-done.3.refs_2_), channel_id=1, source_target_pairs={{0,1},{1,0},{2,3},{3,2},{4,5},{5,4},{6,7},{7,6},{8,9},{9,8},{10,11... | collective-permute-start | bytes 393224 | tf_op jit(solution)/shard_map/ppermute | solution.py:449
  14.3 0.0 collective-permute-done.pair_ref.pair_own
  14.3 0.0 collective-permute-done.1.other_ref.other_own
  14.4 0.0 copy-start.1
  14.4 3.9 %shard_map.103 = (bf16[25,128,128]{2,1,0:T(8,128)(2,1)S(1)}, bf16[25,128,128]{2,1,0:T(8,128)(2,1)S(1)}, bf16[25,64,128]{2,1,0:T(8,128)(2,1)S(1)}, bf16[25,80,128...) custom-call(s32[8,128]{1,0:T(8,128)S(1)} %get-tuple-element.39.slots, ...), custom_call_target="tpu_custom_call", output_to_operand_aliasing={{0}: (5, {}), {1}: (6, {}), {2}: (7, {}), {3}: (8, {})} | custom-call | flops 1610612736 | bytes 6610944 | tf_op jit(solution)/shard_map/pallas_call | solution.py:417
  18.3 0.0 collective-permute-done.2.refs_1_
  18.3 0.5 %shard_map.104 = (bf16[96,1024]{1,0:T(8,128)(2,1)S(1)}, bf16[128,1024]{1,0:T(8,128)(2,1)S(1)}) custom-call(f32[64,1024]{1,0:T(8,128)S(1)} %get-tuple-element.45.att_ref, f32[8,256]{1,0:T(8,128)S(1)} %get-tuple-element.46.t_ref, f32[2,8,128]{2,1,0:T(8,128)S(1)} %get-tuple-element.47.carry_ref, bf16[64,256]{1,0:T(8,128)(2,1)S(1)} %copy-done.1, ...), custom_call_target="tpu_custom_call" | custom-call | flops 67108864 | bytes 1294336 | tf_op jit(solution)/shard_map/pallas_call | solution.py:417
  18.8 1.2 %collective-permute-start.5 = (bf16[128,1024]{1,0:T(8,128)(2,1)S(1)}, bf16[128,1024]{1,0:T(8,128)(2,1)S(1)}, u32[]{:S(2)}, u32[]{:S(2)}) collective-permute-start(bf16[128,1024]{1,0:T(8,128)(2,1)S(1)} %get-tuple-element.54.mine_ref), channel_id=1, source_target_pairs={{0,4},{4,0},{8,12},{12,8},{16,20},{20,16},{24,28},{28,24},{1,5},{5... | collective-permute-start | bytes 786440 | tf_op jit(solution)/shard_map/ppermute | solution.py:433
  20.1 0.7 %collective-permute-start.7 = (bf16[96,1024]{1,0:T(8,128)(2,1)S(1)}, bf16[96,1024]{1,0:T(8,128)(2,1)S(1)}, u32[]{:S(2)}, u32[]{:S(2)}) collective-permute-start(bf16[96,1024]{1,0:T(8,128)(2,1)S(1)} %get-tuple-element.48.z_ref), channel_id=1, source_target_pairs={{4,8},{8,4},{12,16},{16,12},{20,24},{24,20},{5,9},{9,5},{13,17},{1... | collective-permute-start | bytes 589832 | tf_op jit(solution)/shard_map/ppermute | solution.py:439
  20.8 3.3 %shard_map.105 = (bf16[64,1024]{1,0:T(8,128)(2,1)S(1)}, f32[25,128,128]{2,1,0:T(8,128)S(1)}) custom-call(s32[8,128]{1,0:T(8,128)S(1)} %get-tuple-element.39.slots_vmem, bf16[3,64,1024]{2,1,0:T(8,128)(2,1)S(1)} %pad_maximum_fusion.own_ref, bf16[96,1024]{1,0:T(8,128)(2,1)S(1)} %get-tuple-element.48.z_ref, bf16[25,128,128]{2,1,0:T(8,128)(2,1)S(1)} %get-tuple-element.49.ka_ref, ...), custom_call_target="tpu_custom_call" | custom-call | flops 1342177280 | bytes 4411392 | tf_op jit(solution)/shard_map/pallas_call | solution.py:417
  24.1 4.7 %collective-permute-start.6 = (f32[64,256]{1,0:T(8,128)S(1)}, f32[64,256]{1,0:T(8,128)S(1)}, u32[]{:S(2)}, u32[]{:S(2)}) collective-permute-start(f32[64,256]{1,0:T(8,128)S(1)} %shard_map.106.a_ref), channel_id=1, source_target_pairs={{0,16},{4,20},{8,24},{12,28},{16,0},{20,4},{24,8},{28,12},{1,17},{... | collective-permute-start | bytes 196616 | tf_op jit(solution)/shard_map/ppermute | solution.py:462
  28.8 3.5 %shard_map.107 = (bf16[64,1024]{1,0:T(8,128)(2,1)S(1)}, f32[25,128,128]{2,1,0:T(8,128)S(1)}) custom-call(s32[8,128]{1,0:T(8,128)S(1)} %get-tuple-element.39.slots_vmem, bf16[3,64,1024]{2,1,0:T(8,128)(2,1)S(1)} %pad_maximum_fusion.own_ref, bf16[96,1024]{1,0:T(8,128)(2,1)S(1)} %get-tuple-element.48.z_ref, ...), custom_call_target="tpu_custom_call", output_to_operand_aliasing={{0}: (6, {}), {1}: (7, {})} | custom-call | flops 1342177280 | bytes 6180864 | tf_op jit(solution)/shard_map/pallas_call | solution.py:417
  32.3 1.4 %collective-permute-start.8 = (f32[64,256]{1,0:T(8,128)S(1)}, f32[64,256]{1,0:T(8,128)S(1)}, u32[]{:S(2)}, u32[]{:S(2)}) collective-permute-start(f32[64,256]{1,0:T(8,128)S(1)} %shard_map.108.a_ref), channel_id=1, source_target_pairs={{0,8},{4,12},{8,0},{12,4},{16,24},{20,28},{24,16},{28,20},{1,9},{5... | collective-permute-start | bytes 196616 | tf_op jit(solution)/shard_map/ppermute | solution.py:462
  33.7 3.0 %shard_map.109 = (bf16[64,1024]{1,0:T(8,128)(2,1)}, bf16[64,1024]{1,0:T(8,128)(2,1)}, bf16[64,1024]{1,0:T(8,128)(2,1)}) custom-call(bf16[64,1024]{1,0:T(8,128)(2,1)S(1)} %get-tuple-element.66.dq_in, f32[25,128,128]{2,1,0:T(8,128)S(1)} %get-tuple-element.67.past_ref, bf16[3,64,1024]{2,1,0:T(8,128)(2,1)S(1)} %collective-permute-done.pair_ref.pair_own, ...), custom_call_target="tpu_custom_call" | custom-call | flops 1073741824 | bytes 5046272 | tf_op jit(solution)/shard_map/pallas_call | solution.py:417
  36.8 0.6 %shard_map.110 = f32[64,256]{1,0:T(8,128)} custom-call(f32[64,256]{1,0:T(8,128)S(1)} %shard_map.108.a_ref, f32[64,256]{1,0:T(8,128)S(1)} %collective-permute-done.8.b_ref), custom_call_target="tpu_custom_call" | custom-call | bytes 196608 | tf_op jit(solution)/shard_map/pallas_call | solution.py:417
  (12 shorter events, 0.1 us)
Async XLA Ops:
  1.7 12.6 %collective-permute-start = (bf16[3,64,1024]{2,1,0:T(8,128)(2,1)S(1)}, bf16[3,64,1024]{2,1,0:T(8,128)(2,1)S(1)}, u32[]{:S(2)}, u32[]{:S(2)}) collective-permute-start(bf16[3,64,1024]{2,1,0:T(8,128)(2,1)S(1)} %pad_maximum_fusion.own_ref), channel_id=1, source_target_pairs={{0,4},{4,0},{8,12},{12,8},{16,20},{20,16},{24,28},{28,24},{1,5},{5... | collective-permute-start | bytes 1179656 | tf_op jit(solution)/shard_map/ppermute | solution.py:433
  2.2 12.1 %collective-permute-start.1 = (bf16[3,64,1024]{2,1,0:T(8,128)(2,1)S(1)}, bf16[3,64,1024]{2,1,0:T(8,128)(2,1)S(1)}, u32[]{:S(2)}, u32[]{:S(2)}) collective-permute-start(bf16[3,64,1024]{2,1,0:T(8,128)(2,1)S(1)} %pad_maximum_fusion.own_ref), channel_id=1, source_target_pairs={{4,8},{8,4},{12,16},{16,12},{20,24},{24,20},{5,9},{9,5},{13,17},{1... | collective-permute-start | bytes 1179656 | tf_op jit(solution)/shard_map/ppermute | solution.py:439
  2.9 7.4 %collective-permute-start.3 = (bf16[64,1024]{1,0:T(8,128)(2,1)}, bf16[64,1024]{1,0:T(8,128)(2,1)S(1)}, u32[]{:S(2)}, u32[]{:S(2)}) collective-permute-start(bf16[64,1024]{1,0:T(8,128)(2,1)} %refs_0_.1), channel_id=1, source_target_pairs={{0,2},{1,3},{2,0},{3,1},{4,6},{5,7},{6,4},{7,5},{8,10},{9,11},{10,... | collective-permute-start | bytes 393224 | tf_op jit(solution)/shard_map/ppermute | solution.py:449
  6.6 11.7 %collective-permute-start.2 = (bf16[64,1024]{1,0:T(8,128)(2,1)}, bf16[64,1024]{1,0:T(8,128)(2,1)S(1)}, u32[]{:S(2)}, u32[]{:S(2)}) collective-permute-start(bf16[64,1024]{1,0:T(8,128)(2,1)} %refs_0_.1), channel_id=1, source_target_pairs={{0,1},{1,0},{2,3},{3,2},{4,5},{5,4},{6,7},{7,6},{8,9},{9,8},{10,11... | collective-permute-start | bytes 393224 | tf_op jit(solution)/shard_map/ppermute | solution.py:449
  8.2 0.7 %copy-start.2 = (s32[8,8]{1,0:T(8,128)S(1)}, s32[8,8]{1,0:T(8,128)}, u32[]{:S(2)}) copy-start(s32[8,8]{1,0:T(8,128)} %lists_ref.1) | copy-start | bytes 772
  8.8 0.7 %copy-start.3 = (s32[8]{0:T(128)S(1)}, s32[8]{0:T(128)}, u32[]{:S(2)}) copy-start(s32[8]{0:T(128)} %counts_ref.1) | copy-start | bytes 100
  10.3 8.0 %collective-permute-start.4 = (bf16[64,1024]{1,0:T(8,128)(2,1)S(1)}, bf16[64,1024]{1,0:T(8,128)(2,1)S(1)}, u32[]{:S(2)}, u32[]{:S(2)}) collective-permute-start(bf16[64,1024]{1,0:T(8,128)(2,1)S(1)} %collective-permute-done.3.refs_2_), channel_id=1, source_target_pairs={{0,1},{1,0},{2,3},{3,2},{4,5},{5,4},{6,7},{7,6},{8,9},{9,8},{10,11... | collective-permute-start | bytes 393224 | tf_op jit(solution)/shard_map/ppermute | solution.py:449
  14.3 4.0 %copy-start = (bf16[64,1024]{1,0:T(8,128)(2,1)S(1)}, bf16[64,1024]{1,0:T(8,128)(2,1)}, u32[]{:S(2)}) copy-start(bf16[64,1024]{1,0:T(8,128)(2,1)} %refs_0_.1) | copy-start | bytes 393220
  14.4 4.0 %copy-start.1 = (bf16[64,256]{1,0:T(8,128)(2,1)S(1)}, bf16[64,256]{1,0:T(8,128)(2,1)}, u32[]{:S(2)}) copy-start(bf16[64,256]{1,0:T(8,128)(2,1)} %w_ref.1) | copy-start | bytes 98308
  18.8 5.2 %collective-permute-start.5 = (bf16[128,1024]{1,0:T(8,128)(2,1)S(1)}, bf16[128,1024]{1,0:T(8,128)(2,1)S(1)}, u32[]{:S(2)}, u32[]{:S(2)}) collective-permute-start(bf16[128,1024]{1,0:T(8,128)(2,1)S(1)} %get-tuple-element.54.mine_ref), channel_id=1, source_target_pairs={{0,4},{4,0},{8,12},{12,8},{16,20},{20,16},{24,28},{28,24},{1,5},{5... | collective-permute-start | bytes 786440 | tf_op jit(solution)/shard_map/ppermute | solution.py:433
  20.1 13.7 %collective-permute-start.7 = (bf16[96,1024]{1,0:T(8,128)(2,1)S(1)}, bf16[96,1024]{1,0:T(8,128)(2,1)S(1)}, u32[]{:S(2)}, u32[]{:S(2)}) collective-permute-start(bf16[96,1024]{1,0:T(8,128)(2,1)S(1)} %get-tuple-element.48.z_ref), channel_id=1, source_target_pairs={{4,8},{8,4},{12,16},{16,12},{20,24},{24,20},{5,9},{9,5},{13,17},{1... | collective-permute-start | bytes 589832 | tf_op jit(solution)/shard_map/ppermute | solution.py:439
  24.1 8.2 %collective-permute-start.6 = (f32[64,256]{1,0:T(8,128)S(1)}, f32[64,256]{1,0:T(8,128)S(1)}, u32[]{:S(2)}, u32[]{:S(2)}) collective-permute-start(f32[64,256]{1,0:T(8,128)S(1)} %shard_map.106.a_ref), channel_id=1, source_target_pairs={{0,16},{4,20},{8,24},{12,28},{16,0},{20,4},{24,8},{28,12},{1,17},{... | collective-permute-start | bytes 196616 | tf_op jit(solution)/shard_map/ppermute | solution.py:462
  32.3 4.5 %collective-permute-start.8 = (f32[64,256]{1,0:T(8,128)S(1)}, f32[64,256]{1,0:T(8,128)S(1)}, u32[]{:S(2)}, u32[]{:S(2)}) collective-permute-start(f32[64,256]{1,0:T(8,128)S(1)} %shard_map.108.a_ref), channel_id=1, source_target_pairs={{0,8},{4,12},{8,0},{12,4},{16,24},{20,28},{24,16},{28,20},{1,9},{5... | collective-permute-start | bytes 196616 | tf_op jit(solution)/shard_map/ppermute | solution.py:462

commit v5 on v4

--- a/solution.py
+++ b/solution.py
@@ -17,8 +17,8 @@
 RAW = SCALE * LOG2E
 MASKED = -1e30
 AUG = 16
-SIZES = (4, 6, MAX_KEYS)
-EARLY = (4, 4, 4)
+SIZES = (4, 5, 7, MAX_KEYS)
+EARLY = (0, 0, 3, 3)
 F32 = jnp.float32
 BF16 = jnp.bfloat16
 VMEM_LIMIT = 48 * 1024 * 1024
@@ -47,7 +47,8 @@
     return out.astype(BF16)
 
 
-ROW_BIAS, ROW_LSE, ROW_SPREAD, ROW_UP, ROW_DOWN = 0, 3, 8, 12, 13
+ROW_LSE, ROW_SPREAD, ROW_BIAS = 0, 3, 6
+PER_HEAD = 6
 
 
 def three(first, rows):
@@ -125,7 +126,7 @@
 
 
 def add_kernel(a_ref, b_ref, out_ref):
-    out_ref[...] = a_ref[...] + b_ref[...]
+    out_ref[...] = (a_ref[...].astype(F32) + b_ref[...].astype(F32)).astype(out_ref.dtype)
 
 
 def packed(chosen, values):
@@ -146,10 +147,11 @@
 
 def prepare_kernel(
     total, own_ref, lists_ref, counts_ref,
-    slots_ref, carry_ref, bias_ref, ka_ref, va_ref, kn_ref, vn_ref,
+    slots_ref, carry_ref, bias_ref, acc_ref, ka_ref, va_ref, kn_ref, vn_ref,
     wide_ref, counts_smem, sems,
 ):
     copies = start_copies((counts_ref,), (counts_smem,), sems)
+    acc_ref[...] = jnp.zeros_like(acc_ref)
     chans = own_ref.shape[1]
     blocks = own_ref.shape[2] // BLOCK
     ext = blocks + 2 * RIM
@@ -234,23 +236,30 @@
     return x
 
 
-def project_kernel(count, att_ref, t_ref, carry_ref, w_ref, *refs):
-    parts, (z_ref, both_ref) = refs[:count], refs[count:]
+def project_kernel(
+    count, slots_vmem, own_ref, att_ref, t_ref, carry_ref, w_ref, ka_ref, va_ref, kn_ref, acc_in, *refs
+):
+    parts, (z_ref, both_ref, dq_ref, acc_ref, slots_ref, sems) = refs[:count], refs[count:]
+    copies = start_copies((slots_vmem,), (slots_ref,), sems)
     chans, tokens = att_ref.shape
     full = jnp.concatenate([p[...] for p in parts], axis=0)
     turned = reorder(w_ref[...].astype(F32), count).astype(BF16)
     grad = dot(turned, full).astype(BF16)
     z_ref[:chans] = grad
     prod = grad.astype(F32) * att_ref[...]
-    for h in range(chans // HEAD_DIM):
-        spread = jnp.sum(prod[h * HEAD_DIM : (h + 1) * HEAD_DIM], axis=0, keepdims=True)
-        first = chans + h * AUG
-        for i in range(tokens // BLOCK):
+    heads = chans // HEAD_DIM
+    spreads = [
+        jnp.sum(prod[h * HEAD_DIM : (h + 1) * HEAD_DIM], axis=0, keepdims=True)
+        for h in range(heads)
+    ]
+    for i in range(tokens // BLOCK):
+        rows = {}
+        for h in range(heads):
             t = t_ref[i : i + 1, h * BLOCK : (h + 1) * BLOCK]
-            rows = three(ROW_BIAS, ONES) | three(ROW_LSE, split3(-t))
-            rows |= three(ROW_SPREAD, split3(-spread[:, lane_block(i)]))
-            rows |= {ROW_UP: carry_ref[0, i : i + 1, :], ROW_DOWN: carry_ref[1, i : i + 1, :]}
-            z_ref[first : first + AUG, lane_block(i)] = aug_rows(rows, BLOCK)
+            rows |= three(PER_HEAD * h + ROW_LSE, split3(-t))
+            rows |= three(PER_HEAD * h + ROW_SPREAD, split3(-spreads[h][:, lane_block(i)]))
+        rows |= {PER_HEAD * heads + s: carry_ref[s, i : i + 1, :] for s in range(2)}
+        z_ref[chans:, lane_block(i)] = aug_rows(rows, BLOCK)
     rows = z_ref.shape[0]
     both_ref[:rows] = z_ref[...]
     part = reorder(dot_nt(att_ref[...].astype(BF16), full), count)
@@ -259,6 +268,18 @@
     for x, places in zip((high, low), part_places(part.shape, tokens, rows)):
         for i, (row, lanes) in enumerate(places):
             both_ref[row : row + AUG, lanes] = x[i * AUG : (i + 1) * AUG]
+    for copy in copies:
+        copy.wait()
+    blocks = tokens // BLOCK
+
+    def run(most):
+        steps = range(EARLY[SIZES.index(most)] * blocks // 8)
+        if steps:
+            block_grads(
+                steps, most, own_ref, z_ref, ka_ref, va_ref, kn_ref, dq_ref, acc_ref, slots_ref
+            )
+
+    by_need(slots_ref, run)
 
 
 def part_places(shape, tokens, first):
@@ -290,8 +311,11 @@
     width = heads * BLOCK
     q_wide = spread_heads(q_ref[:, here], heads)
     g_wide = spread_heads(z_ref[:chans, here], heads)
-    tiles = [z_ref[chans + h * AUG : chans + (h + 1) * AUG, here] for h in range(heads)]
-    aug = jnp.concatenate(tiles, axis=1)
+    tile = z_ref[chans:, here].astype(F32)
+    at = lax.broadcasted_iota(jnp.int32, tile.shape, 0)
+    ones = jnp.logical_and(at >= ROW_BIAS, at < ROW_BIAS + 3)
+    tiles = [tile] + [pltpu.roll(tile, AUG - PER_HEAD * h, 0) for h in range(1, heads)]
+    aug = jnp.concatenate([jnp.where(ones, 1.0, x).astype(BF16) for x in tiles], axis=1)
     pad = jnp.zeros((BLOCK - chans - AUG, width), BF16)
     none = jnp.zeros((chans, width), BF16)
     q_aug = jnp.concatenate([q_wide, aug, pad], axis=0)
@@ -316,29 +340,36 @@
         acc_ref[slot] += both[j * BLOCK : (j + 1) * BLOCK]
 
 
-def grads_kernel(late, slots_vmem, own_ref, z_ref, ka_ref, va_ref, kn_ref, *refs):
-    dq_ref, acc_ref, slots_ref, sems = refs[-4:]
+def block_grads(steps, count, own_ref, z_ref, ka_ref, va_ref, kn_ref, dq_ref, acc_ref, slots_ref):
+    heads = dq_ref.shape[0] // HEAD_DIM
+
+    def begin(i):
+        slots = [slots_ref[i, j] for j in range(count)]
+        side = query_side(own_ref.at[2], z_ref, lane_block(i))
+        return side, slots, *products(side, slots, ka_ref, va_ref)
+
+    def finish(i, side, slots, probs, dlow):
+        pair_grads(side, slots, probs, dlow, acc_ref)
+        dq = dot(jnp.concatenate([kn_ref[slot] for slot in slots], axis=1), dlow)
+        dq_ref[:, lane_block(i)] = (pick_heads(dq, heads) * SCALE).astype(BF16)
+
+    in_order(steps, begin, finish, 1)
+
+
+def grads_kernel(
+    slots_vmem, own_ref, z_ref, ka_ref, va_ref, kn_ref, dq_in, acc_in,
+    dq_ref, acc_ref, slots_ref, sems,
+):
     copies = start_copies((slots_vmem,), (slots_ref,), sems)
     blocks = dq_ref.shape[1] // BLOCK
-    heads = dq_ref.shape[0] // HEAD_DIM
-    if not late:
-        acc_ref[...] = jnp.zeros_like(acc_ref)
     for copy in copies:
         copy.wait()
 
-    def run(count):
-        def begin(i):
-            slots = [slots_ref[i, j] for j in range(count)]
-            side = query_side(own_ref.at[2], z_ref, lane_block(i))
-            return side, slots, *products(side, slots, ka_ref, va_ref)
-
-        def finish(i, side, slots, probs, dlow):
-            pair_grads(side, slots, probs, dlow, acc_ref)
-            dq = dot(jnp.concatenate([kn_ref[slot] for slot in slots], axis=1), dlow)
-            dq_ref[:, lane_block(i)] = (pick_heads(dq, heads) * SCALE).astype(BF16)
-
-        cut = EARLY[SIZES.index(count)] * blocks // 8
-        in_order(range(cut, blocks) if late else range(cut), begin, finish, 1)
+    def run(most):
+        steps = range(EARLY[SIZES.index(most)] * blocks // 8, blocks)
+        block_grads(
+            steps, most, own_ref, z_ref, ka_ref, va_ref, kn_ref, dq_ref, acc_ref, slots_ref
+        )
 
     by_need(slots_ref, run)
 
@@ -353,7 +384,8 @@
     odd = lax.rem(lax.axis_index("band"), 2) == 1
     for s, (ref, below) in enumerate(((pair_ref, odd), (other_ref, jnp.logical_not(odd)))):
         rows = ref[chans : chans + AUG].astype(F32)
-        row = jnp.where(below, rows[ROW_UP : ROW_UP + 1], rows[ROW_DOWN : ROW_DOWN + 1])
+        up = PER_HEAD * (chans // HEAD_DIM)
+        row = jnp.where(below, rows[up : up + 1], rows[up + 1 : up + 2])
         for i in range(blocks):
             at = s * blocks + i
             lists_vmem[at : at + 1] = row[:, lane_block(i)].astype(jnp.int32)
@@ -463,7 +495,8 @@
 
     def add(self):
         if self.came is not None:
-            shape = jax.ShapeDtypeStruct(self.value.shape, self.value.dtype)
+            kind = BF16 if len(self.steps) == 1 else F32
+            shape = jax.ShapeDtypeStruct(self.value.shape, kind)
             (self.value,) = kernel_call(add_kernel, [shape], [self.value, self.came])
             self.came = None
 
@@ -479,19 +512,20 @@
     shape = jax.ShapeDtypeStruct
     pairs = blocks * MAX_KEYS * width * BLOCK
 
-    if blocks != RIM:
+    if blocks != RIM or PER_HEAD * heads + 2 > AUG:
         raise ValueError("band size")
     like = lambda x: shape(x.shape, x.dtype)
     own = jnp.stack([keys, values, queries])
     other_own = to_other(own, "band")
     pair_own = to_pair(own, "band")
     parts = gathered(grad_out, "head")
-    slots, carry, bias, *state = kernel_call(
+    slots, carry, bias, acc, *state = kernel_call(
         functools.partial(prepare_kernel, total),
         [
             shape((blocks, BLOCK), jnp.int32),
             shape((2, blocks, BLOCK), F32),
             shape((3, ext, BLOCK), F32),
+            shape((ext + 1, BLOCK, 2 * chans), F32),
             shape((ext + 1, BLOCK, BLOCK), BF16),
             shape((ext + 1, BLOCK, BLOCK), BF16),
             shape((ext + 1, chans, BLOCK), BF16),
@@ -510,20 +544,20 @@
         transcendentals=pairs,
         aliases={5 + i: i for i in range(4)},
     )
-    z_rows = chans + heads * AUG
+    z_rows = chans + AUG
     tail = [AUG + term[-1][0] for term in part_places(w_out.shape, tokens, z_rows)][-1]
-    z, z_and_part = kernel_call(
+    data = [ka, va, kn]
+    operands = [slots, own, att, t, carry, w_out] + data + [acc]
+    z, z_and_part, *done = kernel_call(
         functools.partial(project_kernel, head_count),
-        [shape((z_rows, tokens), BF16), shape((tail, tokens), BF16)],
-        [att, t, carry, w_out] + parts,
+        [shape((z_rows, tokens), BF16), shape((tail, tokens), BF16), like(queries), like(acc)],
+        operands + parts,
+        [slots],
         flops=4 * w_out.size * tokens,
+        aliases={len(operands) - 1: 3},
     )
     pair = to_pair(z_and_part, "band")
     other = to_other(z, "band")
-    state = [shape((chans, tokens), BF16), shape((ext + 1, BLOCK, 2 * chans), F32)]
-    common = [slots, own, z, ka, va, kn]
-    cost = dict(flops=5 * pairs * BLOCK, transcendentals=pairs // 2)
-    done = kernel_call(functools.partial(grads_kernel, False), state, common, [slots], **cost)
     done, pair = lax.optimization_barrier((done, pair))
     (part_w,) = kernel_call(
         functools.partial(parts_kernel, z_rows), [shape(w_out.shape, F32)], [z_and_part, pair]
@@ -533,12 +567,13 @@
         sums.send()
         done, sums.value = lax.optimization_barrier((done, sums.value))
     done = kernel_call(
-        functools.partial(grads_kernel, True),
-        state,
-        common + list(done),
+        grads_kernel,
+        [like(x) for x in done],
+        [slots, own, z] + data + list(done),
         [slots],
-        aliases={len(common): 0, len(common) + 1: 1},
-        **cost,
+        flops=10 * pairs * BLOCK,
+        transcendentals=pairs,
+        aliases={6: 0, 7: 1},
     )
     if sums.steps:
         done, sums.came = lax.optimization_barrier((done, sums.came))
@@ -550,7 +585,7 @@
         [shape((chans, tokens), BF16)] * 3,
         list(done) + [pair_own, other_own, pair, other, ka, va],
         scratch=[
-            pltpu.VMEM(state[1].shape, F32),
+            pltpu.VMEM(acc.shape, F32),
             pltpu.VMEM((2,) + queries.shape, BF16),
             pltpu.VMEM((2,) + z.shape, BF16),
             pltpu.VMEM((2 * blocks + 8, BLOCK), jnp.int32),

time: 37.6 us -> 35.9 us (0.955)
  starting transfers between devices: 18.5 us -> 16.3 us
  waiting for transfers between devices: 0.02 us -> 1.3 us
  Pallas kernels: 15.7 us -> 14.9 us
    ppermute x2, starting transfers between devices: 6.12 us -> 4.43 us  [send(): self.came = lax.ppermute(self.value, self.axis, swap)]
    ppermute x2, waiting for transfers between devices: 0.01 us -> 0.83 us  [send(): self.came = lax.ppermute(self.value, self.axis, swap)]
    pallas_call x9 -> x8, Pallas kernels: 15.7 us -> 14.9 us  [kernel_call(): pl.pallas_call(body, out_shape=outs, in_specs=[vmem] * len(operands), out...]
    ppermute x2, waiting for transfers between devices: 0.01 us -> 0.45 us  [to_pair(): lax.ppermute(value, axis, [(i, i ^ 1) for i in range(last + 1) if i ^ 1 <...]
  transfers between devices with their start and end apart: 9 -> 9, of which waited for: 0 -> 2; matrix products, arithmetic and copies ran while one was open for 0% -> 0% of each run, Pallas kernels for 39% -> 33%
where the time goes in v5:
time: 35.9 us; the launch traced here: 35.7 us
  starting transfers between devices  16.3 us (45%)
  Pallas kernels  14.9 us (42%)
  local copies, waits for them, and re-layouts  1.35 us (4%)
  waiting for transfers between devices  1.3 us (4%)
  other arithmetic  1.08 us (3%)
  between operations  0.77 us (2%)
    pallas_call x8, Pallas kernels, kernel_call(): pl.pallas_call(body, out_shape=outs, in_specs=[vmem] * len(operands), out...  14.9 us
    ppermute x3, starting transfers between devices, gathered(): lax.ppermute(x, axis, swap)  9.02 us
    ppermute x2, starting transfers between devices, send(): self.came = lax.ppermute(self.value, self.axis, swap)  4.43 us
    ppermute x2, starting transfers between devices, to_pair(): lax.ppermute(value, axis, [(i, i ^ 1) for i in range(last + 1) if i ^ 1 <...  1.5 us
    unnamed x8, local copies, waits for them, and re-layouts  1.35 us
    ppermute x2, starting transfers between devices, to_other(): lax.ppermute(value, axis, [(i, j) for i, j in swap if 0 <= j <= last])  1.33 us
    another operation x1, other arithmetic, shards(): own = jnp.stack([keys, values, queries])  1.08 us
    ppermute x2, waiting for transfers between devices, send(): self.came = lax.ppermute(self.value, self.axis, swap)  0.83 us
  transfers between devices with their start and end apart: 9, of which 2 were waited for; matrix products, arithmetic and copies ran while one was open for 0% of the time, Pallas kernels for 33%

profile of v5, /device:TPU:0, one launch (start us, length us, event | category | flops | bytes accessed | tf_op | source)
XLA Modules:
  0.0 35.7 jit_solution(11069570241352986139)
XLA Ops:
  0.6 1.1 %pad_maximum_fusion.own_ref = bf16[3,64,1024]{2,1,0:T(8,128)(2,1)S(1)} fusion(bf16[1,64,1024]{2,1,0:T(8,128)(2,1)} %bitcast.3, bf16[1,64,1024]{2,1,0:T(8,128)(2,1)} %bitcast.4, bf16[1,64,1024]{2,1,0:T(8,128)(2,1)} %bitcast.5), kind=kLoop, calls=%fused_computation | loop fusion | flops 393216 | bytes 786432 | tf_op jit(solution)/shard_map/stack | solution.py:518
  1.7 0.5 %collective-permute-start = (bf16[3,64,1024]{2,1,0:T(8,128)(2,1)S(1)}, bf16[3,64,1024]{2,1,0:T(8,128)(2,1)S(1)}, u32[]{:S(2)}, u32[]{:S(2)}) collective-permute-start(bf16[3,64,1024]{2,1,0:T(8,128)(2,1)S(1)} %pad_maximum_fusion.own_ref), channel_id=1, source_target_pairs={{0,4},{4,0},{8,12},{12,8},{16,20},{20,16},{24,28},{28,24},{1,5},{5... | collective-permute-start | bytes 1179656 | tf_op jit(solution)/shard_map/ppermute | solution.py:465
  2.2 0.7 %collective-permute-start.1 = (bf16[3,64,1024]{2,1,0:T(8,128)(2,1)S(1)}, bf16[3,64,1024]{2,1,0:T(8,128)(2,1)S(1)}, u32[]{:S(2)}, u32[]{:S(2)}) collective-permute-start(bf16[3,64,1024]{2,1,0:T(8,128)(2,1)S(1)} %pad_maximum_fusion.own_ref), channel_id=1, source_target_pairs={{4,8},{8,4},{12,16},{16,12},{20,24},{24,20},{5,9},{9,5},{13,17},{1... | collective-permute-start | bytes 1179656 | tf_op jit(solution)/shard_map/ppermute | solution.py:471
  2.9 3.7 %collective-permute-start.3 = (bf16[64,1024]{1,0:T(8,128)(2,1)}, bf16[64,1024]{1,0:T(8,128)(2,1)S(1)}, u32[]{:S(2)}, u32[]{:S(2)}) collective-permute-start(bf16[64,1024]{1,0:T(8,128)(2,1)} %refs_0_.1), channel_id=1, source_target_pairs={{0,2},{1,3},{2,0},{3,1},{4,6},{5,7},{6,4},{7,5},{8,10},{9,11},{10,... | collective-permute-start | bytes 393224 | tf_op jit(solution)/shard_map/ppermute | solution.py:481
  6.6 1.6 %collective-permute-start.2 = (bf16[64,1024]{1,0:T(8,128)(2,1)}, bf16[64,1024]{1,0:T(8,128)(2,1)S(1)}, u32[]{:S(2)}, u32[]{:S(2)}) collective-permute-start(bf16[64,1024]{1,0:T(8,128)(2,1)} %refs_0_.1), channel_id=1, source_target_pairs={{0,1},{1,0},{2,3},{3,2},{4,5},{5,4},{6,7},{7,6},{8,9},{9,8},{10,11... | collective-permute-start | bytes 393224 | tf_op jit(solution)/shard_map/ppermute | solution.py:481
  8.2 0.7 %copy-done.2 = s32[8,8]{1,0:T(8,128)S(1)} copy-done((s32[8,8]{1,0:T(8,128)S(1)}, s32[8,8]{1,0:T(8,128)}, u32[]{:S(2)}) %copy-start.2) | copy-done | bytes 280
  8.9 0.7 %copy-done.3 = s32[8]{0:T(128)S(1)} copy-done((s32[8]{0:T(128)S(1)}, s32[8]{0:T(128)}, u32[]{:S(2)}) %copy-start.3) | copy-done | bytes 56
  9.5 1.0 %shard_map.102 = (s32[8,128]{1,0:T(8,128)S(1)}, f32[2,8,128]{2,1,0:T(8,128)S(1)}, f32[3,24,128]{2,1,0:T(8,128)S(1)}, f32[25,128,128]{2,1,0:T(8,128)S(1)}, bf16[2...) custom-call(bf16[3,64,1024]{2,1,0:T(8,128)(2,1)S(1)} %pad_maximum_fu, ...), custom_call_target="tpu_custom_call" | custom-call | bytes 4641056 | tf_op jit(solution)/shard_map/pallas_call | solution.py:449
  10.6 3.8 %collective-permute-start.4 = (bf16[64,1024]{1,0:T(8,128)(2,1)S(1)}, bf16[64,1024]{1,0:T(8,128)(2,1)S(1)}, u32[]{:S(2)}, u32[]{:S(2)}) collective-permute-start(bf16[64,1024]{1,0:T(8,128)(2,1)S(1)} %collective-permute-done.3.refs_2_), channel_id=1, source_target_pairs={{0,1},{1,0},{2,3},{3,2},{4,5},{5,4},{6,7},{7,6},{8,9},{9,8},{10,11... | collective-permute-start | bytes 393224 | tf_op jit(solution)/shard_map/ppermute | solution.py:481
  14.3 0.0 collective-permute-done.pair_ref.pair_own
  14.3 0.0 collective-permute-done.1.other_ref.other_own
  14.4 0.0 copy-start.1
  14.4 4.0 %shard_map.103 = (bf16[25,128,128]{2,1,0:T(8,128)(2,1)S(1)}, bf16[25,128,128]{2,1,0:T(8,128)(2,1)S(1)}, bf16[25,64,128]{2,1,0:T(8,128)(2,1)S(1)}, bf16[25,80,128...) custom-call(s32[8,128]{1,0:T(8,128)S(1)} %get-tuple-element.40.slots, ...), custom_call_target="tpu_custom_call", output_to_operand_aliasing={{0}: (5, {}), {1}: (6, {}), {2}: (7, {}), {3}: (8, {})} | custom-call | flops 1610612736 | bytes 6610944 | tf_op jit(solution)/shard_map/pallas_call | solution.py:449
  18.3 0.0 collective-permute-done.4.refs_3_
  18.4 2.7 %shard_map.104 = (bf16[80,1024]{1,0:T(8,128)(2,1)S(1)}, bf16[112,1024]{1,0:T(8,128)(2,1)S(1)}, bf16[64,1024]{1,0:T(8,128)(2,1)S(1)}, f32[25,128,128]{2,1,0:T(8,128)S(1)}) custom-call(s32[8,128]{1,0:T(8,128)S(1)} %get-tuple-element.40.slots_vmem, bf16[3,64,1024]{2,1,0:T(8,128)(2,1)S(1)} %pad_maximum_fusion.own_ref, ...), custom_call_target="tpu_custom_call", output_to_operand_aliasing={{3}: (9, {})} | custom-call | flops 67108864 | bytes 7081984 | tf_op jit(solution)/shard_map/pallas_call | solution.py:449
  21.0 1.0 %collective-permute-start.5 = (bf16[112,1024]{1,0:T(8,128)(2,1)S(1)}, bf16[112,1024]{1,0:T(8,128)(2,1)S(1)}, u32[]{:S(2)}, u32[]{:S(2)}) collective-permute-start(bf16[112,1024]{1,0:T(8,128)(2,1)S(1)} %get-tuple-element.56.mine_ref), channel_id=1, source_target_pairs={{0,4},{4,0},{8,12},{12,8},{16,20},{20,16},{24,28},{28,24},{1,5},{5... | collective-permute-start | bytes 688136 | tf_op jit(solution)/shard_map/ppermute | solution.py:465
  22.0 0.7 %collective-permute-start.7 = (bf16[80,1024]{1,0:T(8,128)(2,1)S(1)}, bf16[80,1024]{1,0:T(8,128)(2,1)S(1)}, u32[]{:S(2)}, u32[]{:S(2)}) collective-permute-start(bf16[80,1024]{1,0:T(8,128)(2,1)S(1)} %get-tuple-element.53.z_ref), channel_id=1, source_target_pairs={{4,8},{8,4},{12,16},{16,12},{20,24},{24,20},{5,9},{9,5},{13,17},{1... | collective-permute-start | bytes 491528 | tf_op jit(solution)/shard_map/ppermute | solution.py:471
  22.7 0.4 %collective-permute-done.5.came_ref.pair_ref = bf16[112,1024]{1,0:T(8,128)(2,1)S(1)} collective-permute-done((bf16[112,1024]{1,0:T(8,128)(2,1)S(1)}, bf16[112,1024]{1,0:T(8,128)(2,1)S(1)}, u32[]{:S(2)}, u32[]{:S(2)}) %collective-permute-start.5) | collective-permute-done | bytes 229408 | tf_op jit(solution)/shard_map/ppermute | solution.py:465
  23.2 3.8 %collective-permute-start.6 = (f32[64,256]{1,0:T(8,128)S(1)}, f32[64,256]{1,0:T(8,128)S(1)}, u32[]{:S(2)}, u32[]{:S(2)}) collective-permute-start(f32[64,256]{1,0:T(8,128)S(1)} %shard_map.105.a_ref), channel_id=1, source_target_pairs={{0,16},{4,20},{8,24},{12,28},{16,0},{20,4},{24,8},{28,12},{1,17},{... | collective-permute-start | bytes 196616 | tf_op jit(solution)/shard_map/ppermute | solution.py:494
  26.9 4.1 %shard_map.106 = (bf16[64,1024]{1,0:T(8,128)(2,1)S(1)}, f32[25,128,128]{2,1,0:T(8,128)S(1)}) custom-call(s32[8,128]{1,0:T(8,128)S(1)} %get-tuple-element.40.slots_vmem, bf16[3,64,1024]{2,1,0:T(8,128)(2,1)S(1)} %pad_maximum_fusion.own_ref, bf16[80,1024]{1,0:T(8,128)(2,1)S(1)} %get-tuple-element.53.z_ref, ...), custom_call_target="tpu_custom_call", output_to_operand_aliasing={{0}: (6, {}), {1}: (7, {})} | custom-call | flops 2684354560 | bytes 6148096 | tf_op jit(solution)/shard_map/pallas_call | solution.py:449
  31.1 0.7 %collective-permute-start.8 = (bf16[64,256]{1,0:T(8,128)(2,1)S(1)}, bf16[64,256]{1,0:T(8,128)(2,1)S(1)}, u32[]{:S(2)}, u32[]{:S(2)}) collective-permute-start(bf16[64,256]{1,0:T(8,128)(2,1)S(1)} %shard_map.107.a_ref), channel_id=1, source_target_pairs={{0,8},{4,12},{8,0},{12,4},{16,24},{20,28},{24,16},{28,20},{1,9},{5... | collective-permute-start | bytes 98312 | tf_op jit(solution)/shard_map/ppermute | solution.py:494
  31.7 2.5 %shard_map.108 = (bf16[64,1024]{1,0:T(8,128)(2,1)}, bf16[64,1024]{1,0:T(8,128)(2,1)}, bf16[64,1024]{1,0:T(8,128)(2,1)}) custom-call(bf16[64,1024]{1,0:T(8,128)(2,1)S(1)} %get-tuple-element.68.dq_in, f32[25,128,128]{2,1,0:T(8,128)S(1)} %get-tuple-element.69.past_ref, bf16[3,64,1024]{2,1,0:T(8,128)(2,1)S(1)} %collective-permute-done.pair_ref.pair_own, ...), custom_call_target="tpu_custom_call" | custom-call | flops 1073741824 | bytes 4980736 | tf_op jit(solution)/shard_map/pallas_call | solution.py:449
  34.2 0.8 %collective-permute-done.8.b_ref = bf16[64,256]{1,0:T(8,128)(2,1)S(1)} collective-permute-done((bf16[64,256]{1,0:T(8,128)(2,1)S(1)}, bf16[64,256]{1,0:T(8,128)(2,1)S(1)}, u32[]{:S(2)}, u32[]{:S(2)}) %collective-permute-start.8) | collective-permute-done | bytes 32800 | tf_op jit(solution)/shard_map/ppermute | solution.py:494
  35.0 0.6 %shard_map.109 = f32[64,256]{1,0:T(8,128)} custom-call(bf16[64,256]{1,0:T(8,128)(2,1)S(1)} %shard_map.107.a_ref, bf16[64,256]{1,0:T(8,128)(2,1)S(1)} %collective-permute-done.8.b_ref), custom_call_target="tpu_custom_call" | custom-call | bytes 131072 | tf_op jit(solution)/shard_map/pallas_call | solution.py:449
  (11 shorter events, 0.0 us)
Async XLA Ops:
  1.7 12.6 %collective-permute-start = (bf16[3,64,1024]{2,1,0:T(8,128)(2,1)S(1)}, bf16[3,64,1024]{2,1,0:T(8,128)(2,1)S(1)}, u32[]{:S(2)}, u32[]{:S(2)}) collective-permute-start(bf16[3,64,1024]{2,1,0:T(8,128)(2,1)S(1)} %pad_maximum_fusion.own_ref), channel_id=1, source_target_pairs={{0,4},{4,0},{8,12},{12,8},{16,20},{20,16},{24,28},{28,24},{1,5},{5... | collective-permute-start | bytes 1179656 | tf_op jit(solution)/shard_map/ppermute | solution.py:465
  2.2 12.1 %collective-permute-start.1 = (bf16[3,64,1024]{2,1,0:T(8,128)(2,1)S(1)}, bf16[3,64,1024]{2,1,0:T(8,128)(2,1)S(1)}, u32[]{:S(2)}, u32[]{:S(2)}) collective-permute-start(bf16[3,64,1024]{2,1,0:T(8,128)(2,1)S(1)} %pad_maximum_fusion.own_ref), channel_id=1, source_target_pairs={{4,8},{8,4},{12,16},{16,12},{20,24},{24,20},{5,9},{9,5},{13,17},{1... | collective-permute-start | bytes 1179656 | tf_op jit(solution)/shard_map/ppermute | solution.py:471
  2.9 7.6 %collective-permute-start.3 = (bf16[64,1024]{1,0:T(8,128)(2,1)}, bf16[64,1024]{1,0:T(8,128)(2,1)S(1)}, u32[]{:S(2)}, u32[]{:S(2)}) collective-permute-start(bf16[64,1024]{1,0:T(8,128)(2,1)} %refs_0_.1), channel_id=1, source_target_pairs={{0,2},{1,3},{2,0},{3,1},{4,6},{5,7},{6,4},{7,5},{8,10},{9,11},{10,... | collective-permute-start | bytes 393224 | tf_op jit(solution)/shard_map/ppermute | solution.py:481
  6.6 11.7 %collective-permute-start.2 = (bf16[64,1024]{1,0:T(8,128)(2,1)}, bf16[64,1024]{1,0:T(8,128)(2,1)S(1)}, u32[]{:S(2)}, u32[]{:S(2)}) collective-permute-start(bf16[64,1024]{1,0:T(8,128)(2,1)} %refs_0_.1), channel_id=1, source_target_pairs={{0,1},{1,0},{2,3},{3,2},{4,5},{5,4},{6,7},{7,6},{8,9},{9,8},{10,11... | collective-permute-start | bytes 393224 | tf_op jit(solution)/shard_map/ppermute | solution.py:481
  8.2 0.7 %copy-start.2 = (s32[8,8]{1,0:T(8,128)S(1)}, s32[8,8]{1,0:T(8,128)}, u32[]{:S(2)}) copy-start(s32[8,8]{1,0:T(8,128)} %lists_ref.1) | copy-start | bytes 772
  8.8 0.7 %copy-start.3 = (s32[8]{0:T(128)S(1)}, s32[8]{0:T(128)}, u32[]{:S(2)}) copy-start(s32[8]{0:T(128)} %counts_ref.1) | copy-start | bytes 100
  10.6 7.8 %collective-permute-start.4 = (bf16[64,1024]{1,0:T(8,128)(2,1)S(1)}, bf16[64,1024]{1,0:T(8,128)(2,1)S(1)}, u32[]{:S(2)}, u32[]{:S(2)}) collective-permute-start(bf16[64,1024]{1,0:T(8,128)(2,1)S(1)} %collective-permute-done.3.refs_2_), channel_id=1, source_target_pairs={{0,1},{1,0},{2,3},{3,2},{4,5},{5,4},{6,7},{7,6},{8,9},{9,8},{10,11... | collective-permute-start | bytes 393224 | tf_op jit(solution)/shard_map/ppermute | solution.py:481
  14.3 4.0 %copy-start = (bf16[64,1024]{1,0:T(8,128)(2,1)S(1)}, bf16[64,1024]{1,0:T(8,128)(2,1)}, u32[]{:S(2)}) copy-start(bf16[64,1024]{1,0:T(8,128)(2,1)} %refs_0_.1) | copy-start | bytes 393220
  14.4 4.0 %copy-start.1 = (bf16[64,256]{1,0:T(8,128)(2,1)S(1)}, bf16[64,256]{1,0:T(8,128)(2,1)}, u32[]{:S(2)}) copy-start(bf16[64,256]{1,0:T(8,128)(2,1)} %w_ref.1) | copy-start | bytes 98308
  21.0 2.1 %collective-permute-start.5 = (bf16[112,1024]{1,0:T(8,128)(2,1)S(1)}, bf16[112,1024]{1,0:T(8,128)(2,1)S(1)}, u32[]{:S(2)}, u32[]{:S(2)}) collective-permute-start(bf16[112,1024]{1,0:T(8,128)(2,1)S(1)} %get-tuple-element.56.mine_ref), channel_id=1, source_target_pairs={{0,4},{4,0},{8,12},{12,8},{16,20},{20,16},{24,28},{28,24},{1,5},{5... | collective-permute-start | bytes 688136 | tf_op jit(solution)/shard_map/ppermute | solution.py:465
  22.0 9.7 %collective-permute-start.7 = (bf16[80,1024]{1,0:T(8,128)(2,1)S(1)}, bf16[80,1024]{1,0:T(8,128)(2,1)S(1)}, u32[]{:S(2)}, u32[]{:S(2)}) collective-permute-start(bf16[80,1024]{1,0:T(8,128)(2,1)S(1)} %get-tuple-element.53.z_ref), channel_id=1, source_target_pairs={{4,8},{8,4},{12,16},{16,12},{20,24},{24,20},{5,9},{9,5},{13,17},{1... | collective-permute-start | bytes 491528 | tf_op jit(solution)/shard_map/ppermute | solution.py:471
  23.2 7.9 %collective-permute-start.6 = (f32[64,256]{1,0:T(8,128)S(1)}, f32[64,256]{1,0:T(8,128)S(1)}, u32[]{:S(2)}, u32[]{:S(2)}) collective-permute-start(f32[64,256]{1,0:T(8,128)S(1)} %shard_map.105.a_ref), channel_id=1, source_target_pairs={{0,16},{4,20},{8,24},{12,28},{16,0},{20,4},{24,8},{28,12},{1,17},{... | collective-permute-start | bytes 196616 | tf_op jit(solution)/shard_map/ppermute | solution.py:494
  31.1 4.0 %collective-permute-start.8 = (bf16[64,256]{1,0:T(8,128)(2,1)S(1)}, bf16[64,256]{1,0:T(8,128)(2,1)S(1)}, u32[]{:S(2)}, u32[]{:S(2)}) collective-permute-start(bf16[64,256]{1,0:T(8,128)(2,1)S(1)} %shard_map.107.a_ref), channel_id=1, source_target_pairs={{0,8},{4,12},{8,0},{12,4},{16,24},{20,28},{24,16},{28,20},{1,9},{5... | collective-permute-start | bytes 98312 | tf_op jit(solution)/shard_map/ppermute | solution.py:494

commit v6 on v5

--- a/solution.py
+++ b/solution.py
@@ -18,7 +18,7 @@
 MASKED = -1e30
 AUG = 16
 SIZES = (4, 5, 7, MAX_KEYS)
-EARLY = (0, 0, 3, 3)
+EARLY = (0, 0, 3, 4)
 F32 = jnp.float32
 BF16 = jnp.bfloat16
 VMEM_LIMIT = 48 * 1024 * 1024
@@ -401,7 +401,7 @@
     acc_ref[ext] = past_ref[ext]
     for copy in copies:
         copy.wait()
-    step, many = 1, 6
+    step, many = 1, 9
     count = 0
     for row in range(2 * blocks):
         for c in range(0, MAX_KEYS, step):
@@ -589,7 +589,7 @@
             pltpu.VMEM((2,) + queries.shape, BF16),
             pltpu.VMEM((2,) + z.shape, BF16),
             pltpu.VMEM((2 * blocks + 8, BLOCK), jnp.int32),
-            pltpu.SMEM((2 * blocks * MAX_KEYS + 8,), jnp.int32),
+            pltpu.SMEM((2 * blocks * MAX_KEYS + 16,), jnp.int32),
             pltpu.SMEM((2 * blocks + 8, BLOCK), jnp.int32),
             pltpu.SemaphoreType.DMA((1,)),
         ],

time: 35.9 us -> 35.6 us (level)
  waiting for transfers between devices: 1.3 us -> 0.6 us
    ppermute x2, waiting for transfers between devices: 0.83 us -> 0.03 us  [send(): self.came = lax.ppermute(self.value, self.axis, swap)]
    ppermute x2, starting transfers between devices: 1.5 us -> 0.84 us  [to_pair(): lax.ppermute(value, axis, [(i, i ^ 1) for i in range(last + 1) if i ^ 1 <...]
    ppermute x2, starting transfers between devices: 4.43 us -> 4.96 us  [send(): self.came = lax.ppermute(self.value, self.axis, swap)]
  transfers between devices with their start and end apart: 9 -> 9, of which waited for: 2 -> 1; matrix products, arithmetic and copies ran while one was open for 0% -> 0% of each run, Pallas kernels for 33% -> 32%
where the time goes in v6:
time: 35.6 us; the launch traced here: 35.1 us
  starting transfers between devices  16.2 us (46%)
  Pallas kernels  15.1 us (42%)
  local copies, waits for them, and re-layouts  1.35 us (4%)
  other arithmetic  1.08 us (3%)
  between operations  0.77 us (2%)
  waiting for transfers between devices  0.6 us (2%)
    pallas_call x8, Pallas kernels, kernel_call(): pl.pallas_call(body, out_shape=outs, in_specs=[vmem] * len(operands), out...  15.1 us
    ppermute x3, starting transfers between devices, gathered(): lax.ppermute(x, axis, swap)  9.02 us
    ppermute x2, starting transfers between devices, send(): self.came = lax.ppermute(self.value, self.axis, swap)  4.96 us
    unnamed x8, local copies, waits for them, and re-layouts  1.35 us
    ppermute x2, starting transfers between devices, to_other(): lax.ppermute(value, axis, [(i, j) for i, j in swap if 0 <= j <= last])  1.33 us
    another operation x1, other arithmetic, shards(): own = jnp.stack([keys, values, queries])  1.08 us
    ppermute x2, starting transfers between devices, to_pair(): lax.ppermute(value, axis, [(i, i ^ 1) for i in range(last + 1) if i ^ 1 <...  0.84 us
  transfers between devices with their start and end apart: 9, of which 1 were waited for; matrix products, arithmetic and copies ran while one was open for 0% of the time, Pallas kernels for 32%

profile of v6, /device:TPU:0, one launch (start us, length us, event | category | flops | bytes accessed | tf_op | source)
XLA Modules:
  0.0 35.1 jit_solution(13702322334872444787)
XLA Ops:
  0.6 1.1 %pad_maximum_fusion.own_ref = bf16[3,64,1024]{2,1,0:T(8,128)(2,1)S(1)} fusion(bf16[1,64,1024]{2,1,0:T(8,128)(2,1)} %bitcast.3, bf16[1,64,1024]{2,1,0:T(8,128)(2,1)} %bitcast.4, bf16[1,64,1024]{2,1,0:T(8,128)(2,1)} %bitcast.5), kind=kLoop, calls=%fused_computation | loop fusion | flops 393216 | bytes 786432 | tf_op jit(solution)/shard_map/stack | solution.py:518
  1.7 0.5 %collective-permute-start = (bf16[3,64,1024]{2,1,0:T(8,128)(2,1)S(1)}, bf16[3,64,1024]{2,1,0:T(8,128)(2,1)S(1)}, u32[]{:S(2)}, u32[]{:S(2)}) collective-permute-start(bf16[3,64,1024]{2,1,0:T(8,128)(2,1)S(1)} %pad_maximum_fusion.own_ref), channel_id=1, source_target_pairs={{0,4},{4,0},{8,12},{12,8},{16,20},{20,16},{24,28},{28,24},{1,5},{5... | collective-permute-start | bytes 1179656 | tf_op jit(solution)/shard_map/ppermute | solution.py:465
  2.2 0.7 %collective-permute-start.1 = (bf16[3,64,1024]{2,1,0:T(8,128)(2,1)S(1)}, bf16[3,64,1024]{2,1,0:T(8,128)(2,1)S(1)}, u32[]{:S(2)}, u32[]{:S(2)}) collective-permute-start(bf16[3,64,1024]{2,1,0:T(8,128)(2,1)S(1)} %pad_maximum_fusion.own_ref), channel_id=1, source_target_pairs={{4,8},{8,4},{12,16},{16,12},{20,24},{24,20},{5,9},{9,5},{13,17},{1... | collective-permute-start | bytes 1179656 | tf_op jit(solution)/shard_map/ppermute | solution.py:471
  2.9 3.7 %collective-permute-start.3 = (bf16[64,1024]{1,0:T(8,128)(2,1)}, bf16[64,1024]{1,0:T(8,128)(2,1)S(1)}, u32[]{:S(2)}, u32[]{:S(2)}) collective-permute-start(bf16[64,1024]{1,0:T(8,128)(2,1)} %refs_0_.1), channel_id=1, source_target_pairs={{0,2},{1,3},{2,0},{3,1},{4,6},{5,7},{6,4},{7,5},{8,10},{9,11},{10,... | collective-permute-start | bytes 393224 | tf_op jit(solution)/shard_map/ppermute | solution.py:481
  6.6 1.6 %collective-permute-start.2 = (bf16[64,1024]{1,0:T(8,128)(2,1)}, bf16[64,1024]{1,0:T(8,128)(2,1)S(1)}, u32[]{:S(2)}, u32[]{:S(2)}) collective-permute-start(bf16[64,1024]{1,0:T(8,128)(2,1)} %refs_0_.1), channel_id=1, source_target_pairs={{0,1},{1,0},{2,3},{3,2},{4,5},{5,4},{6,7},{7,6},{8,9},{9,8},{10,11... | collective-permute-start | bytes 393224 | tf_op jit(solution)/shard_map/ppermute | solution.py:481
  8.2 0.7 %copy-done.2 = s32[8,8]{1,0:T(8,128)S(1)} copy-done((s32[8,8]{1,0:T(8,128)S(1)}, s32[8,8]{1,0:T(8,128)}, u32[]{:S(2)}) %copy-start.2) | copy-done | bytes 280
  8.9 0.7 %copy-done.3 = s32[8]{0:T(128)S(1)} copy-done((s32[8]{0:T(128)S(1)}, s32[8]{0:T(128)}, u32[]{:S(2)}) %copy-start.3) | copy-done | bytes 56
  9.5 1.0 %shard_map.102 = (s32[8,128]{1,0:T(8,128)S(1)}, f32[2,8,128]{2,1,0:T(8,128)S(1)}, f32[3,24,128]{2,1,0:T(8,128)S(1)}, f32[25,128,128]{2,1,0:T(8,128)S(1)}, bf16[2...) custom-call(bf16[3,64,1024]{2,1,0:T(8,128)(2,1)S(1)} %pad_maximum_fu, ...), custom_call_target="tpu_custom_call" | custom-call | bytes 4641056 | tf_op jit(solution)/shard_map/pallas_call | solution.py:449
  10.6 0.0 collective-permute-done.3.refs_2_
  10.6 3.8 %collective-permute-start.4 = (bf16[64,1024]{1,0:T(8,128)(2,1)S(1)}, bf16[64,1024]{1,0:T(8,128)(2,1)S(1)}, u32[]{:S(2)}, u32[]{:S(2)}) collective-permute-start(bf16[64,1024]{1,0:T(8,128)(2,1)S(1)} %collective-permute-done.3.refs_2_), channel_id=1, source_target_pairs={{0,1},{1,0},{2,3},{3,2},{4,5},{5,4},{6,7},{7,6},{8,9},{9,8},{10,11... | collective-permute-start | bytes 393224 | tf_op jit(solution)/shard_map/ppermute | solution.py:481
  14.3 0.0 collective-permute-done.pair_ref.pair_own
  14.4 0.0 copy-start.1
  14.4 3.9 %shard_map.103 = (bf16[25,128,128]{2,1,0:T(8,128)(2,1)S(1)}, bf16[25,128,128]{2,1,0:T(8,128)(2,1)S(1)}, bf16[25,64,128]{2,1,0:T(8,128)(2,1)S(1)}, bf16[25,80,128...) custom-call(s32[8,128]{1,0:T(8,128)S(1)} %get-tuple-element.40.slots, ...), custom_call_target="tpu_custom_call", output_to_operand_aliasing={{0}: (5, {}), {1}: (6, {}), {2}: (7, {}), {3}: (8, {})} | custom-call | flops 1610612736 | bytes 6610944 | tf_op jit(solution)/shard_map/pallas_call | solution.py:449
  18.3 0.0 collective-permute-done.4.refs_3_
  18.4 3.3 %shard_map.104 = (bf16[80,1024]{1,0:T(8,128)(2,1)S(1)}, bf16[112,1024]{1,0:T(8,128)(2,1)S(1)}, bf16[64,1024]{1,0:T(8,128)(2,1)S(1)}, f32[25,128,128]{2,1,0:T(8,128)S(1)}) custom-call(s32[8,128]{1,0:T(8,128)S(1)} %get-tuple-element.40.slots_vmem, bf16[3,64,1024]{2,1,0:T(8,128)(2,1)S(1)} %pad_maximum_fusion.own_ref, ...), custom_call_target="tpu_custom_call", output_to_operand_aliasing={{3}: (9, {})} | custom-call | flops 67108864 | bytes 7081984 | tf_op jit(solution)/shard_map/pallas_call | solution.py:449
  21.7 0.3 collective-permute-start.5
  22.0 0.7 %collective-permute-start.7 = (bf16[80,1024]{1,0:T(8,128)(2,1)S(1)}, bf16[80,1024]{1,0:T(8,128)(2,1)S(1)}, u32[]{:S(2)}, u32[]{:S(2)}) collective-permute-start(bf16[80,1024]{1,0:T(8,128)(2,1)S(1)} %get-tuple-element.53.z_ref), channel_id=1, source_target_pairs={{4,8},{8,4},{12,16},{16,12},{20,24},{24,20},{5,9},{9,5},{13,17},{1... | collective-permute-start | bytes 491528 | tf_op jit(solution)/shard_map/ppermute | solution.py:471
  22.7 0.6 %collective-permute-done.5.came_ref.pair_ref = bf16[112,1024]{1,0:T(8,128)(2,1)S(1)} collective-permute-done((bf16[112,1024]{1,0:T(8,128)(2,1)S(1)}, bf16[112,1024]{1,0:T(8,128)(2,1)S(1)}, u32[]{:S(2)}, u32[]{:S(2)}) %collective-permute-start.5) | collective-permute-done | bytes 229408 | tf_op jit(solution)/shard_map/ppermute | solution.py:465
  23.3 3.7 %collective-permute-start.6 = (f32[64,256]{1,0:T(8,128)S(1)}, f32[64,256]{1,0:T(8,128)S(1)}, u32[]{:S(2)}, u32[]{:S(2)}) collective-permute-start(f32[64,256]{1,0:T(8,128)S(1)} %shard_map.105.a_ref), channel_id=1, source_target_pairs={{0,16},{4,20},{8,24},{12,28},{16,0},{20,4},{24,8},{28,12},{1,17},{... | collective-permute-start | bytes 196616 | tf_op jit(solution)/shard_map/ppermute | solution.py:494
  26.9 3.5 %shard_map.106 = (bf16[64,1024]{1,0:T(8,128)(2,1)S(1)}, f32[25,128,128]{2,1,0:T(8,128)S(1)}) custom-call(s32[8,128]{1,0:T(8,128)S(1)} %get-tuple-element.40.slots_vmem, bf16[3,64,1024]{2,1,0:T(8,128)(2,1)S(1)} %pad_maximum_fusion.own_ref, bf16[80,1024]{1,0:T(8,128)(2,1)S(1)} %get-tuple-element.53.z_ref, ...), custom_call_target="tpu_custom_call", output_to_operand_aliasing={{0}: (6, {}), {1}: (7, {})} | custom-call | flops 2684354560 | bytes 6148096 | tf_op jit(solution)/shard_map/pallas_call | solution.py:449
  30.4 1.3 %collective-permute-start.8 = (bf16[64,256]{1,0:T(8,128)(2,1)S(1)}, bf16[64,256]{1,0:T(8,128)(2,1)S(1)}, u32[]{:S(2)}, u32[]{:S(2)}) collective-permute-start(bf16[64,256]{1,0:T(8,128)(2,1)S(1)} %shard_map.107.a_ref), channel_id=1, source_target_pairs={{0,8},{4,12},{8,0},{12,4},{16,24},{20,28},{24,16},{28,20},{1,9},{5... | collective-permute-start | bytes 98312 | tf_op jit(solution)/shard_map/ppermute | solution.py:494
  31.7 2.7 %shard_map.108 = (bf16[64,1024]{1,0:T(8,128)(2,1)}, bf16[64,1024]{1,0:T(8,128)(2,1)}, bf16[64,1024]{1,0:T(8,128)(2,1)}) custom-call(bf16[64,1024]{1,0:T(8,128)(2,1)S(1)} %get-tuple-element.68.dq_in, f32[25,128,128]{2,1,0:T(8,128)S(1)} %get-tuple-element.69.past_ref, bf16[3,64,1024]{2,1,0:T(8,128)(2,1)S(1)} %collective-permute-done.pair_ref.pair_own, ...), custom_call_target="tpu_custom_call" | custom-call | flops 1073741824 | bytes 4980736 | tf_op jit(solution)/shard_map/pallas_call | solution.py:449
  34.4 0.0 collective-permute-done.8.b_ref
  34.5 0.6 %shard_map.109 = f32[64,256]{1,0:T(8,128)} custom-call(bf16[64,256]{1,0:T(8,128)(2,1)S(1)} %shard_map.107.a_ref, bf16[64,256]{1,0:T(8,128)(2,1)S(1)} %collective-permute-done.8.b_ref), custom_call_target="tpu_custom_call" | custom-call | bytes 131072 | tf_op jit(solution)/shard_map/pallas_call | solution.py:449
  (11 shorter events, 0.0 us)
Async XLA Ops:
  1.7 12.6 %collective-permute-start = (bf16[3,64,1024]{2,1,0:T(8,128)(2,1)S(1)}, bf16[3,64,1024]{2,1,0:T(8,128)(2,1)S(1)}, u32[]{:S(2)}, u32[]{:S(2)}) collective-permute-start(bf16[3,64,1024]{2,1,0:T(8,128)(2,1)S(1)} %pad_maximum_fusion.own_ref), channel_id=1, source_target_pairs={{0,4},{4,0},{8,12},{12,8},{16,20},{20,16},{24,28},{28,24},{1,5},{5... | collective-permute-start | bytes 1179656 | tf_op jit(solution)/shard_map/ppermute | solution.py:465
  2.2 12.1 %collective-permute-start.1 = (bf16[3,64,1024]{2,1,0:T(8,128)(2,1)S(1)}, bf16[3,64,1024]{2,1,0:T(8,128)(2,1)S(1)}, u32[]{:S(2)}, u32[]{:S(2)}) collective-permute-start(bf16[3,64,1024]{2,1,0:T(8,128)(2,1)S(1)} %pad_maximum_fusion.own_ref), channel_id=1, source_target_pairs={{4,8},{8,4},{12,16},{16,12},{20,24},{24,20},{5,9},{9,5},{13,17},{1... | collective-permute-start | bytes 1179656 | tf_op jit(solution)/shard_map/ppermute | solution.py:471
  2.9 7.6 %collective-permute-start.3 = (bf16[64,1024]{1,0:T(8,128)(2,1)}, bf16[64,1024]{1,0:T(8,128)(2,1)S(1)}, u32[]{:S(2)}, u32[]{:S(2)}) collective-permute-start(bf16[64,1024]{1,0:T(8,128)(2,1)} %refs_0_.1), channel_id=1, source_target_pairs={{0,2},{1,3},{2,0},{3,1},{4,6},{5,7},{6,4},{7,5},{8,10},{9,11},{10,... | collective-permute-start | bytes 393224 | tf_op jit(solution)/shard_map/ppermute | solution.py:481
  6.6 11.7 %collective-permute-start.2 = (bf16[64,1024]{1,0:T(8,128)(2,1)}, bf16[64,1024]{1,0:T(8,128)(2,1)S(1)}, u32[]{:S(2)}, u32[]{:S(2)}) collective-permute-start(bf16[64,1024]{1,0:T(8,128)(2,1)} %refs_0_.1), channel_id=1, source_target_pairs={{0,1},{1,0},{2,3},{3,2},{4,5},{5,4},{6,7},{7,6},{8,9},{9,8},{10,11... | collective-permute-start | bytes 393224 | tf_op jit(solution)/shard_map/ppermute | solution.py:481
  8.2 0.7 %copy-start.2 = (s32[8,8]{1,0:T(8,128)S(1)}, s32[8,8]{1,0:T(8,128)}, u32[]{:S(2)}) copy-start(s32[8,8]{1,0:T(8,128)} %lists_ref.1) | copy-start | bytes 772
  8.8 0.7 %copy-start.3 = (s32[8]{0:T(128)S(1)}, s32[8]{0:T(128)}, u32[]{:S(2)}) copy-start(s32[8]{0:T(128)} %counts_ref.1) | copy-start | bytes 100
  10.6 7.8 %collective-permute-start.4 = (bf16[64,1024]{1,0:T(8,128)(2,1)S(1)}, bf16[64,1024]{1,0:T(8,128)(2,1)S(1)}, u32[]{:S(2)}, u32[]{:S(2)}) collective-permute-start(bf16[64,1024]{1,0:T(8,128)(2,1)S(1)} %collective-permute-done.3.refs_2_), channel_id=1, source_target_pairs={{0,1},{1,0},{2,3},{3,2},{4,5},{5,4},{6,7},{7,6},{8,9},{9,8},{10,11... | collective-permute-start | bytes 393224 | tf_op jit(solution)/shard_map/ppermute | solution.py:481
  14.3 4.0 %copy-start = (bf16[64,1024]{1,0:T(8,128)(2,1)S(1)}, bf16[64,1024]{1,0:T(8,128)(2,1)}, u32[]{:S(2)}) copy-start(bf16[64,1024]{1,0:T(8,128)(2,1)} %refs_0_.1) | copy-start | bytes 393220
  14.4 4.0 %copy-start.1 = (bf16[64,256]{1,0:T(8,128)(2,1)S(1)}, bf16[64,256]{1,0:T(8,128)(2,1)}, u32[]{:S(2)}) copy-start(bf16[64,256]{1,0:T(8,128)(2,1)} %w_ref.1) | copy-start | bytes 98308
  21.7 1.6 %collective-permute-start.5 = (bf16[112,1024]{1,0:T(8,128)(2,1)S(1)}, bf16[112,1024]{1,0:T(8,128)(2,1)S(1)}, u32[]{:S(2)}, u32[]{:S(2)}) collective-permute-start(bf16[112,1024]{1,0:T(8,128)(2,1)S(1)} %get-tuple-element.56.mine_ref), channel_id=1, source_target_pairs={{0,4},{4,0},{8,12},{12,8},{16,20},{20,16},{24,28},{28,24},{1,5},{5... | collective-permute-start | bytes 688136 | tf_op jit(solution)/shard_map/ppermute | solution.py:465
  22.0 9.7 %collective-permute-start.7 = (bf16[80,1024]{1,0:T(8,128)(2,1)S(1)}, bf16[80,1024]{1,0:T(8,128)(2,1)S(1)}, u32[]{:S(2)}, u32[]{:S(2)}) collective-permute-start(bf16[80,1024]{1,0:T(8,128)(2,1)S(1)} %get-tuple-element.53.z_ref), channel_id=1, source_target_pairs={{4,8},{8,4},{12,16},{16,12},{20,24},{24,20},{5,9},{9,5},{13,17},{1... | collective-permute-start | bytes 491528 | tf_op jit(solution)/shard_map/ppermute | solution.py:471
  23.3 7.2 %collective-permute-start.6 = (f32[64,256]{1,0:T(8,128)S(1)}, f32[64,256]{1,0:T(8,128)S(1)}, u32[]{:S(2)}, u32[]{:S(2)}) collective-permute-start(f32[64,256]{1,0:T(8,128)S(1)} %shard_map.105.a_ref), channel_id=1, source_target_pairs={{0,16},{4,20},{8,24},{12,28},{16,0},{20,4},{24,8},{28,12},{1,17},{... | collective-permute-start | bytes 196616 | tf_op jit(solution)/shard_map/ppermute | solution.py:494
  30.4 4.0 %collective-permute-start.8 = (bf16[64,256]{1,0:T(8,128)(2,1)S(1)}, bf16[64,256]{1,0:T(8,128)(2,1)S(1)}, u32[]{:S(2)}, u32[]{:S(2)}) collective-permute-start(bf16[64,256]{1,0:T(8,128)(2,1)S(1)} %shard_map.107.a_ref), channel_id=1, source_target_pairs={{0,8},{4,12},{8,0},{12,4},{16,24},{20,28},{24,16},{28,20},{1,9},{5... | collective-permute-start | bytes 98312 | tf_op jit(solution)/shard_map/ppermute | solution.py:494
